TPU v7x, 32 devices: a whole 2x2x4 slice. The times are simulated.
32 devices in a mesh: gx: 4 (over z), gy: 8 (over y, x, core).
Axes of the slice: x: 2, y: 2, z: 4, core: 2. Of those that a mesh axis runs over, the one named last changes fastest.
Arguments:
- queries: bfloat16 [1024, 4096], P('gy', 'gx'), may hold values from -8 to 8
- new_kv: bfloat16 [1024, 8, 128], P('gy', 'gx'), may hold values from -8 to 8
- kv_cache: bfloat16 [4096, 8, 128], P('gy', 'gx'), may hold values from -8 to 8
- cache_seg: int32 [4096], P('gy'), may hold values from -1 to 15, as said below
- cache_slot: int32 [1024], P('gy'), may hold values from 0 to 4095, as said below
- token_seg: int32 [1024], P('gy'), may hold values from 0 to 15, never falling along the last dimension, each value on 1 to 512 neighbouring positions
- pad_mask: int32 [1024], P('gy'), may hold values 0 or 1
- sink_logits: float32 [64], P('gx'), may hold values from 0 to 4
- out_weight: bfloat16 [4096, 2880], P('gx', 'gy'), may hold values from -0.75 to 0.75
- out_bias: float32 [2880], P('gx'), may hold values from -2 to 2
Outputs:
- attended: bfloat16 [1024, 2880], P('gy', 'gx')
- cache_out: bfloat16 [4096, 8, 128], P('gy', 'gx')
Inputs may be any that keep to these rules, and one draw needn't show every extreme that they name: `cache_seg`: the sequence whose cached key and value a slot holds, or -1 for an empty slot. Distinct slots, each empty (-1) in cache_seg; cache_slot[t] // 512 == t // 128.
All inputs are finite; a program needn't handle non-finite values. No bound on the sum of `pad_mask` on one device may be relied on, other than what follows from the above.
Results may differ from a plain program's by a relative error of at most 0.015.
Values may be sent and summed in bfloat16 or wider, within the bound.
No kernel may reach another device: no remote copies, remote signals or barrier semaphores. Data moves between devices by JAX's collectives and lax.ppermute only.
A program may use at most 128 MiB of HBM per device.

v0:
```python
import math

import jax
import jax.numpy as jnp
from jax import lax
from jax.sharding import PartitionSpec as P


def shards(
    queries,
    new_kv,
    kv_cache,
    cache_seg,
    cache_slot,
    token_seg,
    pad_mask,
    sink_logits,
    out_weight,
    out_bias,
):
    local_tokens = queries.shape[0]
    local_slots = kv_cache.shape[0]
    local_groups = kv_cache.shape[1]
    head_dim = kv_cache.shape[2] // 2
    group_heads = queries.shape[1] // (local_groups * head_dim)
    scale = head_dim ** (-0.5)
    own_index = lax.axis_index("gy")
    first_token = own_index * local_tokens
    live_rows = pad_mask == 1
    target = jnp.where(live_rows, cache_slot - own_index * local_slots, local_slots)
    cache_out = kv_cache.at[target].set(new_kv, mode="drop")
    token_index = first_token + jnp.arange(local_tokens, dtype=jnp.int32)
    slot_seg = cache_seg.at[target].set(token_seg, mode="drop")
    slot_order = jnp.full((local_slots,), -1, jnp.int32).at[target].set(token_index, mode="drop")
    sink_table = sink_logits.reshape(local_groups, group_heads)
    query_heads = queries.reshape(local_tokens, local_groups, group_heads, head_dim)
    initial = (
        jnp.broadcast_to(sink_table[:, :, None], (local_groups, group_heads, local_tokens)),
        jnp.ones((local_groups, group_heads, local_tokens), jnp.float32),
        jnp.zeros((local_groups, group_heads, local_tokens, head_dim), jnp.float32),
    )
    kv_rows = lax.all_gather(cache_out, "gy", axis=0, tiled=True)
    seg_rows = lax.all_gather(slot_seg, "gy", axis=0, tiled=True)
    order_rows = lax.all_gather(slot_order, "gy", axis=0, tiled=True)
    total_rows = kv_rows.shape[0]
    blk_rows = math.gcd(total_rows, 512)
    count_blocks = total_rows // blk_rows
    stacked = (
        kv_rows.reshape(count_blocks, blk_rows, local_groups, 2 * head_dim),
        seg_rows.reshape(count_blocks, blk_rows),
        order_rows.reshape(count_blocks, blk_rows),
    )

    def one_block(running, block_data):
        run_peak, weight_sum, weighted = running
        block_kv, block_seg, block_order = block_data
        visible = (block_seg[None, :] == token_seg[:, None]) & (
            block_order[None, :] <= token_index[:, None]
        )
        scores = (
            jnp.einsum(
                "tgqd,cgd->gqtc",
                query_heads,
                block_kv[:, :, :head_dim],
                preferred_element_type=jnp.float32,
            )
            * scale
        )
        new_peak = jnp.maximum(run_peak, jnp.max(jnp.where(visible, scores, -jnp.inf), axis=-1))
        rescale = jnp.exp(run_peak - new_peak)
        weights = jnp.where(visible, jnp.exp(scores - new_peak[..., None]), 0.0)
        weight_sum = weight_sum * rescale + jnp.sum(weights, axis=-1)
        weighted = weighted * rescale[..., None] + jnp.einsum(
            "gqtc,cgd->gqtd",
            weights.astype(jnp.bfloat16),
            block_kv[:, :, head_dim:],
            preferred_element_type=jnp.float32,
        )
        return ((new_peak, weight_sum, weighted), None)

    result, unused = lax.scan(one_block, initial, stacked)
    run_peak, weight_sum, weighted = result
    attn_heads = jnp.transpose(weighted / weight_sum[..., None], (2, 0, 1, 3)).reshape(
        local_tokens, local_groups * group_heads * head_dim
    )
    attention = (attn_heads * pad_mask[:, None].astype(jnp.float32)).astype(jnp.bfloat16)
    partial_out = jnp.dot(
        attention,
        lax.all_gather(out_weight, "gy", axis=1, tiled=True),
        preferred_element_type=jnp.float32,
    )
    summed = lax.psum_scatter(
        partial_out.astype(jnp.bfloat16), "gx", scatter_dimension=1, tiled=True
    ).astype(jnp.float32)
    return ((summed + out_bias).astype(jnp.bfloat16), cache_out)


def solution(mesh):
    placed = (
        P("gy", "gx"),
        P("gy", "gx", None),
        P("gy", "gx", None),
        P("gy"),
        P("gy"),
        P("gy"),
        P("gy"),
        P("gx"),
        P("gx", "gy"),
        P("gx"),
    )
    return jax.shard_map(
        shards,
        mesh=mesh,
        in_specs=placed,
        out_specs=(P("gy", "gx"), P("gy", "gx", None)),
        check_vma=False,
    )
```

profile of v0, /device:TPU:0, one launch (start us, length us, event | category | flops | bytes accessed | tf_op | source)
XLA Modules:
  0.0 160.2 jit_solution(16568020966255216594)
XLA Ops:
  7.2 1.0 copy.46
  9.6 9.8 %scatter_fusion.1 = bf16[512,2,128]{2,1,0:T(2,128)(2,1)S(1)} fusion(bf16[512,2,128]{2,1,0:T(2,128)(2,1)S(1)} %copy.46, s32[128]{0:T(128)S(1)} %get-tuple-element.140, bf16[128,2,128]{2,1,0:T(2,128)(2,1)} %param.13), kind=kCustom, calls=%fused_computation.2 | custom fusion | bytes 197120 | tf_op jit(solution)/shard_map/scatter | solution.py:31
  20.9 1.0 scatter_custom_fusion.1
  21.9 10.4 %all-gather.1 = s32[8,1,512]{2,1,0:T(1,128)S(1)} all-gather(s32[1,1,512]{2,1,0:T(1,128)S(1)} %bitcast.77), channel_id=1, replica_groups=mesh['gx'=4,'gy'=8] {'gy'}, dimensions={0}, use_global_device_ids=true | all-gather | bytes 18432 | tf_op jit(solution)/shard_map/all_gather | solution.py:44
  32.2 1.1 scatter_fusion
  33.4 8.9 %all-gather = s32[8,1,512]{2,1,0:T(1,128)S(1)} all-gather(s32[1,1,512]{2,1,0:T(1,128)S(1)} %bitcast.68), channel_id=1, replica_groups=mesh['gx'=4,'gy'=8] {'gy'}, dimensions={0}, use_global_device_ids=true | all-gather | bytes 18432 | tf_op jit(solution)/shard_map/all_gather | solution.py:43
  42.2 1.1 copy.16
  44.1 6.7 %all-gather.5.cloned.1.call-done = bf16[4096,2,128]{2,1,0:T(2,128)(2,1)} async-done(((bf16[512,2,128]{2,1,0:T(2,128)(2,1)}), bf16[4096,2,128]{2,1,0:T(2,128)(2,1)}) %all-gather.5.cloned.1.call-update) | async-done | bytes 2097168 | tf_op jit(solution)/shard_map/all_gather | solution.py:42
  50.9 72.6 %while.15 = (s32[]{:T(128)}, f32[2,8,128]{2,1,0:T(8,128)S(1)}, f32[2,8,128]{2,1,0:T(8,128)S(1)}, f32[2,8,128,64]{2,3,1,0:T(8,128)S(1)}, s32[8,512]{1,0:T(8,128)S...) while((s32[]{:T(128)}, f32[2,8,128]{2,1,0:T(8,128)S(1)}, ...), condition=%wide.region_6.7_spmd.clone, body=%wide.region_3.6_spmd.clone.sunk | while | flops 280565888 | bytes 32388776 | solution.py:81
  50.9 0.9 compare_and_fusion.2
  51.8 1.1 constant_dynamic-slice_fusion.6
  53.9 2.0 %copy-done = f32[2,512,128,8]{2,1,3,0:T(8,128)} copy-done((f32[2,512,128,8]{2,1,3,0:T(8,128)}, f32[2,512,128,8]{2,1,3,0:T(8,128)S(1)}, u32[]{:S(2)}) %copy-start) | copy-done | bytes 4194328 | tf_op jit(solution)/shard_map/while
  55.9 0.8 fusion.33
  56.7 3.2 %fusion.35 = f32[2,8,128,64]{2,3,1,0:T(8,128)S(1)} fusion(f32[2,512,128,8]{2,1,3,0:T(8,128)} %copy-done, f32[2,8,128]{2,1,0:T(8,128)S(1)} %max.5, pred[128,512]{0,1:T(8,128)(4,1)S(1)} %compare_and_fusion.2, f32[2,8,128,64]{2,3,1,0:T(8,128)S(1)} %get-tuple-element.230, f32[2,8,128]{2,1,0:T(8,128)S(1)} %get-tuple-element.214, pred[]{:T(512)S(6)} %compare.3, ...), kind=kOutput, calls=%fused_computation.13.clone.1 | convolution fusion | flops 138805248 | bytes 5455873 | tf_op jit(solution)/shard_map/while/body/eval_jaxpr/gqtc,cgd->gqtd/dot_general | solution.py:73
  60.0 0.9 compare_and_fusion.2
  60.9 1.2 constant_dynamic-slice_fusion.6
  63.0 2.0 %copy-done = f32[2,512,128,8]{2,1,3,0:T(8,128)} copy-done((f32[2,512,128,8]{2,1,3,0:T(8,128)}, f32[2,512,128,8]{2,1,3,0:T(8,128)S(1)}, u32[]{:S(2)}) %copy-start) | copy-done | bytes 4194328 | tf_op jit(solution)/shard_map/while
  65.0 0.8 fusion.33
  65.9 3.2 %fusion.35 = f32[2,8,128,64]{2,3,1,0:T(8,128)S(1)} fusion(f32[2,512,128,8]{2,1,3,0:T(8,128)} %copy-done, f32[2,8,128]{2,1,0:T(8,128)S(1)} %max.5, pred[128,512]{0,1:T(8,128)(4,1)S(1)} %compare_and_fusion.2, f32[2,8,128,64]{2,3,1,0:T(8,128)S(1)} %get-tuple-element.230, f32[2,8,128]{2,1,0:T(8,128)S(1)} %get-tuple-element.214, pred[]{:T(512)S(6)} %compare.3, ...), kind=kOutput, calls=%fused_computation.13.clone.1 | convolution fusion | flops 138805248 | bytes 5455873 | tf_op jit(solution)/shard_map/while/body/eval_jaxpr/gqtc,cgd->gqtd/dot_general | solution.py:73
  69.1 0.9 compare_and_fusion.2
  70.0 1.1 constant_dynamic-slice_fusion.6
  72.1 2.0 %copy-done = f32[2,512,128,8]{2,1,3,0:T(8,128)} copy-done((f32[2,512,128,8]{2,1,3,0:T(8,128)}, f32[2,512,128,8]{2,1,3,0:T(8,128)S(1)}, u32[]{:S(2)}) %copy-start) | copy-done | bytes 4194328 | tf_op jit(solution)/shard_map/while
  74.0 0.8 fusion.33
  74.9 3.3 %fusion.35 = f32[2,8,128,64]{2,3,1,0:T(8,128)S(1)} fusion(f32[2,512,128,8]{2,1,3,0:T(8,128)} %copy-done, f32[2,8,128]{2,1,0:T(8,128)S(1)} %max.5, pred[128,512]{0,1:T(8,128)(4,1)S(1)} %compare_and_fusion.2, f32[2,8,128,64]{2,3,1,0:T(8,128)S(1)} %get-tuple-element.230, f32[2,8,128]{2,1,0:T(8,128)S(1)} %get-tuple-element.214, pred[]{:T(512)S(6)} %compare.3, ...), kind=kOutput, calls=%fused_computation.13.clone.1 | convolution fusion | flops 138805248 | bytes 5455873 | tf_op jit(solution)/shard_map/while/body/eval_jaxpr/gqtc,cgd->gqtd/dot_general | solution.py:73
  78.2 0.9 compare_and_fusion.2
  79.1 1.1 constant_dynamic-slice_fusion.6
  81.2 2.0 %copy-done = f32[2,512,128,8]{2,1,3,0:T(8,128)} copy-done((f32[2,512,128,8]{2,1,3,0:T(8,128)}, f32[2,512,128,8]{2,1,3,0:T(8,128)S(1)}, u32[]{:S(2)}) %copy-start) | copy-done | bytes 4194328 | tf_op jit(solution)/shard_map/while
  84.1 3.2 %fusion.35 = f32[2,8,128,64]{2,3,1,0:T(8,128)S(1)} fusion(f32[2,512,128,8]{2,1,3,0:T(8,128)} %copy-done, f32[2,8,128]{2,1,0:T(8,128)S(1)} %max.5, pred[128,512]{0,1:T(8,128)(4,1)S(1)} %compare_and_fusion.2, f32[2,8,128,64]{2,3,1,0:T(8,128)S(1)} %get-tuple-element.230, f32[2,8,128]{2,1,0:T(8,128)S(1)} %get-tuple-element.214, pred[]{:T(512)S(6)} %compare.3, ...), kind=kOutput, calls=%fused_computation.13.clone.1 | convolution fusion | flops 138805248 | bytes 5455873 | tf_op jit(solution)/shard_map/while/body/eval_jaxpr/gqtc,cgd->gqtd/dot_general | solution.py:73
  87.3 0.9 compare_and_fusion.2
  88.2 1.1 constant_dynamic-slice_fusion.6
  90.3 2.0 %copy-done = f32[2,512,128,8]{2,1,3,0:T(8,128)} copy-done((f32[2,512,128,8]{2,1,3,0:T(8,128)}, f32[2,512,128,8]{2,1,3,0:T(8,128)S(1)}, u32[]{:S(2)}) %copy-start) | copy-done | bytes 4194328 | tf_op jit(solution)/shard_map/while
  93.1 3.2 %fusion.35 = f32[2,8,128,64]{2,3,1,0:T(8,128)S(1)} fusion(f32[2,512,128,8]{2,1,3,0:T(8,128)} %copy-done, f32[2,8,128]{2,1,0:T(8,128)S(1)} %max.5, pred[128,512]{0,1:T(8,128)(4,1)S(1)} %compare_and_fusion.2, f32[2,8,128,64]{2,3,1,0:T(8,128)S(1)} %get-tuple-element.230, f32[2,8,128]{2,1,0:T(8,128)S(1)} %get-tuple-element.214, pred[]{:T(512)S(6)} %compare.3, ...), kind=kOutput, calls=%fused_computation.13.clone.1 | convolution fusion | flops 138805248 | bytes 5455873 | tf_op jit(solution)/shard_map/while/body/eval_jaxpr/gqtc,cgd->gqtd/dot_general | solution.py:73
  96.4 0.9 compare_and_fusion.2
  97.3 1.1 constant_dynamic-slice_fusion.6
  99.4 2.0 %copy-done = f32[2,512,128,8]{2,1,3,0:T(8,128)} copy-done((f32[2,512,128,8]{2,1,3,0:T(8,128)}, f32[2,512,128,8]{2,1,3,0:T(8,128)S(1)}, u32[]{:S(2)}) %copy-start) | copy-done | bytes 4194328 | tf_op jit(solution)/shard_map/while
  102.2 3.2 %fusion.35 = f32[2,8,128,64]{2,3,1,0:T(8,128)S(1)} fusion(f32[2,512,128,8]{2,1,3,0:T(8,128)} %copy-done, f32[2,8,128]{2,1,0:T(8,128)S(1)} %max.5, pred[128,512]{0,1:T(8,128)(4,1)S(1)} %compare_and_fusion.2, f32[2,8,128,64]{2,3,1,0:T(8,128)S(1)} %get-tuple-element.230, f32[2,8,128]{2,1,0:T(8,128)S(1)} %get-tuple-element.214, pred[]{:T(512)S(6)} %compare.3, ...), kind=kOutput, calls=%fused_computation.13.clone.1 | convolution fusion | flops 138805248 | bytes 5455873 | tf_op jit(solution)/shard_map/while/body/eval_jaxpr/gqtc,cgd->gqtd/dot_general | solution.py:73
  105.5 0.9 compare_and_fusion.2
  106.3 1.1 constant_dynamic-slice_fusion.6
  108.4 2.0 %copy-done = f32[2,512,128,8]{2,1,3,0:T(8,128)} copy-done((f32[2,512,128,8]{2,1,3,0:T(8,128)}, f32[2,512,128,8]{2,1,3,0:T(8,128)S(1)}, u32[]{:S(2)}) %copy-start) | copy-done | bytes 4194328 | tf_op jit(solution)/shard_map/while
  110.4 0.8 fusion.33
  111.3 3.2 %fusion.35 = f32[2,8,128,64]{2,3,1,0:T(8,128)S(1)} fusion(f32[2,512,128,8]{2,1,3,0:T(8,128)} %copy-done, f32[2,8,128]{2,1,0:T(8,128)S(1)} %max.5, pred[128,512]{0,1:T(8,128)(4,1)S(1)} %compare_and_fusion.2, f32[2,8,128,64]{2,3,1,0:T(8,128)S(1)} %get-tuple-element.230, f32[2,8,128]{2,1,0:T(8,128)S(1)} %get-tuple-element.214, pred[]{:T(512)S(6)} %compare.3, ...), kind=kOutput, calls=%fused_computation.13.clone.1 | convolution fusion | flops 138805248 | bytes 5455873 | tf_op jit(solution)/shard_map/while/body/eval_jaxpr/gqtc,cgd->gqtd/dot_general | solution.py:73
  114.5 0.9 compare_and_fusion.2
  115.4 1.1 constant_dynamic-slice_fusion.6
  117.5 2.0 %copy-done = f32[2,512,128,8]{2,1,3,0:T(8,128)} copy-done((f32[2,512,128,8]{2,1,3,0:T(8,128)}, f32[2,512,128,8]{2,1,3,0:T(8,128)S(1)}, u32[]{:S(2)}) %copy-start) | copy-done | bytes 4194328 | tf_op jit(solution)/shard_map/while
  120.4 3.2 %fusion.35 = f32[2,8,128,64]{2,3,1,0:T(8,128)S(1)} fusion(f32[2,512,128,8]{2,1,3,0:T(8,128)} %copy-done, f32[2,8,128]{2,1,0:T(8,128)S(1)} %max.5, pred[128,512]{0,1:T(8,128)(4,1)S(1)} %compare_and_fusion.2, f32[2,8,128,64]{2,3,1,0:T(8,128)S(1)} %get-tuple-element.230, f32[2,8,128]{2,1,0:T(8,128)S(1)} %get-tuple-element.214, pred[]{:T(512)S(6)} %compare.3, ...), kind=kOutput, calls=%fused_computation.13.clone.1 | convolution fusion | flops 138805248 | bytes 5455873 | tf_op jit(solution)/shard_map/while/body/eval_jaxpr/gqtc,cgd->gqtd/dot_general | solution.py:73
  123.7 5.3 %convolution_convert_fusion = bf16[128,2880]{0,1:T(8,128)(2,1)} fusion(bf16[1024,2880]{0,1:T(8,128)(2,1)} %all-gather.7.cloned.1.call-done, bf16[128,1024]{0,1:T(8,128)(2,1)S(1)} %fusion.17), kind=kOutput, calls=%fused_computation.28 | convolution fusion | flops 755343360 | bytes 6897664 | tf_op jit(solution)/shard_map/dot_general | solution.py:87
  129.0 22.9 %reduce-scatter.2.cloned.1.call-done = bf16[128,720]{0,1:T(8,128)(2,1)} async-done(((bf16[128,2880]{0,1:T(8,128)(2,1)}), bf16[128,720]{0,1:T(8,128)(2,1)}) %reduce-scatter.2.cloned.1.call-update) | async-done | bytes 184336 | tf_op jit(solution)/shard_map/reduce_scatter | solution.py:92
  151.9 1.8 %add_convert_fusion = bf16[128,720]{0,1:T(8,128)(2,1)} fusion(bf16[128,720]{0,1:T(8,128)(2,1)} %reduce-scatter.2.cloned.1.call-done, f32[720]{0:T(1024)S(1)} %copy-done.2), kind=kLoop, calls=%fused_computation.31 | loop fusion | flops 276480 | bytes 371520 | tf_op jit(solution)/shard_map/convert_element_type | solution.py:95
  (89 shorter events, 15.0 us)
Async XLA Ops:
  7.2 43.7 %all-gather.5.cloned.1.call-start = ((), (), s32[]{:S(2)}) async-start(), calls=%async_computation.1 | async-start | bytes 2359296 | tf_op jit(solution)/shard_map/all_gather | solution.py:42
  19.3 0.7 copy-start.1
  20.1 103.6 %all-gather.7.cloned.1.call-start = ((), (), s32[]{:S(2)}) async-start(), calls=%async_computation.2 | async-start | bytes 6635520 | tf_op jit(solution)/shard_map/all_gather | solution.py:89
  20.8 131.1 %reduce-scatter.2.cloned.1.call-start = ((), (), s32[]{:S(2)}) async-start(), calls=%async_computation.3 | async-start | bytes 921600 | tf_op jit(solution)/shard_map/reduce_scatter | solution.py:92
  53.9 2.0 %copy-start = (f32[2,512,128,8]{2,1,3,0:T(8,128)}, f32[2,512,128,8]{2,1,3,0:T(8,128)S(1)}, u32[]{:S(2)}) copy-start(f32[2,512,128,8]{2,1,3,0:T(8,128)S(1)} %get-tuple-element.212) | copy-start | bytes 12582916 | tf_op jit(solution)/shard_map/while
  63.0 2.0 %copy-start = (f32[2,512,128,8]{2,1,3,0:T(8,128)}, f32[2,512,128,8]{2,1,3,0:T(8,128)S(1)}, u32[]{:S(2)}) copy-start(f32[2,512,128,8]{2,1,3,0:T(8,128)S(1)} %get-tuple-element.212) | copy-start | bytes 12582916 | tf_op jit(solution)/shard_map/while
  72.0 2.0 %copy-start = (f32[2,512,128,8]{2,1,3,0:T(8,128)}, f32[2,512,128,8]{2,1,3,0:T(8,128)S(1)}, u32[]{:S(2)}) copy-start(f32[2,512,128,8]{2,1,3,0:T(8,128)S(1)} %get-tuple-element.212) | copy-start | bytes 12582916 | tf_op jit(solution)/shard_map/while
  81.2 2.0 %copy-start = (f32[2,512,128,8]{2,1,3,0:T(8,128)}, f32[2,512,128,8]{2,1,3,0:T(8,128)S(1)}, u32[]{:S(2)}) copy-start(f32[2,512,128,8]{2,1,3,0:T(8,128)S(1)} %get-tuple-element.212) | copy-start | bytes 12582916 | tf_op jit(solution)/shard_map/while
  90.3 2.0 %copy-start = (f32[2,512,128,8]{2,1,3,0:T(8,128)}, f32[2,512,128,8]{2,1,3,0:T(8,128)S(1)}, u32[]{:S(2)}) copy-start(f32[2,512,128,8]{2,1,3,0:T(8,128)S(1)} %get-tuple-element.212) | copy-start | bytes 12582916 | tf_op jit(solution)/shard_map/while
  99.4 2.0 %copy-start = (f32[2,512,128,8]{2,1,3,0:T(8,128)}, f32[2,512,128,8]{2,1,3,0:T(8,128)S(1)}, u32[]{:S(2)}) copy-start(f32[2,512,128,8]{2,1,3,0:T(8,128)S(1)} %get-tuple-element.212) | copy-start | bytes 12582916 | tf_op jit(solution)/shard_map/while
  108.4 2.0 %copy-start = (f32[2,512,128,8]{2,1,3,0:T(8,128)}, f32[2,512,128,8]{2,1,3,0:T(8,128)S(1)}, u32[]{:S(2)}) copy-start(f32[2,512,128,8]{2,1,3,0:T(8,128)S(1)} %get-tuple-element.212) | copy-start | bytes 12582916 | tf_op jit(solution)/shard_map/while
  117.5 2.0 %copy-start = (f32[2,512,128,8]{2,1,3,0:T(8,128)}, f32[2,512,128,8]{2,1,3,0:T(8,128)S(1)}, u32[]{:S(2)}) copy-start(f32[2,512,128,8]{2,1,3,0:T(8,128)S(1)} %get-tuple-element.212) | copy-start | bytes 12582916 | tf_op jit(solution)/shard_map/while
  123.6 28.2 %copy-start.2 = (f32[720]{0:T(1024)S(1)}, f32[720]{0:T(1024)}, u32[]{:S(2)}) copy-start(f32[720]{0:T(1024)} %param.21) | copy-start | bytes 8644
Sparse Core Ops, SparseCore 0:
  20.2 30.5 all-gather.4
  52.7 43.8 all-gather.6
  129.1 22.7 reduce-scatter.1
where the time goes:
time: 161 us; the launch traced here: 160 us
  local copies, waits for them, and re-layouts  42.5 us (26%)
  matrix products  36.9 us (23%)
  waiting for transfers between devices  30.4 us (19%)
  blocking collectives  19.2 us (12%)
  other arithmetic  16.4 us (10%)
  between operations  13.8 us (9%)
    dot_general x8, matrix products, one_block(): jnp.einsum('gqtc,cgd->gqtd', weights.astype(jnp.bfloat16), block_kv[:, :,...  25.5 us
    reduce_scatter x1, waiting for transfers between devices, shards(): lax.psum_scatter(partial_out.astype(jnp.bfloat16), 'gx', scatter_dimensio...  22.9 us
    while x24, local copies, waits for them, and re-layouts  15.9 us
    dynamic_slice x24, local copies, waits for them, and re-layouts, shards(): result, unused = lax.scan(one_block, initial, stacked)  10.5 us
    all_gather x1, blocking collectives, shards(): order_rows = lax.all_gather(slot_order, 'gy', axis=0, tiled=True)  10.4 us
    scatter x1, local copies, waits for them, and re-layouts, shards(): cache_out = kv_cache.at[target].set(new_kv, mode='drop')  9.75 us
    all_gather x1, blocking collectives, shards(): seg_rows = lax.all_gather(slot_seg, 'gy', axis=0, tiled=True)  8.88 us
    and x8, other arithmetic, one_block(): (block_seg[None, :] == token_seg[:, None]) & (block_order[None, :] <= tok...  6.87 us
  transfers between devices with their start and end apart: 3, of which 2 were waited for; matrix products, arithmetic and copies ran while one was open for 38% of the time, Pallas kernels for 0%

commit v1 on v0

--- a/solution.py
+++ b/solution.py
@@ -1,23 +1,244 @@
+import functools
 import math
 
 import jax
 import jax.numpy as jnp
 from jax import lax
+from jax.experimental import pallas as pl
+from jax.experimental.pallas import tpu as pltpu
 from jax.sharding import PartitionSpec as P
 
-
-def shards(
-    queries,
-    new_kv,
-    kv_cache,
-    cache_seg,
-    cache_slot,
-    token_seg,
-    pad_mask,
-    sink_logits,
-    out_weight,
-    out_bias,
-):
+F32 = jnp.float32
+BF16 = jnp.bfloat16
+HIDE = -1e30
+VMEM = pl.BlockSpec(memory_space=pltpu.VMEM)
+SMEM = pl.BlockSpec(memory_space=pltpu.SMEM)
+
+
+def iota(shape, dim):
+    return lax.broadcasted_iota(jnp.int32, shape, dim)
+
+
+def to_column(row):
+    n = row.shape[1]
+    eye = iota((n, n), 0) == iota((n, n), 1)
+    return jnp.sum(jnp.where(eye, row, 0.0), axis=1, keepdims=True)
+
+
+def dot_nt(a, b):
+    return lax.dot_general(a, b, (((1,), (1,)), ((), ())), preferred_element_type=F32)
+
+
+def prep_kernel(base_ref, kv_ref, new_ref, cseg_ref, slot_ref, tseg_ref, pad_ref, cache_ref, rows_ref):
+    slots, tokens = kv_ref.shape[0], new_ref.shape[0]
+    groups = kv_ref.shape[1] // 128
+    target = jnp.where(pad_ref[...] == 1, slot_ref[...] - base_ref[0], -1).astype(F32)
+    place = (iota((slots, tokens), 0).astype(F32) == target).astype(BF16)
+    moved = jnp.dot(place, new_ref[...], preferred_element_type=F32)
+    written = jnp.dot(place, jnp.ones((tokens, 128), BF16), preferred_element_type=F32)
+    written = jnp.concatenate([written] * groups, axis=1)
+    cache = jnp.where(written > 0.5, moved, kv_ref[...].astype(F32)).astype(BF16)
+    cache_ref[...] = cache
+
+    back = to_column(target) == iota((tokens, slots), 1).astype(F32)
+    order = jnp.sum(jnp.where(back, (iota((tokens, slots), 0) + 1).astype(F32), 0.0), axis=0, keepdims=True) - 1.0
+    new_seg = jnp.sum(jnp.where(back, to_column(tseg_ref[...].astype(F32)), 0.0), axis=0, keepdims=True)
+    seg = jnp.where(order >= 0.0, new_seg, cseg_ref[...].astype(F32))
+    lane = iota((1, slots), 1).astype(F32)
+    key = jnp.where(seg < 0.0, 64.0, seg) * slots + lane
+    rank = jnp.sum(jnp.where(to_column(key) < key, 1.0, 0.0), axis=0, keepdims=True)
+    perm = (iota((slots, slots), 0).astype(F32) == rank).astype(BF16)
+    rows = jnp.dot(perm, cache, preferred_element_type=F32).astype(BF16)
+    for g in range(groups):
+        rows_ref[g * slots : (g + 1) * slots, :] = rows[:, g * 128 : (g + 1) * 128]
+    sub = iota((8, slots), 0)
+    labels = jnp.where(sub == 0, seg, jnp.where(sub == 1, order, 0.0)).astype(BF16)
+    labels = dot_nt(labels, perm)
+    parts = [labels[r : r + 1, c : c + 128] for r in range(2) for c in range(0, slots, 128)]
+    parts.append(jnp.zeros((16 - len(parts), 128), F32))
+    rows_ref[groups * slots :, :] = jnp.concatenate(parts, axis=0).astype(BF16)
+
+
+def attend_kernel(first, last, count, *refs):
+    off_ref, sink_ref, q_ref, tseg_ref, pad_ref = refs[:5]
+    rows_refs = refs[5 : 5 + count]
+    rest = refs[5 + count :]
+    state_ref = None if first else rest[0]
+    out_ref = rest[0 if first else 1]
+    q_scr, = rest[(1 if first else 2) :]
+    tokens = q_ref.shape[0]
+    heads = q_ref.shape[1] // 64
+    groups = 2
+    slots = (rows_refs[0].shape[0] - 16) // groups
+    per = heads // groups
+    zero = jnp.zeros((tokens, 64), BF16)
+    scale = jnp.array(0.125, BF16)
+    for h in range(heads):
+        q_scr[h * tokens : (h + 1) * tokens, :] = jnp.concatenate([q_ref[:, h * 64 : h * 64 + 64] * scale, zero], axis=1)
+    tseg = to_column(tseg_ref[...].astype(F32))
+    tok = iota((tokens, 128), 0).astype(F32)
+    biases = []
+    for b in range(count):
+        meta = rows_refs[b][groups * slots :, :].astype(F32)
+        n = slots // 128
+        parts = []
+        for c in range(n):
+            seg, order = meta[c : c + 1, :], meta[n + c : n + c + 1, :]
+            seen = (seg == tseg) & ((order < 0.0) | (order + off_ref[b].astype(F32) <= tok))
+            parts.append(jnp.where(seen, 0.0, HIDE))
+        biases.append(jnp.concatenate(parts, axis=1))
+    left = iota((slots, 128), 1) < 64
+    lanes = iota((4 * tokens, 128), 1)
+    for g in range(groups):
+        keys = [rows_refs[b][g * slots : (g + 1) * slots, :] for b in range(count)]
+        vals = [jnp.where(left, jnp.ones_like(k), k) for k in keys]
+        for part in range(per // 4):
+            h0 = g * per + part * 4
+            q = q_scr[h0 * tokens : (h0 + 4) * tokens, :]
+            scores = []
+            for b in range(count):
+                s = dot_nt(q, keys[b]).reshape(4, tokens, slots) + biases[b][None]
+                scores.append(s.reshape(4 * tokens, slots))
+            if first:
+                peak = jnp.concatenate([jnp.full((tokens, 1), sink_ref[h0 + i], F32) for i in range(4)], axis=0)
+                total = jnp.where(lanes < 64, 1.0, 0.0)
+            else:
+                state = state_ref[h0 * tokens : (h0 + 4) * tokens, :]
+                peak = state[:, 32:33]
+                total = state
+            top = functools.reduce(jnp.maximum, [jnp.max(s, axis=1, keepdims=True) for s in scores], peak)
+            total = total * jnp.exp(peak - top)
+            for b in range(count):
+                weights = jnp.exp(scores[b] - top).astype(BF16)
+                total = total + jnp.dot(weights, vals[b], preferred_element_type=F32)
+            if not last:
+                out_ref[h0 * tokens : (h0 + 4) * tokens, :] = jnp.where((lanes >= 32) & (lanes < 64), top, total)
+            else:
+                live = to_column(pad_ref[...].astype(F32))
+                for i in range(0, 4, 2):
+                    pair = []
+                    for u in (i, i + 1):
+                        one = total[u * tokens : (u + 1) * tokens, :]
+                        pair.append(one[:, 64:128] / one[:, 0:1] * live)
+                    out_ref[:, (h0 + i) * 64 : (h0 + i + 2) * 64] = jnp.concatenate(pair, axis=1).astype(BF16)
+
+
+def attend(first, last, off, sink, q, tseg, pad, rows, state):
+    count = len(rows)
+    tokens, width = q.shape
+    heads = width // 64
+    out = jax.ShapeDtypeStruct((tokens, width), BF16) if last else jax.ShapeDtypeStruct((heads * tokens, 128), F32)
+    args = [off, sink, q, tseg, pad, *rows] + ([] if first else [state])
+    return pl.pallas_call(
+        functools.partial(attend_kernel, first, last, count),
+        out_shape=out,
+        in_specs=[SMEM, SMEM] + [VMEM] * (len(args) - 2),
+        out_specs=VMEM,
+        scratch_shapes=[pltpu.VMEM((heads * tokens, 128), BF16)],
+        compiler_params=pltpu.CompilerParams(vmem_limit_bytes=40 * 2**20),
+        cost_estimate=pl.CostEstimate(flops=4 * heads * tokens * 512 * count * 128, bytes_accessed=3 * 2**20, transcendentals=heads * tokens * 512 * count),
+    )(*args)
+
+
+def project_kernel(pos_ref, own_ref, other_ref, w0_ref, w1_ref, w2_ref, w3_ref, keep_a, keep_b, send_a, send_b):
+    core, swap = pos_ref[0], pos_ref[1]
+    tokens = own_ref.shape[0]
+    rows = jnp.concatenate([own_ref[...], other_ref[...]], axis=0)
+
+    def block(one, two):
+        a = jnp.dot(rows, one[...], preferred_element_type=F32).astype(BF16)
+        b = jnp.dot(rows, two[...], preferred_element_type=F32).astype(BF16)
+        return jnp.where(core == 0, jnp.concatenate([a, b], axis=1), jnp.concatenate([b, a], axis=1))
+
+    here, there = block(w0_ref, w1_ref), block(w2_ref, w3_ref)
+    a = jnp.where(swap == 0, here, there)
+    b = jnp.where(swap == 0, there, here)
+    keep_a[...] = a[:tokens]
+    send_a[...] = a[tokens:]
+    keep_b[...] = b[:tokens]
+    send_b[...] = b[tokens:]
+
+
+def tuned(queries, new_kv, kv_cache, cache_seg, cache_slot, token_seg, pad_mask, sink_logits, out_weight, out_bias):
+    tokens, slots = queries.shape[0], kv_cache.shape[0]
+    groups = kv_cache.shape[1]
+    plane, own = lax.axis_index("gx"), lax.axis_index("gy")
+    core, x, y = own % 2, (own // 2) % 2, own // 4
+
+    def gy(value, m):
+        return lax.ppermute(value, "gy", [(i, i ^ m) for i in range(8)])
+
+    def gx(value, m):
+        return lax.ppermute(value, "gx", [(i, i ^ m) for i in range(4)])
+
+    tseg, pad = token_seg.reshape(1, tokens), pad_mask.reshape(1, tokens)
+    cache, rows = pl.pallas_call(
+        prep_kernel,
+        out_shape=(
+            jax.ShapeDtypeStruct((slots, groups * 128), BF16),
+            jax.ShapeDtypeStruct((groups * slots + 16, 128), BF16),
+        ),
+        in_specs=[SMEM] + [VMEM] * 6,
+        out_specs=(VMEM, VMEM),
+        compiler_params=pltpu.CompilerParams(vmem_limit_bytes=32 * 2**20),
+    )(
+        (own * slots).reshape(1).astype(jnp.int32),
+        kv_cache.reshape(slots, groups * 128),
+        new_kv.reshape(tokens, groups * 128),
+        cache_seg.reshape(1, slots),
+        cache_slot.reshape(1, tokens),
+        tseg,
+        pad,
+    )
+    cache_out = cache.reshape(slots, groups, 128)
+
+    rows_x = gy(rows, 2)
+    rows_y = gy(rows, 4)
+    rows_d = gy(rows_x, 4)
+    near = [rows, gy(rows, 1)]
+    along_x = [rows_x, gy(rows_x, 1)]
+    along_y = [rows_y, gy(rows_y, 1)]
+    diagonal = [rows_d, gy(rows_d, 1)]
+    w1 = gy(out_weight, 1)
+    w2 = gy(out_weight, 2)
+    w3 = gy(w2, 1)
+
+    def offsets(m):
+        return jnp.stack([((own ^ m) - own) * tokens, ((own ^ m ^ 1) - own) * tokens]).astype(jnp.int32)
+
+    step = functools.partial(attend, sink=sink_logits, q=queries, tseg=tseg, pad=pad)
+    state = step(True, False, offsets(0), rows=near, state=None)
+    state = step(False, False, offsets(2), rows=along_x, state=state)
+    state = step(False, False, offsets(4), rows=along_y, state=state)
+    attention = step(False, True, offsets(6), rows=diagonal, state=state)
+    other = gy(attention, 4)
+
+    width = out_weight.shape[1] * 2
+    part = jax.ShapeDtypeStruct((tokens, width), BF16)
+    low = plane % 2
+    pos = jnp.stack([core, jnp.where(x == 1 - low, 0, 1)]).astype(jnp.int32)
+    keep_a, keep_b, send_a, send_b = pl.pallas_call(
+        project_kernel,
+        out_shape=(part,) * 4,
+        in_specs=[SMEM] + [VMEM] * 6,
+        out_specs=(VMEM,) * 4,
+        compiler_params=pltpu.CompilerParams(vmem_limit_bytes=32 * 2**20),
+    )(pos, attention, other, out_weight, w1, w2, w3)
+
+    got_a = gy(send_a, 4)
+    got_z = gx(keep_a, 1)
+    got_b = gy(send_b, 4)
+    got_w = gx(got_a, 1)
+    mine = keep_b.astype(F32) + got_z.astype(F32)
+    theirs = got_b.astype(F32) + got_w.astype(F32)
+    same = y == plane // 2
+    final = jnp.where(same, mine, theirs)
+    away = jnp.where(same, theirs, mine).astype(BF16)
+    got = gx(away, 2)
+    return (final + got.astype(F32) + out_bias).astype(BF16), cache_out
+
+
+def plain(queries, new_kv, kv_cache, cache_seg, cache_slot, token_seg, pad_mask, sink_logits, out_weight, out_bias):
     local_tokens = queries.shape[0]
     local_slots = kv_cache.shape[0]
     local_groups = kv_cache.shape[1]
@@ -54,16 +275,9 @@
     def one_block(running, block_data):
         run_peak, weight_sum, weighted = running
         block_kv, block_seg, block_order = block_data
-        visible = (block_seg[None, :] == token_seg[:, None]) & (
-            block_order[None, :] <= token_index[:, None]
-        )
+        visible = (block_seg[None, :] == token_seg[:, None]) & (block_order[None, :] <= token_index[:, None])
         scores = (
-            jnp.einsum(
-                "tgqd,cgd->gqtc",
-                query_heads,
-                block_kv[:, :, :head_dim],
-                preferred_element_type=jnp.float32,
-            )
+            jnp.einsum("tgqd,cgd->gqtc", query_heads, block_kv[:, :, :head_dim], preferred_element_type=jnp.float32)
             * scale
         )
         new_peak = jnp.maximum(run_peak, jnp.max(jnp.where(visible, scores, -jnp.inf), axis=-1))
@@ -85,9 +299,7 @@
     )
     attention = (attn_heads * pad_mask[:, None].astype(jnp.float32)).astype(jnp.bfloat16)
     partial_out = jnp.dot(
-        attention,
-        lax.all_gather(out_weight, "gy", axis=1, tiled=True),
-        preferred_element_type=jnp.float32,
+        attention, lax.all_gather(out_weight, "gy", axis=1, tiled=True), preferred_element_type=jnp.float32
     )
     summed = lax.psum_scatter(
         partial_out.astype(jnp.bfloat16), "gx", scatter_dimension=1, tiled=True
@@ -108,8 +320,9 @@
         P("gx", "gy"),
         P("gx"),
     )
+    small = mesh.shape["gy"] == 8 and mesh.shape["gx"] == 4
     return jax.shard_map(
-        shards,
+        tuned if small else plain,
         mesh=mesh,
         in_specs=placed,
         out_specs=(P("gy", "gx"), P("gy", "gx", None)),

time: 161 us -> 89.2 us (0.55)
  matrix products: 36.9 us -> 0 us
  local copies, waits for them, and re-layouts: 42.5 us -> 9.73 us
  Pallas kernels: 0 us -> 22.6 us
  blocking collectives: 19.2 us -> 0 us
  starting transfers between devices: 0.12 us -> 17.5 us
  other arithmetic: 16.4 us -> 0.61 us
  between operations: 13.8 us -> 0.89 us
  waiting for transfers between devices: 30.4 us -> 37.5 us
    ppermute x0 -> x16, waiting for transfers between devices: none -> 37.5 us  [the longest x13 29.8 us: gy(): return lax.ppermute(value, 'gy', [(i, i ^ m) for i in range(8)])]
    dot_general x17 -> x0, matrix products: 36.9 us -> none  [the longest x8 25.5 us: one_block(): jnp.einsum('gqtc,cgd->gqtd', weights.astype(jnp.bfloat16), block_kv[:, :,...]
    reduce_scatter x1 -> x0, waiting for transfers between devices: 22.9 us -> none  [shards(): lax.psum_scatter(partial_out.astype(jnp.bfloat16), 'gx', scatter_dimensio...]
    pallas_call x0 -> x6, Pallas kernels: none -> 22.6 us  [the longest x4 18.8 us: attend(): pl.pallas_call(functools.partial(attend_kernel, first, last, count), out_...]
    all_gather x2 -> x0, blocking collectives: 19.2 us -> none  [the longest x1 10.4 us: shards(): order_rows = lax.all_gather(slot_order, 'gy', axis=0, tiled=True)]
    ppermute x0 -> x16, starting transfers between devices: none -> 17.5 us  [the longest x13 11.3 us: gy(): return lax.ppermute(value, 'gy', [(i, i ^ m) for i in range(8)])]
    while x24 -> x0, local copies, waits for them, and re-layouts: 15.9 us -> none
    scatter x3 -> x0, local copies, waits for them, and re-layouts: 11.8 us -> none  [the longest x1 9.75 us: shards(): cache_out = kv_cache.at[target].set(new_kv, mode='drop')]
  transfers between devices with their start and end apart: 3 -> 16, of which waited for: 2 -> 7; matrix products, arithmetic and copies ran while one was open for 38% -> 8% of each run, Pallas kernels for 0% -> 22%
where the time goes in v1:
time: 89.2 us; the launch traced here: 88.8 us
  waiting for transfers between devices  37.5 us (42%)
  Pallas kernels  22.6 us (25%)
  starting transfers between devices  17.5 us (20%)
  local copies, waits for them, and re-layouts  9.73 us (11%)
    ppermute x13, waiting for transfers between devices, gy(): return lax.ppermute(value, 'gy', [(i, i ^ m) for i in range(8)])  29.8 us
    pallas_call x4, Pallas kernels, attend(): pl.pallas_call(functools.partial(attend_kernel, first, last, count), out_...  18.8 us
    ppermute x13, starting transfers between devices, gy(): return lax.ppermute(value, 'gy', [(i, i ^ m) for i in range(8)])  11.3 us
    ppermute x3, waiting for transfers between devices, gx(): return lax.ppermute(value, 'gx', [(i, i ^ m) for i in range(4)])  7.72 us
    ppermute x3, starting transfers between devices, gx(): return lax.ppermute(value, 'gx', [(i, i ^ m) for i in range(4)])  6.2 us
    unnamed x30, local copies, waits for them, and re-layouts  4.56 us
    ppermute x3, local copies, waits for them, and re-layouts, gy(): return lax.ppermute(value, 'gy', [(i, i ^ m) for i in range(8)])  4.41 us
    pallas_call x1, Pallas kernels, tuned(): pl.pallas_call(project_kernel, out_shape=(part,) * 4, in_specs=[SMEM] + [...  3 us
  transfers between devices with their start and end apart: 16, of which 7 were waited for; matrix products, arithmetic and copies ran while one was open for 8% of the time, Pallas kernels for 22%

profile of v1, /device:TPU:0, one launch (start us, length us, event | category | flops | bytes accessed | tf_op | source)
XLA Modules:
  0.0 88.8 jit_solution(14466938379774415077)
XLA Ops:
  0.6 3.0 %collective-permute-start.9 = (bf16[1024,360]{0,1:T(8,128)(2,1)}, bf16[1024,360]{0,1:T(8,128)(2,1)}, u32[]{:S(2)}, u32[]{:S(2)}) collective-permute-start(bf16[1024,360]{0,1:T(8,128)(2,1)} %param.18), channel_id=1, source_target_pairs={{0,2},{1,3},{2,0},{3,1},{4,6},{5,7},{6,4},{7,5},{8,10},{9,11},{10,... | collective-permute-start | bytes 2211848 | tf_op jit(solution)/shard_map/ppermute | solution.py:169
  3.6 1.0 %copy.25 = bf16[64,8,2,128]{3,1,2,0:T(8,128)(2,1)S(1)} copy(bf16[64,8,2,128]{3,2,1,0:T(2,128)(2,1)} %bitcast.36) | data formatting | bytes 524288
  4.7 0.0 copy-start.4
  4.7 0.0 copy-start.5
  4.7 0.0 copy-start.7
  4.8 0.6 copy-done.4
  5.4 0.0 copy-done.7
  5.4 0.7 shard_map.113
  6.2 0.7 copy-done
  6.9 0.0 collective-permute-start
  6.9 2.0 %collective-permute-start.3 = (bf16[1040,128]{1,0:T(8,128)(2,1)S(1)}, bf16[1040,128]{1,0:T(8,128)(2,1)S(1)}, u32[]{:S(2)}, u32[]{:S(2)}) collective-permute-start(bf16[1040,128]{1,0:T(8,128)(2,1)S(1)} %get-tuple-element.8.refs_5_), channel_id=1, source_target_pairs={{0,4},{1,5},{2,6},{3,7},{4,0},{5,1},{6,2},{7,3},{8,12},{9,13},{10,... | collective-permute-start | bytes 798728 | tf_op jit(solution)/shard_map/ppermute | solution.py:169
  8.9 0.1 pad_add_fusion.4.refs_0_
  9.0 17.0 %collective-permute-done.refs_5_ = bf16[1040,128]{1,0:T(8,128)(2,1)S(1)} collective-permute-done((bf16[1040,128]{1,0:T(8,128)(2,1)S(1)}, bf16[1040,128]{1,0:T(8,128)(2,1)S(1)}, u32[]{:S(2)}, u32[]{:S(2)}) %collective-permute-start) | collective-permute-done | bytes 266272 | tf_op jit(solution)/shard_map/ppermute | solution.py:169
  26.0 1.8 %collective-permute-start.1 = (bf16[1040,128]{1,0:T(8,128)(2,1)S(1)}, bf16[1040,128]{1,0:T(8,128)(2,1)S(1)}, u32[]{:S(2)}, u32[]{:S(2)}) collective-permute-start(bf16[1040,128]{1,0:T(8,128)(2,1)S(1)} %collective-permute-done.refs_5_), channel_id=1, source_target_pairs={{0,4},{1,5},{2,6},{3,7},{4,0},{5,1},{6,2},{7,3},{8,12},{9,13},{10,... | collective-permute-start | bytes 798728 | tf_op jit(solution)/shard_map/ppermute | solution.py:169
  27.8 0.1 pad_add_fusion.3.refs_0_
  27.9 0.1 pad_add_fusion.2.refs_0_
  28.0 0.5 collective-permute-start.8
  28.5 0.1 collective-permute-start.4
  28.6 0.4 collective-permute-start.10
  29.0 0.1 pad_add_fusion.1.refs_0_
  29.1 4.6 %collective-permute-done.1.refs_5_ = bf16[1040,128]{1,0:T(8,128)(2,1)S(1)} collective-permute-done((bf16[1040,128]{1,0:T(8,128)(2,1)S(1)}, bf16[1040,128]{1,0:T(8,128)(2,1)S(1)}, u32[]{:S(2)}, u32[]{:S(2)}) %collective-permute-start.1) | collective-permute-done | bytes 266272 | tf_op jit(solution)/shard_map/ppermute | solution.py:169
  33.6 4.5 %shard_map.114.refs_7_ = f32[2048,128]{1,0:T(8,128)S(1)} custom-call(s32[2]{0:T(128)S(1)} %pad_add_fusion.4.refs_0_, f32[16]{0:T(128)S(1)} %copy-done.9, bf16[128,1024]{1,0:T(8,128)(2,1)S(1)} %copy-done.8, s32[1,128]{1,0:T(1,128)S(1)} %bitcast.27, s32[1,128]{1,0:T(1,128)S(1)} %bitcast.32, bf16[1040,128]{1,0:T(8,128)(2,1)S(1)} %get-tuple-element.8.refs_5_, ...), custom_call_target="tpu_custom_call" | custom-call | flops 1073741824 | bytes 3145728 | tf_op jit(solution)/shard_map/pallas_call | solution.py:132
  38.2 4.7 %shard_map.115.refs_7_ = f32[2048,128]{1,0:T(8,128)S(1)} custom-call(s32[2]{0:T(128)S(1)} %pad_add_fusion.3.refs_0_, f32[16]{0:T(128)S(1)} %copy-done.9, bf16[128,1024]{1,0:T(8,128)(2,1)S(1)} %copy-done.8, s32[1,128]{1,0:T(1,128)S(1)} %bitcast.28, s32[1,128]{1,0:T(1,128)S(1)} %bitcast.33, bf16[1040,128]{1,0:T(8,128)(2,1)S(1)} %collective-permute-done.refs_5_, ...), custom_call_target="tpu_custom_call" | custom-call | flops 1073741824 | bytes 3145728 | tf_op jit(solution)/shard_map/pallas_call | solution.py:132
  42.8 4.9 %shard_map.116.refs_7_ = f32[2048,128]{1,0:T(8,128)S(1)} custom-call(s32[2]{0:T(128)S(1)} %pad_add_fusion.2.refs_0_, f32[16]{0:T(128)S(1)} %copy-done.9, bf16[128,1024]{1,0:T(8,128)(2,1)S(1)} %copy-done.8, s32[1,128]{1,0:T(1,128)S(1)} %bitcast.29, s32[1,128]{1,0:T(1,128)S(1)} %bitcast.34, bf16[1040,128]{1,0:T(8,128)(2,1)S(1)} %collective-permute-done.3.refs_5_, ...), custom_call_target="tpu_custom_call" | custom-call | flops 1073741824 | bytes 3145728 | tf_op jit(solution)/shard_map/pallas_call | solution.py:132
  47.8 4.8 %shard_map.117.own_ref = bf16[128,1024]{1,0:T(8,128)(2,1)S(1)} custom-call(s32[2]{0:T(128)S(1)} %pad_add_fusion.1.refs_0_, f32[16]{0:T(128)S(1)} %copy-done.9, bf16[128,1024]{1,0:T(8,128)(2,1)S(1)} %copy-done.8, s32[1,128]{1,0:T(1,128)S(1)} %bitcast.30, s32[1,128]{1,0:T(1,128)S(1)} %bitcast.35, bf16[1040,128]{1,0:T(8,128)(2,1)S(1)} %collective-permute-done.1.refs_5_, ...), custom_call_target="tpu_custom_call" | custom-call | flops 1073741824 | bytes 3145728 | tf_op jit(solution)/shard_map/pallas_call | solution.py:132
  52.5 0.0 copy-start.2
  52.6 1.5 %collective-permute-start.7 = (bf16[128,1024]{1,0:T(8,128)(2,1)S(1)}, bf16[128,1024]{1,0:T(8,128)(2,1)}, u32[]{:S(2)}, u32[]{:S(2)}) collective-permute-start(bf16[128,1024]{1,0:T(8,128)(2,1)S(1)} %shard_map.117.own_ref), channel_id=1, source_target_pairs={{0,4},{1,5},{2,6},{3,7},{4,0},{5,1},{6,2},{7,3},{8,12},{9,13},{10,... | collective-permute-start | bytes 786440 | tf_op jit(solution)/shard_map/ppermute | solution.py:169
  54.1 0.4 copy.16.w0_ref
  54.5 0.1 pad_add_fusion.pos_ref
  54.5 1.5 %copy.18.w2_ref = bf16[1024,360]{1,0:T(8,128)(2,1)S(1)} copy(bf16[1024,360]{0,1:T(8,128)(2,1)} %collective-permute-done.9) | data formatting | bytes 1474560 | tf_op jit(solution)/shard_map/ppermute | solution.py:169
  56.0 1.5 %copy.17.w1_ref = bf16[1024,360]{1,0:T(8,128)(2,1)S(1)} copy(bf16[1024,360]{0,1:T(8,128)(2,1)} %collective-permute-done.8) | data formatting | bytes 1474560 | tf_op jit(solution)/shard_map/ppermute | solution.py:169
  57.5 1.5 %copy.19.w3_ref = bf16[1024,360]{1,0:T(8,128)(2,1)S(1)} copy(bf16[1024,360]{0,1:T(8,128)(2,1)} %collective-permute-done.10) | data formatting | bytes 1474560 | tf_op jit(solution)/shard_map/ppermute | solution.py:169
  59.0 2.4 %collective-permute-done.7.other_ref = bf16[128,1024]{1,0:T(8,128)(2,1)} collective-permute-done((bf16[128,1024]{1,0:T(8,128)(2,1)S(1)}, bf16[128,1024]{1,0:T(8,128)(2,1)}, u32[]{:S(2)}, u32[]{:S(2)}) %collective-permute-start.7) | collective-permute-done | bytes 262176 | tf_op jit(solution)/shard_map/ppermute | solution.py:169
  61.4 0.9 %copy-done.3 = bf16[128,1024]{1,0:T(8,128)(2,1)S(1)} copy-done((bf16[128,1024]{1,0:T(8,128)(2,1)S(1)}, bf16[128,1024]{1,0:T(8,128)(2,1)}, u32[]{:S(2)}) %copy-start.3) | copy-done | bytes 262168
  62.4 3.0 %shard_map.118 = (bf16[128,720]{1,0:T(8,128)(2,1)}, bf16[128,720]{1,0:T(8,128)(2,1)S(1)}, bf16[128,720]{1,0:T(8,128)(2,1)S(1)}, bf16[128,720]{1,0:T(8,128)(2,1)}) custom-call(s32[2]{0:T(128)S(1)} %pad_add_fusion.pos_ref, bf16[128,1024]{1,0:T(8,128)(2,1)S(1)} %copy-done.3, bf16[128,1024]{1,0:T(8,128)(2,1)} %collective-permute-done.7.other_ref, ...), custom_call_target="tpu_custom_call" | custom-call | tf_op jit(solution)/shard_map/pallas_call | solution.py:220
  65.4 1.5 %collective-permute-start.13 = (bf16[128,720]{1,0:T(8,128)(2,1)S(1)}, bf16[128,720]{1,0:T(8,128)(2,1)S(1)}, u32[]{:S(2)}, u32[]{:S(2)}) collective-permute-start(bf16[128,720]{1,0:T(8,128)(2,1)S(1)} %get-tuple-element.12), channel_id=1, source_target_pairs={{0,4},{1,5},{2,6},{3,7},{4,0},{5,1},{6,2},{7,3},{8,12},{9,13},{10,... | collective-permute-start | bytes 552968 | tf_op jit(solution)/shard_map/ppermute | solution.py:169
  66.8 1.6 %collective-permute-start.11 = (bf16[128,720]{1,0:T(8,128)(2,1)}, bf16[128,720]{1,0:T(8,128)(2,1)S(1)}, u32[]{:S(2)}, u32[]{:S(2)}) collective-permute-start(bf16[128,720]{1,0:T(8,128)(2,1)} %get-tuple-element.10), channel_id=1, source_target_pairs={{0,8},{8,0},{16,24},{24,16},{1,9},{9,1},{17,25},{25,17},{2,10},{10... | collective-permute-start | bytes 552968 | tf_op jit(solution)/shard_map/ppermute | solution.py:172
  68.4 0.5 collective-permute-start.12
  68.9 4.3 %collective-permute-done.13 = bf16[128,720]{1,0:T(8,128)(2,1)S(1)} collective-permute-done((bf16[128,720]{1,0:T(8,128)(2,1)S(1)}, bf16[128,720]{1,0:T(8,128)(2,1)S(1)}, u32[]{:S(2)}, u32[]{:S(2)}) %collective-permute-start.13) | collective-permute-done | bytes 184352 | tf_op jit(solution)/shard_map/ppermute | solution.py:169
  73.2 1.5 %collective-permute-start.14 = (bf16[128,720]{1,0:T(8,128)(2,1)S(1)}, bf16[128,720]{1,0:T(8,128)(2,1)S(1)}, u32[]{:S(2)}, u32[]{:S(2)}) collective-permute-start(bf16[128,720]{1,0:T(8,128)(2,1)S(1)} %collective-permute-done.13), channel_id=1, source_target_pairs={{0,8},{8,0},{16,24},{24,16},{1,9},{9,1},{17,25},{25,17},{2,10},{10... | collective-permute-start | bytes 552968 | tf_op jit(solution)/shard_map/ppermute | solution.py:172
  74.7 1.4 %collective-permute-done.12 = bf16[128,720]{1,0:T(8,128)(2,1)S(1)} collective-permute-done((bf16[128,720]{1,0:T(8,128)(2,1)}, bf16[128,720]{1,0:T(8,128)(2,1)S(1)}, u32[]{:S(2)}, u32[]{:S(2)}) %collective-permute-start.12) | collective-permute-done | bytes 184352 | tf_op jit(solution)/shard_map/ppermute | solution.py:169
  76.1 2.7 %collective-permute-done.14 = bf16[128,720]{1,0:T(8,128)(2,1)S(1)} collective-permute-done((bf16[128,720]{1,0:T(8,128)(2,1)S(1)}, bf16[128,720]{1,0:T(8,128)(2,1)S(1)}, u32[]{:S(2)}, u32[]{:S(2)}) %collective-permute-start.14) | collective-permute-done | bytes 184352 | tf_op jit(solution)/shard_map/ppermute | solution.py:172
  78.9 0.1 select_convert_fusion
  79.0 3.1 %collective-permute-start.15 = (bf16[128,720]{1,0:T(8,128)(2,1)S(1)}, bf16[128,720]{1,0:T(8,128)(2,1)S(1)}, u32[]{:S(2)}, u32[]{:S(2)}) collective-permute-start(bf16[128,720]{1,0:T(8,128)(2,1)S(1)} %select_convert_fusion), channel_id=1, source_target_pairs={{0,16},{8,24},{16,0},{24,8},{1,17},{9,25},{17,1},{25,9},{2,18},{10... | collective-permute-start | bytes 552968 | tf_op jit(solution)/shard_map/ppermute | solution.py:172
  82.1 0.8 reshape.36
  82.9 5.0 %collective-permute-done.15 = bf16[128,720]{1,0:T(8,128)(2,1)S(1)} collective-permute-done((bf16[128,720]{1,0:T(8,128)(2,1)S(1)}, bf16[128,720]{1,0:T(8,128)(2,1)S(1)}, u32[]{:S(2)}, u32[]{:S(2)}) %collective-permute-start.15) | collective-permute-done | bytes 184352 | tf_op jit(solution)/shard_map/ppermute | solution.py:172
  87.9 0.1 add_convert_fusion
  88.0 0.8 copy.20
  (31 shorter events, 0.1 us)
Async XLA Ops:
  0.6 27.9 %collective-permute-start.9 = (bf16[1024,360]{0,1:T(8,128)(2,1)}, bf16[1024,360]{0,1:T(8,128)(2,1)}, u32[]{:S(2)}, u32[]{:S(2)}) collective-permute-start(bf16[1024,360]{0,1:T(8,128)(2,1)} %param.18), channel_id=1, source_target_pairs={{0,2},{1,3},{2,0},{3,1},{4,6},{5,7},{6,4},{7,5},{8,10},{9,11},{10,... | collective-permute-start | bytes 2211848 | tf_op jit(solution)/shard_map/ppermute | solution.py:169
  3.6 1.0 %copy-start.11 = (bf16[128,2,128]{2,1,0:T(2,128)(2,1)S(1)}, bf16[128,2,128]{2,1,0:T(2,128)(2,1)}, u32[]{:S(2)}) copy-start(bf16[128,2,128]{2,1,0:T(2,128)(2,1)} %param.11) | copy-start | bytes 196612
  3.6 30.0 %copy-start.8 = (bf16[128,1024]{1,0:T(8,128)(2,1)S(1)}, bf16[128,1024]{1,0:T(8,128)(2,1)}, u32[]{:S(2)}) copy-start(bf16[128,1024]{1,0:T(8,128)(2,1)} %refs_2_.7) | copy-start | bytes 786436
  4.7 0.7 copy-start.4
  4.7 0.7 copy-start.5
  4.7 0.7 copy-start.6
  4.7 0.7 copy-start.7
  6.2 0.7 copy-start
  6.9 19.2 %collective-permute-start = (bf16[1040,128]{1,0:T(8,128)(2,1)S(1)}, bf16[1040,128]{1,0:T(8,128)(2,1)S(1)}, u32[]{:S(2)}, u32[]{:S(2)}) collective-permute-start(bf16[1040,128]{1,0:T(8,128)(2,1)S(1)} %get-tuple-element.8.refs_5_), channel_id=1, source_target_pairs={{0,2},{1,3},{2,0},{3,1},{4,6},{5,7},{6,4},{7,5},{8,10},{9,11},{10,... | collective-permute-start | bytes 798728 | tf_op jit(solution)/shard_map/ppermute | solution.py:169
  6.9 21.1 %collective-permute-start.6 = (bf16[1040,128]{1,0:T(8,128)(2,1)S(1)}, bf16[1040,128]{1,0:T(8,128)(2,1)S(1)}, u32[]{:S(2)}, u32[]{:S(2)}) collective-permute-start(bf16[1040,128]{1,0:T(8,128)(2,1)S(1)} %get-tuple-element.8.refs_5_), channel_id=1, source_target_pairs={{0,1},{1,0},{2,3},{3,2},{4,5},{5,4},{6,7},{7,6},{8,9},{9,8},{10,11... | collective-permute-start | bytes 798728 | tf_op jit(solution)/shard_map/ppermute | solution.py:169
  6.9 21.6 %collective-permute-start.3 = (bf16[1040,128]{1,0:T(8,128)(2,1)S(1)}, bf16[1040,128]{1,0:T(8,128)(2,1)S(1)}, u32[]{:S(2)}, u32[]{:S(2)}) collective-permute-start(bf16[1040,128]{1,0:T(8,128)(2,1)S(1)} %get-tuple-element.8.refs_5_), channel_id=1, source_target_pairs={{0,4},{1,5},{2,6},{3,7},{4,0},{5,1},{6,2},{7,3},{8,12},{9,13},{10,... | collective-permute-start | bytes 798728 | tf_op jit(solution)/shard_map/ppermute | solution.py:169
  26.0 7.6 %collective-permute-start.1 = (bf16[1040,128]{1,0:T(8,128)(2,1)S(1)}, bf16[1040,128]{1,0:T(8,128)(2,1)S(1)}, u32[]{:S(2)}, u32[]{:S(2)}) collective-permute-start(bf16[1040,128]{1,0:T(8,128)(2,1)S(1)} %collective-permute-done.refs_5_), channel_id=1, source_target_pairs={{0,4},{1,5},{2,6},{3,7},{4,0},{5,1},{6,2},{7,3},{8,12},{9,13},{10,... | collective-permute-start | bytes 798728 | tf_op jit(solution)/shard_map/ppermute | solution.py:169
  27.9 10.3 %collective-permute-start.5 = (bf16[1040,128]{1,0:T(8,128)(2,1)S(1)}, bf16[1040,128]{1,0:T(8,128)(2,1)S(1)}, u32[]{:S(2)}, u32[]{:S(2)}) collective-permute-start(bf16[1040,128]{1,0:T(8,128)(2,1)S(1)} %collective-permute-done.refs_5_), channel_id=1, source_target_pairs={{0,1},{1,0},{2,3},{3,2},{4,5},{5,4},{6,7},{7,6},{8,9},{9,8},{10,11... | collective-permute-start | bytes 798728 | tf_op jit(solution)/shard_map/ppermute | solution.py:169
  28.0 28.1 %collective-permute-start.8 = (bf16[1024,360]{0,1:T(8,128)(2,1)}, bf16[1024,360]{0,1:T(8,128)(2,1)}, u32[]{:S(2)}, u32[]{:S(2)}) collective-permute-start(bf16[1024,360]{0,1:T(8,128)(2,1)} %param.18), channel_id=1, source_target_pairs={{0,1},{1,0},{2,3},{3,2},{4,5},{5,4},{6,7},{7,6},{8,9},{9,8},{10,11... | collective-permute-start | bytes 2211848 | tf_op jit(solution)/shard_map/ppermute | solution.py:169
  28.5 14.4 %collective-permute-start.4 = (bf16[1040,128]{1,0:T(8,128)(2,1)S(1)}, bf16[1040,128]{1,0:T(8,128)(2,1)S(1)}, u32[]{:S(2)}, u32[]{:S(2)}) collective-permute-start(bf16[1040,128]{1,0:T(8,128)(2,1)S(1)} %collective-permute-done.3.refs_5_), channel_id=1, source_target_pairs={{0,1},{1,0},{2,3},{3,2},{4,5},{5,4},{6,7},{7,6},{8,9},{9,8},{10,11... | collective-permute-start | bytes 798728 | tf_op jit(solution)/shard_map/ppermute | solution.py:169
  28.6 28.9 %collective-permute-start.10 = (bf16[1024,360]{0,1:T(8,128)(2,1)}, bf16[1024,360]{0,1:T(8,128)(2,1)}, u32[]{:S(2)}, u32[]{:S(2)}) collective-permute-start(bf16[1024,360]{0,1:T(8,128)(2,1)} %collective-permute-done.9), channel_id=1, source_target_pairs={{0,1},{1,0},{2,3},{3,2},{4,5},{5,4},{6,7},{7,6},{8,9},{9,8},{10,11... | collective-permute-start | bytes 2211848 | tf_op jit(solution)/shard_map/ppermute | solution.py:169
  29.0 4.6 %copy-start.9 = (f32[16]{0:T(128)S(1)}, f32[16]{0:T(128)}, u32[]{:S(2)}) copy-start(f32[16]{0:T(128)} %refs_1_.7) | copy-start | bytes 196
  33.6 14.1 %collective-permute-start.2 = (bf16[1040,128]{1,0:T(8,128)(2,1)S(1)}, bf16[1040,128]{1,0:T(8,128)(2,1)S(1)}, u32[]{:S(2)}, u32[]{:S(2)}) collective-permute-start(bf16[1040,128]{1,0:T(8,128)(2,1)S(1)} %collective-permute-done.1.refs_5_), channel_id=1, source_target_pairs={{0,1},{1,0},{2,3},{3,2},{4,5},{5,4},{6,7},{7,6},{8,9},{9,8},{10,11... | collective-permute-start | bytes 798728 | tf_op jit(solution)/shard_map/ppermute | solution.py:169
  47.7 6.3 %copy-start.10 = (bf16[1024,360]{0,1:T(8,128)(2,1)S(1)}, bf16[1024,360]{0,1:T(8,128)(2,1)}, u32[]{:S(2)}) copy-start(bf16[1024,360]{0,1:T(8,128)(2,1)} %param.18) | copy-start | bytes 2211844
  52.5 1.9 %copy-start.2 = (bf16[128,1024]{1,0:T(8,128)(2,1)}, bf16[128,1024]{1,0:T(8,128)(2,1)S(1)}, u32[]{:S(2)}) copy-start(bf16[128,1024]{1,0:T(8,128)(2,1)S(1)} %shard_map.117.own_ref) | copy-start | bytes 786436
  52.6 8.9 %collective-permute-start.7 = (bf16[128,1024]{1,0:T(8,128)(2,1)S(1)}, bf16[128,1024]{1,0:T(8,128)(2,1)}, u32[]{:S(2)}, u32[]{:S(2)}) collective-permute-start(bf16[128,1024]{1,0:T(8,128)(2,1)S(1)} %shard_map.117.own_ref), channel_id=1, source_target_pairs={{0,4},{1,5},{2,6},{3,7},{4,0},{5,1},{6,2},{7,3},{8,12},{9,13},{10,... | collective-permute-start | bytes 786440 | tf_op jit(solution)/shard_map/ppermute | solution.py:169
  61.4 1.0 %copy-start.3 = (bf16[128,1024]{1,0:T(8,128)(2,1)S(1)}, bf16[128,1024]{1,0:T(8,128)(2,1)}, u32[]{:S(2)}) copy-start(bf16[128,1024]{1,0:T(8,128)(2,1)} %copy-done.2) | copy-start | bytes 786436
  65.4 7.8 %collective-permute-start.13 = (bf16[128,720]{1,0:T(8,128)(2,1)S(1)}, bf16[128,720]{1,0:T(8,128)(2,1)S(1)}, u32[]{:S(2)}, u32[]{:S(2)}) collective-permute-start(bf16[128,720]{1,0:T(8,128)(2,1)S(1)} %get-tuple-element.12), channel_id=1, source_target_pairs={{0,4},{1,5},{2,6},{3,7},{4,0},{5,1},{6,2},{7,3},{8,12},{9,13},{10,... | collective-permute-start | bytes 552968 | tf_op jit(solution)/shard_map/ppermute | solution.py:169
  66.8 7.9 %collective-permute-start.11 = (bf16[128,720]{1,0:T(8,128)(2,1)}, bf16[128,720]{1,0:T(8,128)(2,1)S(1)}, u32[]{:S(2)}, u32[]{:S(2)}) collective-permute-start(bf16[128,720]{1,0:T(8,128)(2,1)} %get-tuple-element.10), channel_id=1, source_target_pairs={{0,8},{8,0},{16,24},{24,16},{1,9},{9,1},{17,25},{25,17},{2,10},{10... | collective-permute-start | bytes 552968 | tf_op jit(solution)/shard_map/ppermute | solution.py:172
  68.4 7.7 %collective-permute-start.12 = (bf16[128,720]{1,0:T(8,128)(2,1)}, bf16[128,720]{1,0:T(8,128)(2,1)S(1)}, u32[]{:S(2)}, u32[]{:S(2)}) collective-permute-start(bf16[128,720]{1,0:T(8,128)(2,1)} %get-tuple-element.11), channel_id=1, source_target_pairs={{0,4},{1,5},{2,6},{3,7},{4,0},{5,1},{6,2},{7,3},{8,12},{9,13},{10,... | collective-permute-start | bytes 552968 | tf_op jit(solution)/shard_map/ppermute | solution.py:169
  73.2 5.7 %collective-permute-start.14 = (bf16[128,720]{1,0:T(8,128)(2,1)S(1)}, bf16[128,720]{1,0:T(8,128)(2,1)S(1)}, u32[]{:S(2)}, u32[]{:S(2)}) collective-permute-start(bf16[128,720]{1,0:T(8,128)(2,1)S(1)} %collective-permute-done.13), channel_id=1, source_target_pairs={{0,8},{8,0},{16,24},{24,16},{1,9},{9,1},{17,25},{25,17},{2,10},{10... | collective-permute-start | bytes 552968 | tf_op jit(solution)/shard_map/ppermute | solution.py:172
  78.9 3.2 %copy-start.1 = (bf16[512,256]{1,0:T(8,128)(2,1)S(1)}, bf16[512,256]{1,0:T(8,128)(2,1)}, u32[]{:S(2)}) copy-start(bf16[512,256]{1,0:T(8,128)(2,1)} %copy-done) | copy-start | bytes 786436
  79.0 8.9 %collective-permute-start.15 = (bf16[128,720]{1,0:T(8,128)(2,1)S(1)}, bf16[128,720]{1,0:T(8,128)(2,1)S(1)}, u32[]{:S(2)}, u32[]{:S(2)}) collective-permute-start(bf16[128,720]{1,0:T(8,128)(2,1)S(1)} %select_convert_fusion), channel_id=1, source_target_pairs={{0,16},{8,24},{16,0},{24,8},{1,17},{9,25},{17,1},{25,9},{2,18},{10... | collective-permute-start | bytes 552968 | tf_op jit(solution)/shard_map/ppermute | solution.py:172
  82.1 5.8 %copy-start.12 = (f32[720]{0:T(1024)S(1)}, f32[720]{0:T(1024)}, u32[]{:S(2)}) copy-start(f32[720]{0:T(1024)} %param.19) | copy-start | bytes 8644

commit v2 on v0

--- a/solution.py
+++ b/solution.py
@@ -1,23 +1,321 @@
+import functools
 import math
 
 import jax
 import jax.numpy as jnp
 from jax import lax
+from jax.experimental import pallas as pl
+from jax.experimental.pallas import tpu as pltpu
 from jax.sharding import PartitionSpec as P
 
-
-def shards(
-    queries,
-    new_kv,
-    kv_cache,
-    cache_seg,
-    cache_slot,
-    token_seg,
-    pad_mask,
-    sink_logits,
-    out_weight,
-    out_bias,
-):
+F32 = jnp.float32
+BF16 = jnp.bfloat16
+HIDE = -1e30
+VMEM = pl.BlockSpec(memory_space=pltpu.VMEM)
+SMEM = pl.BlockSpec(memory_space=pltpu.SMEM)
+HBM = pl.BlockSpec(memory_space=pltpu.HBM)
+
+
+def iota(shape, dim):
+    return lax.broadcasted_iota(jnp.int32, shape, dim)
+
+
+def to_column(row):
+    n = row.shape[1]
+    eye = iota((n, n), 0) == iota((n, n), 1)
+    return jnp.sum(jnp.where(eye, row, 0.0), axis=1, keepdims=True)
+
+
+def dot_nt(a, b):
+    return lax.dot_general(a, b, (((1,), (1,)), ((), ())), preferred_element_type=F32)
+
+
+def merged(base_ref, kv_ref, new_ref, slot_ref, pad_ref):
+    slots, tokens = kv_ref.shape[0], new_ref.shape[0]
+    groups = kv_ref.shape[1] // 128
+    target = jnp.where(pad_ref[...] == 1, slot_ref[...] - base_ref[0], -1).astype(F32)
+    place = (iota((slots, tokens), 0).astype(F32) == target).astype(BF16)
+    moved = jnp.dot(place, new_ref[...], preferred_element_type=F32)
+    written = jnp.dot(place, jnp.ones((tokens, 128), BF16), preferred_element_type=F32)
+    written = jnp.concatenate([written] * groups, axis=1)
+    return jnp.where(written > 0.5, moved, kv_ref[...].astype(F32)).astype(BF16), target
+
+
+def cache_kernel(base_ref, kv_ref, new_ref, slot_ref, pad_ref, cache_ref):
+    cache_ref[...] = merged(base_ref, kv_ref, new_ref, slot_ref, pad_ref)[0]
+
+
+def sort_kernel(base_ref, *refs):
+    sources, rows_ref, held, arrived = refs[:6], refs[6], refs[7:13], refs[13]
+    copies = [pltpu.make_async_copy(a, b, arrived.at[i]) for i, (a, b) in enumerate(zip(sources, held))]
+    for copy in copies:
+        copy.start()
+    for copy in copies:
+        copy.wait()
+    kv_ref, new_ref, slot_ref, pad_ref, cseg_ref, tseg_ref = held
+    slots, tokens = kv_ref.shape[0], new_ref.shape[0]
+    groups = kv_ref.shape[1] // 128
+    cache, target = merged(base_ref, kv_ref, new_ref, slot_ref, pad_ref)
+    back = to_column(target) == iota((tokens, slots), 1).astype(F32)
+    order = jnp.sum(jnp.where(back, (iota((tokens, slots), 0) + 1).astype(F32), 0.0), axis=0, keepdims=True) - 1.0
+    new_seg = jnp.sum(jnp.where(back, to_column(tseg_ref[...].astype(F32)), 0.0), axis=0, keepdims=True)
+    seg = jnp.where(order >= 0.0, new_seg, cseg_ref[...].astype(F32))
+    lane = iota((1, slots), 1).astype(F32)
+    key = jnp.where(seg < 0.0, 64.0, seg) * slots + lane
+    rank = jnp.sum(jnp.where(to_column(key) < key, 1.0, 0.0), axis=0, keepdims=True)
+    perm = (iota((slots, slots), 0).astype(F32) == rank).astype(BF16)
+    rows = jnp.dot(perm, cache, preferred_element_type=F32).astype(BF16)
+    wide = groups * 128
+    lane, turn = iota((128, wide), 1), iota((128, wide), 0)
+    lane = lane - (turn // 64) * 128
+    turn = turn % 64
+    rows_ref[:slots, :] = dot_nt(rows, (lane == turn).astype(BF16)).astype(BF16)
+    vals = dot_nt((lane == turn + 64).astype(BF16), rows).astype(BF16)
+    for c in range(slots // 128):
+        rows_ref[slots + c * 128 : slots + (c + 1) * 128, :] = vals[:, c * 128 : (c + 1) * 128]
+    sub = iota((8, slots), 0)
+    labels = jnp.where(sub == 0, seg, jnp.where(sub == 1, order, 0.0)).astype(BF16)
+    labels = dot_nt(labels, perm)
+    parts = [labels[r : r + 1, c : c + 128] for r in range(2) for c in range(0, slots, 128)]
+    parts.append(jnp.zeros((16 - len(parts), 128), F32))
+    rows_ref[2 * slots :, :] = jnp.concatenate(parts, axis=0).astype(BF16)
+
+
+def attend_kernel(first, last, count, *refs):
+    off_ref, sink_ref, seg_ref, q_ref, tseg_ref, pad_ref = refs[:6]
+    rows_refs = refs[6 : 6 + count]
+    given_ref, out_ref, extra_ref, q_scr, key_scr, val_scr, bias_scr, acc_scr, moved = refs[6 + count :]
+    if first:
+        load = pltpu.make_async_copy(given_ref, extra_ref, moved.at[0])
+    else:
+        load = pltpu.make_async_copy(given_ref, acc_scr, moved.at[0])
+        extra_ref[...] = jnp.zeros_like(extra_ref)
+    load.start()
+    tokens = q_ref.shape[1]
+    heads = q_ref.shape[0] // 64
+    slots = (rows_refs[0].shape[0] - 16) // 2
+    tiles = slots // 128
+    zero = jnp.zeros((64, tokens), BF16)
+    scale = jnp.array(0.125, BF16)
+    for h in range(heads):
+        q = q_ref[h * 64 : (h + 1) * 64, :] * scale
+        pair = [q, zero] if h < heads // 2 else [zero, q]
+        q_scr[:, h * tokens : (h + 1) * tokens] = jnp.concatenate(pair, axis=0)
+    tseg = tseg_ref[...].astype(F32)
+    tok = iota((128, tokens), 1).astype(F32)
+    low, high = seg_ref[0].astype(F32), seg_ref[tokens - 1].astype(F32)
+
+    eye = (iota((128, 128), 0) == iota((128, 128), 1)).astype(BF16)
+    row = iota((16, 128), 0)
+    labels, flags = [], jnp.zeros((16, 1), F32)
+    for b in range(count):
+        meta = rows_refs[b][2 * slots :, :]
+        labels.append(dot_nt(eye, meta))
+        meta = meta.astype(F32)
+        hit = jnp.where((meta >= low) & (meta <= high) & (row < tiles), 1.0, 0.0)
+        place = jnp.left_shift(1, iota((16, 1), 0) + b * tiles).astype(F32)
+        flags = flags + jnp.max(hit, axis=1, keepdims=True) * place
+    flags = jnp.sum(flags).astype(jnp.int32)
+
+    used = jnp.int32(0)
+    for b in range(count):
+        for c in range(tiles):
+            wanted = ((flags >> (b * tiles + c)) & 1) == 1
+
+            @pl.when(wanted)
+            def _(b=b, c=c, used=used):
+                seg, order = labels[b][:, c : c + 1], labels[b][:, tiles + c : tiles + c + 1]
+                seen = (seg == tseg) & ((order < 0.0) | (order + off_ref[b].astype(F32) <= tok))
+                at = pl.multiple_of(used * 128, 128)
+                bias_scr[pl.ds(at, 128), :] = jnp.where(seen, 0.0, HIDE)
+                key_scr[pl.ds(at, 128), :] = rows_refs[b][c * 128 : (c + 1) * 128, :]
+                val_scr[:, pl.ds(at, 128)] = rows_refs[b][slots + c * 128 : slots + (c + 1) * 128, :]
+
+            used = used + wanted.astype(jnp.int32)
+    for extra in range(1):
+        at = pl.multiple_of(used * 128, 128)
+        bias_scr[pl.ds(at, 128), :] = jnp.full((128, tokens), HIDE, F32)
+        key_scr[pl.ds(at, 128), :] = jnp.zeros((128, 128), BF16)
+        val_scr[:, pl.ds(at, 128)] = jnp.zeros((128, 128), BF16)
+
+    if first:
+        for h in range(heads):
+            span = slice(h * tokens, (h + 1) * tokens)
+            acc_scr[:64, span] = jnp.zeros((64, tokens), F32)
+            acc_scr[64:72, span] = jnp.ones((8, tokens), F32)
+            acc_scr[72:80, span] = jnp.full((8, tokens), sink_ref[h], F32)
+    else:
+        load.wait()
+    half = heads // 2 * tokens
+
+    def pair(index, carry):
+        at = pl.multiple_of(index * 256, 256)
+        keys = key_scr[pl.ds(at, 256), :]
+        bias = jnp.concatenate([bias_scr[pl.ds(at, 256), :]] * (heads // 2), axis=1)
+        ones = jnp.ones((16, 256), BF16)
+        spans = [slice(group * half, (group + 1) * half) for group in range(2)]
+        scores = [jnp.dot(keys, q_scr[:, span], preferred_element_type=F32) + bias for span in spans]
+        peaks = [acc_scr[72:73, span] for span in spans]
+        tops = [jnp.maximum(jnp.max(s, axis=0, keepdims=True), p) for s, p in zip(scores, peaks)]
+        weights = [jnp.exp(s - t).astype(BF16) for s, t in zip(scores, tops)]
+        for group, span in enumerate(spans):
+            vals = jnp.concatenate([val_scr[group * 64 : (group + 1) * 64, pl.ds(at, 256)], ones], axis=0)
+            new = jnp.dot(vals, weights[group], preferred_element_type=F32)[:72, :]
+            acc_scr[:72, span] = acc_scr[:72, span] * jnp.exp(peaks[group] - tops[group]) + new
+            acc_scr[72:80, span] = jnp.broadcast_to(tops[group], (8, half))
+        return carry
+
+    lax.fori_loop(0, (used + 1) // 2, pair, 0)
+    if not last:
+        save = pltpu.make_async_copy(acc_scr, out_ref, moved.at[1])
+        save.start()
+        save.wait()
+        if first:
+            load.wait()
+    else:
+        live = pad_ref[...].astype(F32)
+        for h in range(heads):
+            span = slice(h * tokens, (h + 1) * tokens)
+            out_ref[h * 64 : (h + 1) * 64, :] = (acc_scr[:64, span] / acc_scr[64:65, span] * live).astype(BF16)
+
+
+def attend(first, last, off, sink, q, seg, tseg, pad, rows, given):
+    count = len(rows)
+    width, tokens = q.shape
+    heads = width // 64
+    slots = (rows[0].shape[0] - 16) // 2
+    out = jax.ShapeDtypeStruct((width, tokens), BF16) if last else jax.ShapeDtypeStruct((80, heads * tokens), F32)
+    args = [off, sink, seg, q, tseg, pad, *rows, given]
+    extra = jax.ShapeDtypeStruct(given.shape, given.dtype) if first else jax.ShapeDtypeStruct((8, 128), F32)
+    return pl.pallas_call(
+        functools.partial(attend_kernel, first, last, count),
+        out_shape=(out, extra),
+        in_specs=[SMEM] * 3 + [VMEM] * (3 + count) + [HBM],
+        out_specs=(VMEM if last else HBM, HBM if first else VMEM),
+        scratch_shapes=[
+            pltpu.VMEM((128, heads * tokens), BF16),
+            pltpu.VMEM((count * slots + 256, 128), BF16),
+            pltpu.VMEM((128, count * slots + 256), BF16),
+            pltpu.VMEM((count * slots + 256, tokens), F32),
+            pltpu.VMEM((80, heads * tokens), F32),
+            pltpu.SemaphoreType.DMA((2,)),
+        ],
+        compiler_params=pltpu.CompilerParams(vmem_limit_bytes=16 * 2**20),
+        cost_estimate=pl.CostEstimate(
+            flops=4 * heads * tokens * slots * count * 128,
+            bytes_accessed=3 * 2**20,
+            transcendentals=heads * tokens * slots * count,
+        ),
+    )(*args)
+
+
+def project_kernel(pos_ref, rows_ref, w0_ref, w1_ref, w2_ref, w3_ref, a_ref, b_ref):
+    core, swap = pos_ref[0], pos_ref[1]
+    rows = rows_ref[...]
+
+    def block(one, two):
+        a = jnp.dot(one[...], rows, preferred_element_type=F32)
+        b = jnp.dot(two[...], rows, preferred_element_type=F32)
+        return jnp.where(core == 0, jnp.concatenate([a, b], axis=0), jnp.concatenate([b, a], axis=0)).astype(BF16)
+
+    here, there = block(w0_ref, w1_ref), block(w2_ref, w3_ref)
+    a_ref[...] = jnp.where(swap == 0, here, there)
+    b_ref[...] = jnp.where(swap == 0, there, here)
+
+
+def tuned(queries, new_kv, kv_cache, cache_seg, cache_slot, token_seg, pad_mask, sink_logits, out_weight, out_bias):
+    tokens, slots = queries.shape[0], kv_cache.shape[0]
+    groups = kv_cache.shape[1]
+    plane, own = lax.axis_index("gx"), lax.axis_index("gy")
+    core, x, y = own % 2, (own // 2) % 2, own // 4
+
+    def gy(value, m):
+        return lax.ppermute(value, "gy", [(i, i ^ m) for i in range(8)])
+
+    def gx(value, m):
+        return lax.ppermute(value, "gx", [(i, i ^ m) for i in range(4)])
+
+    tseg, pad = token_seg.reshape(1, tokens), pad_mask.reshape(1, tokens)
+    store = [
+        (own * slots).reshape(1).astype(jnp.int32),
+        kv_cache.reshape(slots, groups * 128),
+        new_kv.reshape(tokens, groups * 128),
+        cache_slot.reshape(1, tokens),
+        pad,
+    ]
+    rows = pl.pallas_call(
+        sort_kernel,
+        out_shape=jax.ShapeDtypeStruct((groups * slots + 16, 128), BF16),
+        in_specs=[SMEM] + [HBM] * 6,
+        out_specs=VMEM,
+        scratch_shapes=[
+            pltpu.VMEM((slots, groups * 128), BF16),
+            pltpu.VMEM((tokens, groups * 128), BF16),
+            pltpu.VMEM((1, tokens), jnp.int32),
+            pltpu.VMEM((1, tokens), jnp.int32),
+            pltpu.VMEM((1, slots), jnp.int32),
+            pltpu.VMEM((1, tokens), jnp.int32),
+            pltpu.SemaphoreType.DMA((6,)),
+        ],
+        compiler_params=pltpu.CompilerParams(vmem_limit_bytes=16 * 2**20),
+    )(*store, cache_seg.reshape(1, slots), tseg)
+
+    rows_x = gy(rows, 2)
+    rows_y = gy(rows, 4)
+    near = [rows, gy(rows, 1)]
+    w0 = out_weight.T
+
+    def offsets(m):
+        return jnp.stack([((own ^ m) - own) * tokens, ((own ^ m ^ 1) - own) * tokens]).astype(jnp.int32)
+
+    turned = queries.T
+    step = functools.partial(attend, sink=sink_logits, q=turned, seg=token_seg, tseg=tseg, pad=pad)
+    state, sent = step(True, False, offsets(0), rows=near, given=w0)
+    rows_d = gy(rows_x, 4)
+    w2 = gy(sent, 2)
+    along = [rows_x, gy(rows_x, 1), rows_y, gy(rows_y, 1)]
+    both = jnp.concatenate([offsets(2), offsets(4)])
+    state, done = step(False, False, both, rows=along, given=state)
+    w1 = gy(sent, 1)
+    diagonal = [rows_d, gy(rows_d, 1)]
+    attention, done = step(False, True, offsets(6), rows=diagonal, given=state)
+    other = gy(attention, 4)
+    w2 = w2 + done[0, 0].astype(BF16)
+    w3 = gy(w2, 1)
+
+    part = jax.ShapeDtypeStruct((out_weight.shape[1] * 2, tokens), BF16)
+    pos = jnp.stack([core, jnp.where(x == 1 - plane % 2, 0, 1)]).astype(jnp.int32)
+    project = pl.pallas_call(
+        project_kernel,
+        out_shape=(part, part),
+        in_specs=[SMEM] + [VMEM] * 5,
+        out_specs=(VMEM, VMEM),
+        compiler_params=pltpu.CompilerParams(vmem_limit_bytes=16 * 2**20),
+        cost_estimate=pl.CostEstimate(flops=2 * 1024 * 1440 * 256, bytes_accessed=4 * 2**20, transcendentals=0),
+    )
+    keep_a, keep_b = project(pos, attention, w0, w1, w2, w3)
+    got_k = gx(keep_a, 1)
+    send_a, send_b = project(pos, other, w0, w1, w2, w3)
+    got_s = gx(send_a, 1)
+    got = gy((send_b.astype(F32) + got_s.astype(F32)).astype(BF16), 4)
+    cache = pl.pallas_call(
+        cache_kernel,
+        out_shape=jax.ShapeDtypeStruct((slots, groups * 128), BF16),
+        in_specs=[SMEM] + [VMEM] * 4,
+        out_specs=VMEM,
+        compiler_params=pltpu.CompilerParams(vmem_limit_bytes=16 * 2**20),
+    )(*store)
+    mine = keep_b.astype(F32) + got_k.astype(F32)
+    theirs = got.astype(F32)
+    same = y == plane // 2
+    final = jnp.where(same, mine, theirs)
+    away = jnp.where(same, theirs, mine).astype(BF16)
+    last = gx(away, 2)
+    out = (final + last.astype(F32) + out_bias[:, None]).astype(BF16)
+    return out.T, cache.reshape(slots, groups, 128)
+
+
+def plain(queries, new_kv, kv_cache, cache_seg, cache_slot, token_seg, pad_mask, sink_logits, out_weight, out_bias):
     local_tokens = queries.shape[0]
     local_slots = kv_cache.shape[0]
     local_groups = kv_cache.shape[1]
@@ -54,16 +352,9 @@
     def one_block(running, block_data):
         run_peak, weight_sum, weighted = running
         block_kv, block_seg, block_order = block_data
-        visible = (block_seg[None, :] == token_seg[:, None]) & (
-            block_order[None, :] <= token_index[:, None]
-        )
+        visible = (block_seg[None, :] == token_seg[:, None]) & (block_order[None, :] <= token_index[:, None])
         scores = (
-            jnp.einsum(
-                "tgqd,cgd->gqtc",
-                query_heads,
-                block_kv[:, :, :head_dim],
-                preferred_element_type=jnp.float32,
-            )
+            jnp.einsum("tgqd,cgd->gqtc", query_heads, block_kv[:, :, :head_dim], preferred_element_type=jnp.float32)
             * scale
         )
         new_peak = jnp.maximum(run_peak, jnp.max(jnp.where(visible, scores, -jnp.inf), axis=-1))
@@ -85,9 +376,7 @@
     )
     attention = (attn_heads * pad_mask[:, None].astype(jnp.float32)).astype(jnp.bfloat16)
     partial_out = jnp.dot(
-        attention,
-        lax.all_gather(out_weight, "gy", axis=1, tiled=True),
-        preferred_element_type=jnp.float32,
+        attention, lax.all_gather(out_weight, "gy", axis=1, tiled=True), preferred_element_type=jnp.float32
     )
     summed = lax.psum_scatter(
         partial_out.astype(jnp.bfloat16), "gx", scatter_dimension=1, tiled=True
@@ -108,8 +397,9 @@
         P("gx", "gy"),
         P("gx"),
     )
+    small = mesh.shape["gy"] == 8 and mesh.shape["gx"] == 4
     return jax.shard_map(
-        shards,
+        tuned if small else plain,
         mesh=mesh,
         in_specs=placed,
         out_specs=(P("gy", "gx"), P("gy", "gx", None)),

time: 161 us -> 73.1 us (0.45)
  local copies, waits for them, and re-layouts: 42.5 us -> 5.12 us
  matrix products: 36.9 us -> 0 us
  Pallas kernels: 0 us -> 19.9 us
  starting transfers between devices: 0.12 us -> 19.6 us
  blocking collectives: 19.2 us -> 0 us
  other arithmetic: 16.4 us -> 3.09 us
  between operations: 13.8 us -> 0.87 us
  waiting for transfers between devices: 30.4 us -> 24.5 us
    dot_general x17 -> x0, matrix products: 36.9 us -> none  [the longest x8 25.5 us: one_block(): jnp.einsum('gqtc,cgd->gqtd', weights.astype(jnp.bfloat16), block_kv[:, :,...]
    ppermute x0 -> x15, waiting for transfers between devices: none -> 24.5 us  [the longest x12 14.4 us: gy(): return lax.ppermute(value, 'gy', [(i, i ^ m) for i in range(8)])]
    reduce_scatter x1 -> x0, waiting for transfers between devices: 22.9 us -> none  [shards(): lax.psum_scatter(partial_out.astype(jnp.bfloat16), 'gx', scatter_dimensio...]
    pallas_call x0 -> x7, Pallas kernels: none -> 19.9 us  [the longest x3 13.9 us: attend(): pl.pallas_call(functools.partial(attend_kernel, first, last, count), out_...]
    ppermute x0 -> x15, starting transfers between devices: none -> 19.6 us  [the longest x12 14.9 us: gy(): return lax.ppermute(value, 'gy', [(i, i ^ m) for i in range(8)])]
    all_gather x2 -> x0, blocking collectives: 19.2 us -> none  [the longest x1 10.4 us: shards(): order_rows = lax.all_gather(slot_order, 'gy', axis=0, tiled=True)]
    while x24 -> x0, local copies, waits for them, and re-layouts: 15.9 us -> none
    scatter x3 -> x0, local copies, waits for them, and re-layouts: 11.8 us -> none  [the longest x1 9.75 us: shards(): cache_out = kv_cache.at[target].set(new_kv, mode='drop')]
  transfers between devices with their start and end apart: 3 -> 15, of which waited for: 2 -> 6; matrix products, arithmetic and copies ran while one was open for 38% -> 5% of each run, Pallas kernels for 0% -> 23%
where the time goes in v2:
time: 73.1 us; the launch traced here: 73 us
  waiting for transfers between devices  24.5 us (34%)
  Pallas kernels  19.9 us (27%)
  starting transfers between devices  19.6 us (27%)
  local copies, waits for them, and re-layouts  5.12 us (7%)
  other arithmetic  3.09 us (4%)
  between operations  0.87 us (1%)
    ppermute x12, starting transfers between devices, gy(): return lax.ppermute(value, 'gy', [(i, i ^ m) for i in range(8)])  14.9 us
    ppermute x12, waiting for transfers between devices, gy(): return lax.ppermute(value, 'gy', [(i, i ^ m) for i in range(8)])  14.4 us
    pallas_call x3, Pallas kernels, attend(): pl.pallas_call(functools.partial(attend_kernel, first, last, count), out_...  13.9 us
    ppermute x3, waiting for transfers between devices, gx(): return lax.ppermute(value, 'gx', [(i, i ^ m) for i in range(4)])  10 us
    ppermute x3, starting transfers between devices, gx(): return lax.ppermute(value, 'gx', [(i, i ^ m) for i in range(4)])  4.77 us
    unnamed x25, local copies, waits for them, and re-layouts  3.84 us
    pallas_call x1, Pallas kernels, tuned(): keep_a, keep_b = project(pos, attention, w0, w1, w2, w3)  2.58 us
    pallas_call x1, Pallas kernels, tuned(): send_a, send_b = project(pos, other, w0, w1, w2, w3)  1.9 us
  transfers between devices with their start and end apart: 15, of which 6 were waited for; matrix products, arithmetic and copies ran while one was open for 5% of the time, Pallas kernels for 23%

profile of v2, /device:TPU:0, one launch (start us, length us, event | category | flops | bytes accessed | tf_op | source)
XLA Modules:
  0.0 73.0 jit_solution(17357406979992497110)
XLA Ops:
  0.7 1.0 %copy.17 = bf16[64,8,2,128]{3,1,2,0:T(8,128)(2,1)S(1)} copy(bf16[64,8,2,128]{3,2,1,0:T(2,128)(2,1)} %bitcast.49) | data formatting | bytes 524288
  1.7 0.0 copy-start
  1.8 1.3 %shard_map.113.refs_6_ = bf16[1040,128]{1,0:T(8,128)(2,1)S(1)} custom-call(s32[1]{0:T(128)} %bitcast.7.base_ref, bf16[512,256]{1,0:T(8,128)(2,1)S(1)} %bitcast.30, bf16[128,256]{1,0:T(8,128)(2,1)S(1)} %bitcast.32, s32[1,128]{1,0:T(1,128)S(1)} %bitcast.43, s32[1,128]{1,0:T(1,128)S(1)} %bitcast.38, s32[1,512]{1,0:T(1,128)S(1)} %bitcast.37, s32[1,128]{1,0:T(1,128)S(1)} %bitcast.45), custom_call_target="tpu_custom_call" | custom-call | tf_op jit(solution)/shard_map/pallas_call | solution.py:246
  3.1 0.5 collective-permute-start.6
  3.6 2.6 %collective-permute-start = (bf16[1040,128]{1,0:T(8,128)(2,1)S(1)}, bf16[1040,128]{1,0:T(8,128)(2,1)S(1)}, u32[]{:S(2)}, u32[]{:S(2)}) collective-permute-start(bf16[1040,128]{1,0:T(8,128)(2,1)S(1)} %shard_map.113.refs_6_), channel_id=1, source_target_pairs={{0,2},{1,3},{2,0},{3,1},{4,6},{5,7},{6,4},{7,5},{8,10},{9,11},{10,... | collective-permute-start | bytes 798728 | tf_op jit(solution)/shard_map/ppermute | solution.py:233
  6.2 1.5 %collective-permute-start.4 = (bf16[1040,128]{1,0:T(8,128)(2,1)S(1)}, bf16[1040,128]{1,0:T(8,128)(2,1)S(1)}, u32[]{:S(2)}, u32[]{:S(2)}) collective-permute-start(bf16[1040,128]{1,0:T(8,128)(2,1)S(1)} %shard_map.113.refs_6_), channel_id=1, source_target_pairs={{0,4},{1,5},{2,6},{3,7},{4,0},{5,1},{6,2},{7,3},{8,12},{9,13},{10,... | collective-permute-start | bytes 798728 | tf_op jit(solution)/shard_map/ppermute | solution.py:233
  7.7 0.2 copy.12
  7.9 0.1 pad_add_fusion.3.refs_0_
  8.0 0.7 copy-done.5
  8.6 3.5 %shard_map.114 = (f32[80,2048]{1,0:T(8,128)S(1)}, bf16[360,1024]{1,0:T(8,128)(2,1)}) custom-call(s32[2]{0:T(128)S(1)} %pad_add_fusion.3.refs_0_, f32[16]{0:T(128)S(1)} %copy-done.5, s32[128]{0:T(128)S(1)} %copy-done.4, bf16[1024,128]{1,0:T(8,128)(2,1)S(1)} %bitcast.34, s32[1,128]{1,0:T(1,128)S(1)} %bitcast.46, s32[1,128]{1,0:T(1,128)S(1)} %bitcast.39, ...), custom_call_target="tpu_custom_call" | custom-call | flops 1073741824 | bytes 3145728 | tf_op jit(solution)/shard_map/pallas_call | solution.py:190
  12.1 0.8 %copy-done.6 = f32[80,2048]{1,0:T(8,128)} copy-done((f32[80,2048]{1,0:T(8,128)}, f32[80,2048]{1,0:T(8,128)S(1)}, u32[]{:S(2)}) %copy-start.6) | copy-done | bytes 655384
  12.9 0.5 collective-permute-start.8
  13.5 1.7 %collective-permute-start.1 = (bf16[1040,128]{1,0:T(8,128)(2,1)S(1)}, bf16[1040,128]{1,0:T(8,128)(2,1)}, u32[]{:S(2)}, u32[]{:S(2)}) collective-permute-start(bf16[1040,128]{1,0:T(8,128)(2,1)S(1)} %collective-permute-done.refs_6_), channel_id=1, source_target_pairs={{0,4},{1,5},{2,6},{3,7},{4,0},{5,1},{6,2},{7,3},{8,12},{9,13},{10,... | collective-permute-start | bytes 798728 | tf_op jit(solution)/shard_map/ppermute | solution.py:233
  15.2 0.5 collective-permute-start.5
  15.7 0.1 pad_add_fusion.1.refs_0_
  15.8 5.7 %collective-permute-done.1.refs_6_ = bf16[1040,128]{1,0:T(8,128)(2,1)} collective-permute-done((bf16[1040,128]{1,0:T(8,128)(2,1)S(1)}, bf16[1040,128]{1,0:T(8,128)(2,1)}, u32[]{:S(2)}, u32[]{:S(2)}) %collective-permute-start.1) | collective-permute-done | bytes 266272 | tf_op jit(solution)/shard_map/ppermute | solution.py:233
  21.5 0.0 collective-permute-start.2
  21.5 0.1 pad_add_fusion.2.refs_0_
  21.5 0.5 collective-permute-start.7
  22.1 0.0 collective-permute-done.3.refs_7_
  22.1 0.0 collective-permute-done.5.refs_9_
  22.1 1.1 %copy-done.7 = f32[80,2048]{1,0:T(8,128)S(1)} copy-done((f32[80,2048]{1,0:T(8,128)S(1)}, f32[80,2048]{1,0:T(8,128)}, u32[]{:S(2)}) %copy-start.7) | copy-done | bytes 655384
  23.2 7.0 %shard_map.115 = (f32[80,2048]{1,0:T(8,128)S(1)}, f32[8,128]{1,0:T(8,128)}) custom-call(s32[4]{0:T(128)S(1)} %pad_add_fusion.2.refs_0_, f32[16]{0:T(128)S(1)} %copy-done.5, s32[128]{0:T(128)S(1)} %copy-done.4, bf16[1024,128]{1,0:T(8,128)(2,1)S(1)} %bitcast.35, s32[1,128]{1,0:T(1,128)S(1)} %bitcast.47, s32[1,128]{1,0:T(1,128)S(1)} %bitcast.40, ...), custom_call_target="tpu_custom_call" | custom-call | flops 2147483648 | bytes 3145728 | tf_op jit(solution)/shard_map/pallas_call | solution.py:190
  30.1 0.0 collective-permute-done.2.refs_7_
  30.1 3.4 %shard_map.116 = (bf16[1024,128]{1,0:T(8,128)(2,1)}, f32[8,128]{1,0:T(8,128)S(1)}) custom-call(s32[2]{0:T(128)S(1)} %pad_add_fusion.1.refs_0_, f32[16]{0:T(128)S(1)} %copy-done.5, s32[128]{0:T(128)S(1)} %copy-done.4, bf16[1024,128]{1,0:T(8,128)(2,1)S(1)} %bitcast.36, s32[1,128]{1,0:T(1,128)S(1)} %bitcast.48, s32[1,128]{1,0:T(1,128)S(1)} %bitcast.41, ...), custom_call_target="tpu_custom_call" | custom-call | flops 1073741824 | bytes 3145728 | tf_op jit(solution)/shard_map/pallas_call | solution.py:190
  33.6 0.5 slice.4
  34.1 0.0 collective-permute-done.8
  34.1 1.8 %broadcast_add_fusion.w2_ref = bf16[360,1024]{1,0:T(8,128)(2,1)S(1)} fusion(bf16[360,1024]{1,0:T(8,128)(2,1)} %collective-permute-done.8, bf16[]{:T(256)} %bitcast.16), kind=kLoop, calls=%fused_computation.8 | loop fusion | flops 368640 | bytes 1474562 | tf_op jit(solution)/shard_map/add | solution.py:283
  35.9 0.1 collective-permute-start.9
  36.0 5.3 %collective-permute-start.11 = (bf16[1024,128]{1,0:T(8,128)(2,1)}, bf16[1024,128]{1,0:T(8,128)(2,1)}, u32[]{:S(2)}, u32[]{:S(2)}) collective-permute-start(bf16[1024,128]{1,0:T(8,128)(2,1)} %get-tuple-element.13.rows_ref), channel_id=1, source_target_pairs={{0,4},{1,5},{2,6},{3,7},{4,0},{5,1},{6,2},{7,3},{8,12},{9,13},{10,... | collective-permute-start | bytes 786440 | tf_op jit(solution)/shard_map/ppermute | solution.py:233
  41.3 0.1 pad_add_fusion.pos_ref
  41.4 7.1 %collective-permute-done.11.rows_ref = bf16[1024,128]{1,0:T(8,128)(2,1)} collective-permute-done((bf16[1024,128]{1,0:T(8,128)(2,1)}, bf16[1024,128]{1,0:T(8,128)(2,1)}, u32[]{:S(2)}, u32[]{:S(2)}) %collective-permute-start.11) | collective-permute-done | bytes 262176 | tf_op jit(solution)/shard_map/ppermute | solution.py:233
  48.5 1.9 %shard_map.118 = (bf16[720,128]{1,0:T(8,128)(2,1)S(1)}, bf16[720,128]{1,0:T(8,128)(2,1)S(1)}) custom-call(s32[2]{0:T(128)S(1)} %pad_add_fusion.pos_ref, bf16[1024,128]{1,0:T(8,128)(2,1)} %collective-permute-done.11.rows_ref, bf16[360,1024]{1,0:T(8,128)(2,1)S(1)} %bitcast.28, bf16[360,1024]{1,0:T(8,128)(2,1)S(1)} %collective-permute-done.7.w1_ref, ...), custom_call_target="tpu_custom_call" | custom-call | flops 754974720 | bytes 4194304 | tf_op jit(solution)/shard_map/pallas_call | solution.py:298
  50.4 1.6 %collective-permute-start.12 = (bf16[720,128]{1,0:T(8,128)(2,1)S(1)}, bf16[720,128]{1,0:T(8,128)(2,1)S(1)}, u32[]{:S(2)}, u32[]{:S(2)}) collective-permute-start(bf16[720,128]{1,0:T(8,128)(2,1)S(1)} %get-tuple-element.19), channel_id=1, source_target_pairs={{0,8},{8,0},{16,24},{24,16},{1,9},{9,1},{17,25},{25,17},{2,10},{10... | collective-permute-start | bytes 552968 | tf_op jit(solution)/shard_map/ppermute | solution.py:236
  52.0 2.6 %shard_map.117 = (bf16[720,128]{1,0:T(8,128)(2,1)}, bf16[720,128]{1,0:T(8,128)(2,1)S(1)}) custom-call(s32[2]{0:T(128)S(1)} %pad_add_fusion.pos_ref, bf16[1024,128]{1,0:T(8,128)(2,1)} %get-tuple-element.13.rows_ref, bf16[360,1024]{1,0:T(8,128)(2,1)S(1)} %bitcast.29, bf16[360,1024]{1,0:T(8,128)(2,1)S(1)} %collective-permute-done.7.w1_ref, ...), custom_call_target="tpu_custom_call" | custom-call | flops 754974720 | bytes 4194304 | tf_op jit(solution)/shard_map/pallas_call | solution.py:296
  54.6 0.5 collective-permute-start.10
  55.1 1.8 %collective-permute-done.12 = bf16[720,128]{1,0:T(8,128)(2,1)S(1)} collective-permute-done((bf16[720,128]{1,0:T(8,128)(2,1)S(1)}, bf16[720,128]{1,0:T(8,128)(2,1)S(1)}, u32[]{:S(2)}, u32[]{:S(2)}) %collective-permute-start.12) | collective-permute-done | bytes 184352 | tf_op jit(solution)/shard_map/ppermute | solution.py:236
  56.9 0.1 add_convert_fusion
  56.9 1.6 %collective-permute-start.13 = (bf16[720,128]{1,0:T(8,128)(2,1)S(1)}, bf16[720,128]{1,0:T(8,128)(2,1)S(1)}, u32[]{:S(2)}, u32[]{:S(2)}) collective-permute-start(bf16[720,128]{1,0:T(8,128)(2,1)S(1)} %add_convert_fusion), channel_id=1, source_target_pairs={{0,4},{1,5},{2,6},{3,7},{4,0},{5,1},{6,2},{7,3},{8,12},{9,13},{10,... | collective-permute-start | bytes 552968 | tf_op jit(solution)/shard_map/ppermute | solution.py:233
  58.6 2.4 %collective-permute-done.10 = bf16[720,128]{1,0:T(8,128)(2,1)S(1)} collective-permute-done((bf16[720,128]{1,0:T(8,128)(2,1)}, bf16[720,128]{1,0:T(8,128)(2,1)S(1)}, u32[]{:S(2)}, u32[]{:S(2)}) %collective-permute-start.10) | collective-permute-done | bytes 184352 | tf_op jit(solution)/shard_map/ppermute | solution.py:236
  61.0 1.6 %collective-permute-done.13 = bf16[720,128]{1,0:T(8,128)(2,1)S(1)} collective-permute-done((bf16[720,128]{1,0:T(8,128)(2,1)S(1)}, bf16[720,128]{1,0:T(8,128)(2,1)S(1)}, u32[]{:S(2)}, u32[]{:S(2)}) %collective-permute-start.13) | collective-permute-done | bytes 184352 | tf_op jit(solution)/shard_map/ppermute | solution.py:233
  62.5 0.1 fusion.3
  62.6 2.7 %collective-permute-start.14 = (bf16[720,128]{1,0:T(8,128)(2,1)S(1)}, bf16[720,128]{1,0:T(8,128)(2,1)S(1)}, u32[]{:S(2)}, u32[]{:S(2)}) collective-permute-start(bf16[720,128]{1,0:T(8,128)(2,1)S(1)} %fusion.3), channel_id=1, source_target_pairs={{0,16},{8,24},{16,0},{24,8},{1,17},{9,25},{17,1},{25,9},{2,18},{10... | collective-permute-start | bytes 552968 | tf_op jit(solution)/shard_map/ppermute | solution.py:236
  65.3 0.2 shard_map.119
  65.6 0.0 copy-start.10
  65.6 0.8 %reshape.37 = bf16[512,2,128]{2,1,0:T(2,128)(2,1)} reshape(bf16[512,256]{1,0:T(8,128)(2,1)S(1)} %shard_map.119) | data formatting | bytes 524288 | tf_op jit(solution)/shard_map/reshape | solution.py:315
  66.3 5.9 %collective-permute-done.14 = bf16[720,128]{1,0:T(8,128)(2,1)S(1)} collective-permute-done((bf16[720,128]{1,0:T(8,128)(2,1)S(1)}, bf16[720,128]{1,0:T(8,128)(2,1)S(1)}, u32[]{:S(2)}, u32[]{:S(2)}) %collective-permute-start.14) | collective-permute-done | bytes 184352 | tf_op jit(solution)/shard_map/ppermute | solution.py:236
  72.2 0.8 %fusion.4 = bf16[128,720]{0,1:T(8,128)(2,1)} fusion(bf16[720,128]{1,0:T(8,128)(2,1)S(1)} %collective-permute-done.14, bf16[720,128]{1,0:T(8,128)(2,1)S(1)} %collective-permute-done.13, bf16[720,128]{1,0:T(8,128)(2,1)S(1)} %collective-permute-done.10, bf16[720,128]{1,0:T(8,128)(2,1)S(1)} %get-tuple-element.16, f32[720]{0:T(1024)S(1)} %copy-done.10, pred[]{:T(512)S(6)} %eq.10), kind=kLoop, calls=%fused_computation.10 | loop fusion | flops 829440 | bytes 924481 | tf_op jit(solution)/shard_map/transpose | solution.py:315
  (25 shorter events, 0.1 us)
Async XLA Ops:
  0.6 1.1 %copy-start.9 = (bf16[128,2,128]{2,1,0:T(2,128)(2,1)S(1)}, bf16[128,2,128]{2,1,0:T(2,128)(2,1)}, u32[]{:S(2)}) copy-start(bf16[128,2,128]{2,1,0:T(2,128)(2,1)} %param.11) | copy-start | bytes 196612
  0.6 1.1 %copy-start.1 = (s32[512]{0:T(512)S(1)}, s32[512]{0:T(512)}, u32[]{:S(2)}) copy-start(s32[512]{0:T(512)} %param.13) | copy-start | bytes 6148
  0.7 1.1 %copy-start.2 = (s32[128]{0:T(128)S(1)}, s32[128]{0:T(128)}, u32[]{:S(2)}) copy-start(s32[128]{0:T(128)} %param.16) | copy-start | bytes 1540
  0.7 1.1 %copy-start.3 = (s32[128]{0:T(128)S(1)}, s32[128]{0:T(128)}, u32[]{:S(2)}) copy-start(s32[128]{0:T(128)} %param.14) | copy-start | bytes 1540
  0.7 1.1 %copy-start.4 = (s32[128]{0:T(128)S(1)}, s32[128]{0:T(128)}, u32[]{:S(2)}) copy-start(s32[128]{0:T(128)} %refs_2_.5) | copy-start | bytes 1540
  0.7 7.0 %copy-start.8 = (bf16[128,1024]{1,0:T(8,128)(2,1)S(1)}, bf16[128,1024]{1,0:T(8,128)(2,1)}, u32[]{:S(2)}) copy-start(bf16[128,1024]{1,0:T(8,128)(2,1)} %param.10) | copy-start | bytes 786436
  1.7 6.2 %copy-start = (bf16[1024,360]{0,1:T(8,128)(2,1)S(1)}, bf16[1024,360]{0,1:T(8,128)(2,1)}, u32[]{:S(2)}) copy-start(bf16[1024,360]{0,1:T(8,128)(2,1)} %param.18) | copy-start | bytes 2211844
  3.1 4.9 %collective-permute-start.6 = (bf16[1040,128]{1,0:T(8,128)(2,1)S(1)}, bf16[1040,128]{1,0:T(8,128)(2,1)S(1)}, u32[]{:S(2)}, u32[]{:S(2)}) collective-permute-start(bf16[1040,128]{1,0:T(8,128)(2,1)S(1)} %shard_map.113.refs_6_), channel_id=1, source_target_pairs={{0,1},{1,0},{2,3},{3,2},{4,5},{5,4},{6,7},{7,6},{8,9},{9,8},{10,11... | collective-permute-start | bytes 798728 | tf_op jit(solution)/shard_map/ppermute | solution.py:233
  3.6 9.9 %collective-permute-start = (bf16[1040,128]{1,0:T(8,128)(2,1)S(1)}, bf16[1040,128]{1,0:T(8,128)(2,1)S(1)}, u32[]{:S(2)}, u32[]{:S(2)}) collective-permute-start(bf16[1040,128]{1,0:T(8,128)(2,1)S(1)} %shard_map.113.refs_6_), channel_id=1, source_target_pairs={{0,2},{1,3},{2,0},{3,1},{4,6},{5,7},{6,4},{7,5},{8,10},{9,11},{10,... | collective-permute-start | bytes 798728 | tf_op jit(solution)/shard_map/ppermute | solution.py:233
  6.2 9.0 %collective-permute-start.4 = (bf16[1040,128]{1,0:T(8,128)(2,1)S(1)}, bf16[1040,128]{1,0:T(8,128)(2,1)S(1)}, u32[]{:S(2)}, u32[]{:S(2)}) collective-permute-start(bf16[1040,128]{1,0:T(8,128)(2,1)S(1)} %shard_map.113.refs_6_), channel_id=1, source_target_pairs={{0,4},{1,5},{2,6},{3,7},{4,0},{5,1},{6,2},{7,3},{8,12},{9,13},{10,... | collective-permute-start | bytes 798728 | tf_op jit(solution)/shard_map/ppermute | solution.py:233
  8.0 0.7 copy-start.5
  12.1 0.8 %copy-start.6 = (f32[80,2048]{1,0:T(8,128)}, f32[80,2048]{1,0:T(8,128)S(1)}, u32[]{:S(2)}) copy-start(f32[80,2048]{1,0:T(8,128)S(1)} %get-tuple-element.11.refs_10_) | copy-start | bytes 1966084
  12.9 21.2 %collective-permute-start.8 = (bf16[360,1024]{1,0:T(8,128)(2,1)}, bf16[360,1024]{1,0:T(8,128)(2,1)}, u32[]{:S(2)}, u32[]{:S(2)}) collective-permute-start(bf16[360,1024]{1,0:T(8,128)(2,1)} %get-tuple-element.14), channel_id=1, source_target_pairs={{0,2},{1,3},{2,0},{3,1},{4,6},{5,7},{6,4},{7,5},{8,10},{9,11},{10,... | collective-permute-start | bytes 2211848 | tf_op jit(solution)/shard_map/ppermute | solution.py:233
  13.5 8.0 %collective-permute-start.1 = (bf16[1040,128]{1,0:T(8,128)(2,1)S(1)}, bf16[1040,128]{1,0:T(8,128)(2,1)}, u32[]{:S(2)}, u32[]{:S(2)}) collective-permute-start(bf16[1040,128]{1,0:T(8,128)(2,1)S(1)} %collective-permute-done.refs_6_), channel_id=1, source_target_pairs={{0,4},{1,5},{2,6},{3,7},{4,0},{5,1},{6,2},{7,3},{8,12},{9,13},{10,... | collective-permute-start | bytes 798728 | tf_op jit(solution)/shard_map/ppermute | solution.py:233
  15.2 6.9 %collective-permute-start.3 = (bf16[1040,128]{1,0:T(8,128)(2,1)S(1)}, bf16[1040,128]{1,0:T(8,128)(2,1)}, u32[]{:S(2)}, u32[]{:S(2)}) collective-permute-start(bf16[1040,128]{1,0:T(8,128)(2,1)S(1)} %collective-permute-done.refs_6_), channel_id=1, source_target_pairs={{0,1},{1,0},{2,3},{3,2},{4,5},{5,4},{6,7},{7,6},{8,9},{9,8},{10,11... | collective-permute-start | bytes 798728 | tf_op jit(solution)/shard_map/ppermute | solution.py:233
  15.2 6.9 %collective-permute-start.5 = (bf16[1040,128]{1,0:T(8,128)(2,1)S(1)}, bf16[1040,128]{1,0:T(8,128)(2,1)S(1)}, u32[]{:S(2)}, u32[]{:S(2)}) collective-permute-start(bf16[1040,128]{1,0:T(8,128)(2,1)S(1)} %collective-permute-done.4.refs_8_), channel_id=1, source_target_pairs={{0,1},{1,0},{2,3},{3,2},{4,5},{5,4},{6,7},{7,6},{8,9},{9,8},{10,11... | collective-permute-start | bytes 798728 | tf_op jit(solution)/shard_map/ppermute | solution.py:233
  21.5 8.7 %collective-permute-start.2 = (bf16[1040,128]{1,0:T(8,128)(2,1)}, bf16[1040,128]{1,0:T(8,128)(2,1)S(1)}, u32[]{:S(2)}, u32[]{:S(2)}) collective-permute-start(bf16[1040,128]{1,0:T(8,128)(2,1)} %collective-permute-done.1.refs_6_), channel_id=1, source_target_pairs={{0,1},{1,0},{2,3},{3,2},{4,5},{5,4},{6,7},{7,6},{8,9},{9,8},{10,11... | collective-permute-start | bytes 798728 | tf_op jit(solution)/shard_map/ppermute | solution.py:233
  21.5 19.8 %collective-permute-start.7 = (bf16[360,1024]{1,0:T(8,128)(2,1)}, bf16[360,1024]{1,0:T(8,128)(2,1)S(1)}, u32[]{:S(2)}, u32[]{:S(2)}) collective-permute-start(bf16[360,1024]{1,0:T(8,128)(2,1)} %get-tuple-element.14), channel_id=1, source_target_pairs={{0,1},{1,0},{2,3},{3,2},{4,5},{5,4},{6,7},{7,6},{8,9},{9,8},{10,11... | collective-permute-start | bytes 2211848 | tf_op jit(solution)/shard_map/ppermute | solution.py:233
  22.1 1.1 %copy-start.7 = (f32[80,2048]{1,0:T(8,128)S(1)}, f32[80,2048]{1,0:T(8,128)}, u32[]{:S(2)}) copy-start(f32[80,2048]{1,0:T(8,128)} %copy-done.6) | copy-start | bytes 1966084
  35.9 12.6 %collective-permute-start.9 = (bf16[360,1024]{1,0:T(8,128)(2,1)S(1)}, bf16[360,1024]{1,0:T(8,128)(2,1)S(1)}, u32[]{:S(2)}, u32[]{:S(2)}) collective-permute-start(bf16[360,1024]{1,0:T(8,128)(2,1)S(1)} %broadcast_add_fusion.w2_ref), channel_id=1, source_target_pairs={{0,1},{1,0},{2,3},{3,2},{4,5},{5,4},{6,7},{7,6},{8,9},{9,8},{10,11... | collective-permute-start | bytes 2211848 | tf_op jit(solution)/shard_map/ppermute | solution.py:233
  36.0 12.5 %collective-permute-start.11 = (bf16[1024,128]{1,0:T(8,128)(2,1)}, bf16[1024,128]{1,0:T(8,128)(2,1)}, u32[]{:S(2)}, u32[]{:S(2)}) collective-permute-start(bf16[1024,128]{1,0:T(8,128)(2,1)} %get-tuple-element.13.rows_ref), channel_id=1, source_target_pairs={{0,4},{1,5},{2,6},{3,7},{4,0},{5,1},{6,2},{7,3},{8,12},{9,13},{10,... | collective-permute-start | bytes 786440 | tf_op jit(solution)/shard_map/ppermute | solution.py:233
  50.4 6.5 %collective-permute-start.12 = (bf16[720,128]{1,0:T(8,128)(2,1)S(1)}, bf16[720,128]{1,0:T(8,128)(2,1)S(1)}, u32[]{:S(2)}, u32[]{:S(2)}) collective-permute-start(bf16[720,128]{1,0:T(8,128)(2,1)S(1)} %get-tuple-element.19), channel_id=1, source_target_pairs={{0,8},{8,0},{16,24},{24,16},{1,9},{9,1},{17,25},{25,17},{2,10},{10... | collective-permute-start | bytes 552968 | tf_op jit(solution)/shard_map/ppermute | solution.py:236
  54.6 6.3 %collective-permute-start.10 = (bf16[720,128]{1,0:T(8,128)(2,1)}, bf16[720,128]{1,0:T(8,128)(2,1)S(1)}, u32[]{:S(2)}, u32[]{:S(2)}) collective-permute-start(bf16[720,128]{1,0:T(8,128)(2,1)} %get-tuple-element.17), channel_id=1, source_target_pairs={{0,8},{8,0},{16,24},{24,16},{1,9},{9,1},{17,25},{25,17},{2,10},{10... | collective-permute-start | bytes 552968 | tf_op jit(solution)/shard_map/ppermute | solution.py:236
  56.9 5.6 %collective-permute-start.13 = (bf16[720,128]{1,0:T(8,128)(2,1)S(1)}, bf16[720,128]{1,0:T(8,128)(2,1)S(1)}, u32[]{:S(2)}, u32[]{:S(2)}) collective-permute-start(bf16[720,128]{1,0:T(8,128)(2,1)S(1)} %add_convert_fusion), channel_id=1, source_target_pairs={{0,4},{1,5},{2,6},{3,7},{4,0},{5,1},{6,2},{7,3},{8,12},{9,13},{10,... | collective-permute-start | bytes 552968 | tf_op jit(solution)/shard_map/ppermute | solution.py:233
  62.6 9.6 %collective-permute-start.14 = (bf16[720,128]{1,0:T(8,128)(2,1)S(1)}, bf16[720,128]{1,0:T(8,128)(2,1)S(1)}, u32[]{:S(2)}, u32[]{:S(2)}) collective-permute-start(bf16[720,128]{1,0:T(8,128)(2,1)S(1)} %fusion.3), channel_id=1, source_target_pairs={{0,16},{8,24},{16,0},{24,8},{1,17},{9,25},{17,1},{25,9},{2,18},{10... | collective-permute-start | bytes 552968 | tf_op jit(solution)/shard_map/ppermute | solution.py:236
  65.6 6.6 %copy-start.10 = (f32[720]{0:T(1024)S(1)}, f32[720]{0:T(1024)}, u32[]{:S(2)}) copy-start(f32[720]{0:T(1024)} %param.19) | copy-start | bytes 8644

commit v3 on v2

--- a/solution.py
+++ b/solution.py
@@ -70,9 +70,7 @@
     lane = lane - (turn // 64) * 128
     turn = turn % 64
     rows_ref[:slots, :] = dot_nt(rows, (lane == turn).astype(BF16)).astype(BF16)
-    vals = dot_nt((lane == turn + 64).astype(BF16), rows).astype(BF16)
-    for c in range(slots // 128):
-        rows_ref[slots + c * 128 : slots + (c + 1) * 128, :] = vals[:, c * 128 : (c + 1) * 128]
+    rows_ref[slots : 2 * slots, :] = dot_nt(rows, (lane == turn + 64).astype(BF16)).astype(BF16)
     sub = iota((8, slots), 0)
     labels = jnp.where(sub == 0, seg, jnp.where(sub == 1, order, 0.0)).astype(BF16)
     labels = dot_nt(labels, perm)
@@ -84,13 +82,14 @@
 def attend_kernel(first, last, count, *refs):
     off_ref, sink_ref, seg_ref, q_ref, tseg_ref, pad_ref = refs[:6]
     rows_refs = refs[6 : 6 + count]
-    given_ref, out_ref, extra_ref, q_scr, key_scr, val_scr, bias_scr, acc_scr, moved = refs[6 + count :]
+    given_ref, out_ref, extra_ref, *sent_ref = refs[6 + count :][: 4 if first else 3]
+    q_scr, key_scr, val_scr, label_scr, row_scr, acc_scr, moved = refs[6 + count :][4 if first else 3 :]
     if first:
-        load = pltpu.make_async_copy(given_ref, extra_ref, moved.at[0])
+        load = pltpu.make_async_copy(given_ref, sent_ref[0], moved.at[0])
     else:
         load = pltpu.make_async_copy(given_ref, acc_scr, moved.at[0])
-        extra_ref[...] = jnp.zeros_like(extra_ref)
     load.start()
+    extra_ref[...] = jnp.zeros_like(extra_ref)
     tokens = q_ref.shape[1]
     heads = q_ref.shape[0] // 64
     slots = (rows_refs[0].shape[0] - 16) // 2
@@ -102,42 +101,46 @@
         pair = [q, zero] if h < heads // 2 else [zero, q]
         q_scr[:, h * tokens : (h + 1) * tokens] = jnp.concatenate(pair, axis=0)
     tseg = tseg_ref[...].astype(F32)
-    tok = iota((128, tokens), 1).astype(F32)
+    tok = iota((1, tokens), 1).astype(F32)
     low, high = seg_ref[0].astype(F32), seg_ref[tokens - 1].astype(F32)
-
     eye = (iota((128, 128), 0) == iota((128, 128), 1)).astype(BF16)
-    row = iota((16, 128), 0)
-    labels, flags = [], jnp.zeros((16, 1), F32)
+    stretches = []
     for b in range(count):
-        meta = rows_refs[b][2 * slots :, :]
-        labels.append(dot_nt(eye, meta))
-        meta = meta.astype(F32)
-        hit = jnp.where((meta >= low) & (meta <= high) & (row < tiles), 1.0, 0.0)
-        place = jnp.left_shift(1, iota((16, 1), 0) + b * tiles).astype(F32)
-        flags = flags + jnp.max(hit, axis=1, keepdims=True) * place
-    flags = jnp.sum(flags).astype(jnp.int32)
+        meta = rows_refs[b][2 * slots :, :].astype(F32)
+        real = (iota((16, 128), 0) < tiles) & (meta >= 0.0)
+        counts = jnp.where(real & (meta < low), 1.0, 0.0) + jnp.where(real & (meta <= high), 1024.0, 0.0)
+        counts = jnp.sum(jnp.sum(counts, axis=0, keepdims=True), axis=1, keepdims=True).astype(jnp.int32)
+        begin, end = (counts & 1023) >> 4, (counts >> 10) + 31 >> 4
+        stretches.append(begin + (end << 6))
+        for c in range(tiles):
+            order = meta[tiles + c : tiles + c + 1, :]
+            order = jnp.where(order < 0.0, -1.0, jnp.clip(order + off_ref[b].astype(F32), -1.0, tokens))
+            label = jnp.concatenate([meta[c : c + 1, :], order, jnp.zeros((14, 128), F32)], axis=0)
+            label_scr[b, c * 128 : (c + 1) * 128, :16] = dot_nt(eye, label.astype(BF16))
+        label_scr[b, slots:, :16] = jnp.full((32, 16), -1.0, F32)
+    packed = [stretches[b] + (stretches[b + 1] << 12) for b in range(0, count, 2)]
+    packed = [jnp.sum(p) for p in packed]
 
     used = jnp.int32(0)
     for b in range(count):
-        for c in range(tiles):
-            wanted = ((flags >> (b * tiles + c)) & 1) == 1
-
-            @pl.when(wanted)
-            def _(b=b, c=c, used=used):
-                seg, order = labels[b][:, c : c + 1], labels[b][:, tiles + c : tiles + c + 1]
-                seen = (seg == tseg) & ((order < 0.0) | (order + off_ref[b].astype(F32) <= tok))
-                at = pl.multiple_of(used * 128, 128)
-                bias_scr[pl.ds(at, 128), :] = jnp.where(seen, 0.0, HIDE)
-                key_scr[pl.ds(at, 128), :] = rows_refs[b][c * 128 : (c + 1) * 128, :]
-                val_scr[:, pl.ds(at, 128)] = rows_refs[b][slots + c * 128 : slots + (c + 1) * 128, :]
-
-            used = used + wanted.astype(jnp.int32)
-    for extra in range(1):
-        at = pl.multiple_of(used * 128, 128)
-        bias_scr[pl.ds(at, 128), :] = jnp.full((128, tokens), HIDE, F32)
-        key_scr[pl.ds(at, 128), :] = jnp.zeros((128, 128), BF16)
-        val_scr[:, pl.ds(at, 128)] = jnp.zeros((128, 128), BF16)
-
+        stretch = packed[b // 2] >> (12 * (b % 2))
+        begin = stretch & 63
+        steps = jnp.maximum(((stretch >> 6) & 63) - begin, 0) >> 1
+
+        def move(i, carry, b=b, begin=begin, used=used):
+            at = pl.multiple_of(begin * 16 + i * 32, 16)
+            to = pl.multiple_of(used + i * 32, 32)
+            key_scr[pl.ds(to, 32), :] = rows_refs[b][pl.ds(at, 32), :]
+            val_scr[pl.ds(to, 32), :] = rows_refs[b][pl.ds(pl.multiple_of(slots + at, 16), 32), :]
+            row_scr[pl.ds(to, 32), :] = label_scr[b, pl.ds(at, 32), :]
+            return carry
+
+        lax.fori_loop(0, steps, move, 0)
+        used = used + steps * 32
+    rest = pl.ds(pl.multiple_of(used, 32), 256)
+    key_scr[rest, :] = jnp.zeros((256, 128), BF16)
+    val_scr[rest, :] = jnp.zeros((256, 128), BF16)
+    row_scr[rest, :] = jnp.full((256, 128), -1.0, F32)
     if first:
         for h in range(heads):
             span = slice(h * tokens, (h + 1) * tokens)
@@ -151,7 +154,10 @@
     def pair(index, carry):
         at = pl.multiple_of(index * 256, 256)
         keys = key_scr[pl.ds(at, 256), :]
-        bias = jnp.concatenate([bias_scr[pl.ds(at, 256), :]] * (heads // 2), axis=1)
+        rows = row_scr[pl.ds(at, 256), :]
+        seen = (rows[:, :1] == tseg) & (rows[:, 1:2] <= tok)
+        bias = jnp.concatenate([jnp.where(seen, 0.0, HIDE)] * (heads // 2), axis=1)
+        turned = dot_nt(eye, val_scr[pl.ds(at, 256), :]).astype(BF16)
         ones = jnp.ones((16, 256), BF16)
         spans = [slice(group * half, (group + 1) * half) for group in range(2)]
         scores = [jnp.dot(keys, q_scr[:, span], preferred_element_type=F32) + bias for span in spans]
@@ -159,13 +165,13 @@
         tops = [jnp.maximum(jnp.max(s, axis=0, keepdims=True), p) for s, p in zip(scores, peaks)]
         weights = [jnp.exp(s - t).astype(BF16) for s, t in zip(scores, tops)]
         for group, span in enumerate(spans):
-            vals = jnp.concatenate([val_scr[group * 64 : (group + 1) * 64, pl.ds(at, 256)], ones], axis=0)
+            vals = jnp.concatenate([turned[group * 64 : (group + 1) * 64, :], ones], axis=0)
             new = jnp.dot(vals, weights[group], preferred_element_type=F32)[:72, :]
             acc_scr[:72, span] = acc_scr[:72, span] * jnp.exp(peaks[group] - tops[group]) + new
             acc_scr[72:80, span] = jnp.broadcast_to(tops[group], (8, half))
         return carry
 
-    lax.fori_loop(0, (used + 1) // 2, pair, 0)
+    lax.fori_loop(0, (used + 255) // 256, pair, 0)
     if not last:
         save = pltpu.make_async_copy(acc_scr, out_ref, moved.at[1])
         save.start()
@@ -184,41 +190,47 @@
     width, tokens = q.shape
     heads = width // 64
     slots = (rows[0].shape[0] - 16) // 2
-    out = jax.ShapeDtypeStruct((width, tokens), BF16) if last else jax.ShapeDtypeStruct((80, heads * tokens), F32)
+    if last:
+        out = (jax.ShapeDtypeStruct((width, tokens), BF16), jax.ShapeDtypeStruct((1, width), BF16))
+    else:
+        out = (jax.ShapeDtypeStruct((80, heads * tokens), F32), jax.ShapeDtypeStruct((1, 128), BF16))
+    if first:
+        out += (jax.ShapeDtypeStruct(given.shape, given.dtype),)
     args = [off, sink, seg, q, tseg, pad, *rows, given]
-    extra = jax.ShapeDtypeStruct(given.shape, given.dtype) if first else jax.ShapeDtypeStruct((8, 128), F32)
     return pl.pallas_call(
         functools.partial(attend_kernel, first, last, count),
-        out_shape=(out, extra),
+        out_shape=out,
         in_specs=[SMEM] * 3 + [VMEM] * (3 + count) + [HBM],
-        out_specs=(VMEM if last else HBM, HBM if first else VMEM),
+        out_specs=(VMEM if last else HBM, VMEM) + ((HBM,) if first else ()),
         scratch_shapes=[
             pltpu.VMEM((128, heads * tokens), BF16),
             pltpu.VMEM((count * slots + 256, 128), BF16),
-            pltpu.VMEM((128, count * slots + 256), BF16),
-            pltpu.VMEM((count * slots + 256, tokens), F32),
+            pltpu.VMEM((count * slots + 256, 128), BF16),
+            pltpu.VMEM((count, slots + 32, 128), F32),
+            pltpu.VMEM((count * slots + 256, 128), F32),
             pltpu.VMEM((80, heads * tokens), F32),
             pltpu.SemaphoreType.DMA((2,)),
         ],
         compiler_params=pltpu.CompilerParams(vmem_limit_bytes=16 * 2**20),
         cost_estimate=pl.CostEstimate(
-            flops=4 * heads * tokens * slots * count * 128,
-            bytes_accessed=3 * 2**20,
-            transcendentals=heads * tokens * slots * count,
+            flops=1 * heads * tokens * slots * count * 128,
+            bytes_accessed=10**6,
+            transcendentals=0,
         ),
     )(*args)
 
 
-def project_kernel(pos_ref, rows_ref, w0_ref, w1_ref, w2_ref, w3_ref, a_ref, b_ref):
+def project_kernel(pos_ref, rows_ref, w0_ref, w1_ref, w2_ref, *refs):
     core, swap = pos_ref[0], pos_ref[1]
+    *w3_refs, a_ref, b_ref = refs
     rows = rows_ref[...]
 
     def block(one, two):
-        a = jnp.dot(one[...], rows, preferred_element_type=F32)
-        b = jnp.dot(two[...], rows, preferred_element_type=F32)
-        return jnp.where(core == 0, jnp.concatenate([a, b], axis=0), jnp.concatenate([b, a], axis=0)).astype(BF16)
-
-    here, there = block(w0_ref, w1_ref), block(w2_ref, w3_ref)
+        a = [jnp.dot(one[...], rows, preferred_element_type=F32)]
+        b = [jnp.dot(w[...], rows, preferred_element_type=F32) for w in two]
+        return jnp.where(core == 0, jnp.concatenate(a + b, axis=0), jnp.concatenate(b + a, axis=0)).astype(BF16)
+
+    here, there = block(w0_ref, [w1_ref]), block(w2_ref, w3_refs)
     a_ref[...] = jnp.where(swap == 0, here, there)
     b_ref[...] = jnp.where(swap == 0, there, here)
 
@@ -270,32 +282,34 @@
 
     turned = queries.T
     step = functools.partial(attend, sink=sink_logits, q=turned, seg=token_seg, tseg=tseg, pad=pad)
-    state, sent = step(True, False, offsets(0), rows=near, given=w0)
+    state, zeros, sent = step(True, False, offsets(0), rows=near, given=w0)
+    rows_x = rows_x + zeros
     rows_d = gy(rows_x, 4)
     w2 = gy(sent, 2)
     along = [rows_x, gy(rows_x, 1), rows_y, gy(rows_y, 1)]
     both = jnp.concatenate([offsets(2), offsets(4)])
-    state, done = step(False, False, both, rows=along, given=state)
+    state, zeros = step(False, False, both, rows=along, given=state)
     w1 = gy(sent, 1)
+    rows_d = rows_d + zeros
     diagonal = [rows_d, gy(rows_d, 1)]
-    attention, done = step(False, True, offsets(6), rows=diagonal, given=state)
+    attention, zeros = step(False, True, offsets(6), rows=diagonal, given=state)
     other = gy(attention, 4)
-    w2 = w2 + done[0, 0].astype(BF16)
-    w3 = gy(w2, 1)
+    third = w2.shape[0] // 3
+    w3 = [gy(w2[i * third : (i + 1) * third] + zeros, 1) for i in range(3)]
 
     part = jax.ShapeDtypeStruct((out_weight.shape[1] * 2, tokens), BF16)
     pos = jnp.stack([core, jnp.where(x == 1 - plane % 2, 0, 1)]).astype(jnp.int32)
     project = pl.pallas_call(
         project_kernel,
         out_shape=(part, part),
-        in_specs=[SMEM] + [VMEM] * 5,
+        in_specs=[SMEM] + [VMEM] * 7,
         out_specs=(VMEM, VMEM),
         compiler_params=pltpu.CompilerParams(vmem_limit_bytes=16 * 2**20),
         cost_estimate=pl.CostEstimate(flops=2 * 1024 * 1440 * 256, bytes_accessed=4 * 2**20, transcendentals=0),
     )
-    keep_a, keep_b = project(pos, attention, w0, w1, w2, w3)
+    keep_a, keep_b = project(pos, attention, w0, w1, w2, *w3)
     got_k = gx(keep_a, 1)
-    send_a, send_b = project(pos, other, w0, w1, w2, w3)
+    send_a, send_b = project(pos, other, w0, w1, w2, *w3)
     got_s = gx(send_a, 1)
     got = gy((send_b.astype(F32) + got_s.astype(F32)).astype(BF16), 4)
     cache = pl.pallas_call(

time: 73.1 us -> 63.3 us (0.87)
  starting transfers between devices: 19.6 us -> 14.2 us
  Pallas kernels: 19.9 us -> 17.7 us
  waiting for transfers between devices: 24.5 us -> 22.6 us
    ppermute x12 -> x14, starting transfers between devices: 14.9 us -> 9.44 us  [gy(): return lax.ppermute(value, 'gy', [(i, i ^ m) for i in range(8)])]
    pallas_call x3, Pallas kernels: 13.9 us -> 11.7 us  [attend(): pl.pallas_call(functools.partial(attend_kernel, first, last, count), out_...]
    ppermute x12 -> x14, waiting for transfers between devices: 14.4 us -> 12.7 us  [gy(): return lax.ppermute(value, 'gy', [(i, i ^ m) for i in range(8)])]
    add x1 -> x3, other arithmetic: 1.81 us -> 1.88 us  [the longest x1 0.97 us: tuned(): rows_d = rows_d + zeros]
  transfers between devices with their start and end apart: 15 -> 17, of which waited for: 6 -> 10; matrix products, arithmetic and copies ran while one was open for 5% -> 5% of each run, Pallas kernels for 23% -> 23%
where the time goes in v3:
time: 63.3 us; the launch traced here: 63.2 us
  waiting for transfers between devices  22.6 us (36%)
  Pallas kernels  17.7 us (28%)
  starting transfers between devices  14.2 us (22%)
  local copies, waits for them, and re-layouts  4.62 us (7%)
  other arithmetic  3.18 us (5%)
  between operations  0.87 us (1%)
    ppermute x14, waiting for transfers between devices, gy(): return lax.ppermute(value, 'gy', [(i, i ^ m) for i in range(8)])  12.7 us
    pallas_call x3, Pallas kernels, attend(): pl.pallas_call(functools.partial(attend_kernel, first, last, count), out_...  11.7 us
    ppermute x3, waiting for transfers between devices, gx(): return lax.ppermute(value, 'gx', [(i, i ^ m) for i in range(4)])  9.93 us
    ppermute x14, starting transfers between devices, gy(): return lax.ppermute(value, 'gy', [(i, i ^ m) for i in range(8)])  9.44 us
    ppermute x3, starting transfers between devices, gx(): return lax.ppermute(value, 'gx', [(i, i ^ m) for i in range(4)])  4.73 us
    unnamed x25, local copies, waits for them, and re-layouts  3.86 us
    pallas_call x1, Pallas kernels, tuned(): keep_a, keep_b = project(pos, attention, w0, w1, w2, *w3)  2.6 us
    pallas_call x1, Pallas kernels, tuned(): send_a, send_b = project(pos, other, w0, w1, w2, *w3)  1.93 us
  transfers between devices with their start and end apart: 17, of which 10 were waited for; matrix products, arithmetic and copies ran while one was open for 5% of the time, Pallas kernels for 23%

profile of v3, /device:TPU:0, one launch (start us, length us, event | category | flops | bytes accessed | tf_op | source)
XLA Modules:
  0.0 63.2 jit_solution(17575826822934458733)
XLA Ops:
  0.7 1.0 %copy.17 = bf16[64,8,2,128]{3,1,2,0:T(8,128)(2,1)S(1)} copy(bf16[64,8,2,128]{3,2,1,0:T(2,128)(2,1)} %bitcast.52) | data formatting | bytes 524288
  1.7 0.0 copy-start
  1.8 1.3 %shard_map.113.refs_6_ = bf16[1040,128]{1,0:T(8,128)(2,1)S(1)} custom-call(s32[1]{0:T(128)} %bitcast.7.base_ref, bf16[512,256]{1,0:T(8,128)(2,1)S(1)} %bitcast.31, bf16[128,256]{1,0:T(8,128)(2,1)S(1)} %bitcast.36, s32[1,128]{1,0:T(1,128)S(1)} %bitcast.48, s32[1,128]{1,0:T(1,128)S(1)} %bitcast.42, s32[1,512]{1,0:T(1,128)S(1)} %bitcast.47, s32[1,128]{1,0:T(1,128)S(1)} %bitcast.38), custom_call_target="tpu_custom_call" | custom-call | tf_op jit(solution)/shard_map/pallas_call | solution.py:258
  3.1 0.5 collective-permute-start.1
  3.6 2.6 %collective-permute-start = (bf16[1040,128]{1,0:T(8,128)(2,1)S(1)}, bf16[1040,128]{1,0:T(8,128)(2,1)S(1)}, u32[]{:S(2)}, u32[]{:S(2)}) collective-permute-start(bf16[1040,128]{1,0:T(8,128)(2,1)S(1)} %shard_map.113.refs_6_), channel_id=1, source_target_pairs={{0,2},{1,3},{2,0},{3,1},{4,6},{5,7},{6,4},{7,5},{8,10},{9,11},{10,... | collective-permute-start | bytes 798728 | tf_op jit(solution)/shard_map/ppermute | solution.py:245
  6.2 1.5 %collective-permute-start.4 = (bf16[1040,128]{1,0:T(8,128)(2,1)S(1)}, bf16[1040,128]{1,0:T(8,128)(2,1)S(1)}, u32[]{:S(2)}, u32[]{:S(2)}) collective-permute-start(bf16[1040,128]{1,0:T(8,128)(2,1)S(1)} %shard_map.113.refs_6_), channel_id=1, source_target_pairs={{0,4},{1,5},{2,6},{3,7},{4,0},{5,1},{6,2},{7,3},{8,12},{9,13},{10,... | collective-permute-start | bytes 798728 | tf_op jit(solution)/shard_map/ppermute | solution.py:245
  7.7 0.2 copy.12
  7.9 0.1 pad_add_fusion.2.refs_0_
  7.9 0.7 %copy-done.6 = f32[16]{0:T(128)S(1)} copy-done((f32[16]{0:T(128)S(1)}, f32[16]{0:T(128)}, u32[]{:S(2)}) %copy-start.6) | copy-done | bytes 88
  8.6 3.1 %shard_map.114 = (f32[80,2048]{1,0:T(8,128)S(1)}, bf16[1,128]{1,0:T(2,128)(2,1)S(1)}, bf16[360,1024]{1,0:T(8,128)(2,1)}) custom-call(s32[2]{0:T(128)S(1)} %pad_add_fusion.2.refs_0_, f32[16]{0:T(128)S(1)} %copy-done.6, s32[128]{0:T(128)S(1)} %copy-done.3, bf16[1024,128]{1,0:T(8,128)(2,1)S(1)} %bitcast.33, s32[1,128]{1,0:T(1,128)S(1)} %bitcast.39, ...), custom_call_target="tpu_custom_call" | custom-call | flops 268435456 | bytes 1000000 | tf_op jit(solution)/shard_map/pallas_call | solution.py:200
  11.7 1.4 %collective-permute-done = bf16[1040,128]{1,0:T(8,128)(2,1)S(1)} collective-permute-done((bf16[1040,128]{1,0:T(8,128)(2,1)S(1)}, bf16[1040,128]{1,0:T(8,128)(2,1)S(1)}, u32[]{:S(2)}, u32[]{:S(2)}) %collective-permute-start) | collective-permute-done | bytes 266272 | tf_op jit(solution)/shard_map/ppermute | solution.py:245
  13.2 0.1 collective-permute-start.3
  13.3 1.4 %collective-permute-done.4.refs_8_ = bf16[1040,128]{1,0:T(8,128)(2,1)S(1)} collective-permute-done((bf16[1040,128]{1,0:T(8,128)(2,1)S(1)}, bf16[1040,128]{1,0:T(8,128)(2,1)S(1)}, u32[]{:S(2)}, u32[]{:S(2)}) %collective-permute-start.4) | collective-permute-done | bytes 266272 | tf_op jit(solution)/shard_map/ppermute | solution.py:245
  14.6 1.5 %collective-permute-start.2 = (bf16[1040,128]{1,0:T(8,128)(2,1)S(1)}, bf16[1040,128]{1,0:T(8,128)(2,1)}, u32[]{:S(2)}, u32[]{:S(2)}) collective-permute-start(bf16[1040,128]{1,0:T(8,128)(2,1)S(1)} %broadcast_add_fusion.1.refs_6_), channel_id=1, source_target_pairs={{0,4},{1,5},{2,6},{3,7},{4,0},{5,1},{6,2},{7,3},{8,12},{9,13},{10,... | collective-permute-start | bytes 798728 | tf_op jit(solution)/shard_map/ppermute | solution.py:245
  16.2 0.1 pad_add_fusion.3.refs_0_
  16.2 0.9 %collective-permute-start.8 = (bf16[360,1024]{1,0:T(8,128)(2,1)}, bf16[360,1024]{1,0:T(8,128)(2,1)S(1)}, u32[]{:S(2)}, u32[]{:S(2)}) collective-permute-start(bf16[360,1024]{1,0:T(8,128)(2,1)} %get-tuple-element.18), channel_id=1, source_target_pairs={{0,2},{1,3},{2,0},{3,1},{4,6},{5,7},{6,4},{7,5},{8,10},{9,11},{10,... | collective-permute-start | bytes 2211848 | tf_op jit(solution)/shard_map/ppermute | solution.py:245
  17.1 4.8 %shard_map.115 = (f32[80,2048]{1,0:T(8,128)S(1)}, bf16[1,128]{1,0:T(2,128)(2,1)S(1)}) custom-call(s32[4]{0:T(128)S(1)} %pad_add_fusion.3.refs_0_, f32[16]{0:T(128)S(1)} %copy-done.6, s32[128]{0:T(128)S(1)} %copy-done.3, bf16[1024,128]{1,0:T(8,128)(2,1)S(1)} %bitcast.34, s32[1,128]{1,0:T(1,128)S(1)} %bitcast.40, s32[1,128]{1,0:T(1,128)S(1)} %bitcast.44, ...), custom_call_target="tpu_custom_call" | custom-call | flops 536870912 | bytes 1000000 | tf_op jit(solution)/shard_map/pallas_call | solution.py:200
  21.9 0.9 %copy-done.1 = f32[80,2048]{1,0:T(8,128)} copy-done((f32[80,2048]{1,0:T(8,128)}, f32[80,2048]{1,0:T(8,128)S(1)}, u32[]{:S(2)}) %copy-start.1) | copy-done | bytes 655384
  22.8 0.7 %collective-permute-done.2 = bf16[1040,128]{1,0:T(8,128)(2,1)} collective-permute-done((bf16[1040,128]{1,0:T(8,128)(2,1)S(1)}, bf16[1040,128]{1,0:T(8,128)(2,1)}, u32[]{:S(2)}, u32[]{:S(2)}) %collective-permute-start.2) | collective-permute-done | bytes 266272 | tf_op jit(solution)/shard_map/ppermute | solution.py:245
  23.5 1.0 %broadcast_add_fusion.refs_6_ = bf16[1040,128]{1,0:T(8,128)(2,1)S(1)} fusion(bf16[1040,128]{1,0:T(8,128)(2,1)} %collective-permute-done.2, bf16[128]{0:T(256)(128)(2,1)S(1)} %bitcast.50), kind=kLoop, calls=%fused_computation.13 | loop fusion | flops 133120 | bytes 532736 | tf_op jit(solution)/shard_map/add | solution.py:293
  24.5 0.1 collective-permute-start.6
  24.6 0.5 collective-permute-start.7
  25.1 0.1 pad_add_fusion.1.refs_0_
  25.2 1.0 %collective-permute-done.6.refs_7_ = bf16[1040,128]{1,0:T(8,128)(2,1)S(1)} collective-permute-done((bf16[1040,128]{1,0:T(8,128)(2,1)S(1)}, bf16[1040,128]{1,0:T(8,128)(2,1)S(1)}, u32[]{:S(2)}, u32[]{:S(2)}) %collective-permute-start.6) | collective-permute-done | bytes 266272 | tf_op jit(solution)/shard_map/ppermute | solution.py:245
  26.1 1.1 %copy-done.2 = f32[80,2048]{1,0:T(8,128)S(1)} copy-done((f32[80,2048]{1,0:T(8,128)S(1)}, f32[80,2048]{1,0:T(8,128)}, u32[]{:S(2)}) %copy-start.2) | copy-done | bytes 655384
  27.2 3.8 %shard_map.116 = (bf16[1024,128]{1,0:T(8,128)(2,1)}, bf16[1,1024]{1,0:T(2,128)(2,1)S(1)}) custom-call(s32[2]{0:T(128)S(1)} %pad_add_fusion.1.refs_0_, f32[16]{0:T(128)S(1)} %copy-done.6, s32[128]{0:T(128)S(1)} %copy-done.3, bf16[1024,128]{1,0:T(8,128)(2,1)S(1)} %bitcast.35, s32[1,128]{1,0:T(1,128)S(1)} %bitcast.41, s32[1,128]{1,0:T(1,128)S(1)} %bitcast.45, ...), custom_call_target="tpu_custom_call" | custom-call | flops 268435456 | bytes 1000000 | tf_op jit(solution)/shard_map/pallas_call | solution.py:200
  31.0 0.6 %collective-permute-start.13 = (bf16[1024,128]{1,0:T(8,128)(2,1)}, bf16[1024,128]{1,0:T(8,128)(2,1)}, u32[]{:S(2)}, u32[]{:S(2)}) collective-permute-start(bf16[1024,128]{1,0:T(8,128)(2,1)} %get-tuple-element.17.rows_ref), channel_id=1, source_target_pairs={{0,4},{1,5},{2,6},{3,7},{4,0},{5,1},{6,2},{7,3},{8,12},{9,13},{10,... | collective-permute-start | bytes 786440 | tf_op jit(solution)/shard_map/ppermute | solution.py:245
  31.7 3.4 %collective-permute-done.8.w2_ref = bf16[360,1024]{1,0:T(8,128)(2,1)S(1)} collective-permute-done((bf16[360,1024]{1,0:T(8,128)(2,1)}, bf16[360,1024]{1,0:T(8,128)(2,1)S(1)}, u32[]{:S(2)}, u32[]{:S(2)}) %collective-permute-start.8) | collective-permute-done | bytes 737312 | tf_op jit(solution)/shard_map/ppermute | solution.py:245
  35.1 0.9 %slice_add_fusion = (bf16[120,1024]{1,0:T(8,128)(2,1)}, bf16[120,1024]{1,0:T(8,128)(2,1)}, bf16[120,1024]{1,0:T(8,128)(2,1)}) fusion(bf16[360,1024]{1,0:T(8,128)(2,1)S(1)} %collective-permute-done.8.w2_ref, bf16[1024]{0:T(1024)(128)(2,1)S(1)} %reduce), kind=kLoop, calls=%fused_computation.9 | loop fusion | flops 368640 | bytes 1476608 | tf_op jit(solution)/shard_map/add | solution.py:298
  36.0 0.5 collective-permute-start.11
  36.5 0.1 pad_add_fusion.pos_ref
  36.5 3.2 %collective-permute-done.13.rows_ref = bf16[1024,128]{1,0:T(8,128)(2,1)} collective-permute-done((bf16[1024,128]{1,0:T(8,128)(2,1)}, bf16[1024,128]{1,0:T(8,128)(2,1)}, u32[]{:S(2)}, u32[]{:S(2)}) %collective-permute-start.13) | collective-permute-done | bytes 262176 | tf_op jit(solution)/shard_map/ppermute | solution.py:245
  39.8 1.9 %shard_map.118 = (bf16[720,128]{1,0:T(8,128)(2,1)S(1)}, bf16[720,128]{1,0:T(8,128)(2,1)S(1)}) custom-call(s32[2]{0:T(128)S(1)} %pad_add_fusion.pos_ref, bf16[1024,128]{1,0:T(8,128)(2,1)} %collective-permute-done.13.rows_ref, bf16[360,1024]{1,0:T(8,128)(2,1)S(1)} %bitcast.29, bf16[360,1024]{1,0:T(8,128)(2,1)S(1)} %collective-permute-done.7.w1_ref, ...), custom_call_target="tpu_custom_call" | custom-call | flops 754974720 | bytes 4194304 | tf_op jit(solution)/shard_map/pallas_call | solution.py:312
  41.7 1.6 %collective-permute-start.14 = (bf16[720,128]{1,0:T(8,128)(2,1)S(1)}, bf16[720,128]{1,0:T(8,128)(2,1)S(1)}, u32[]{:S(2)}, u32[]{:S(2)}) collective-permute-start(bf16[720,128]{1,0:T(8,128)(2,1)S(1)} %get-tuple-element.23), channel_id=1, source_target_pairs={{0,8},{8,0},{16,24},{24,16},{1,9},{9,1},{17,25},{25,17},{2,10},{10... | collective-permute-start | bytes 552968 | tf_op jit(solution)/shard_map/ppermute | solution.py:248
  43.3 2.6 %shard_map.117 = (bf16[720,128]{1,0:T(8,128)(2,1)}, bf16[720,128]{1,0:T(8,128)(2,1)S(1)}) custom-call(s32[2]{0:T(128)S(1)} %pad_add_fusion.pos_ref, bf16[1024,128]{1,0:T(8,128)(2,1)} %get-tuple-element.17.rows_ref, bf16[360,1024]{1,0:T(8,128)(2,1)S(1)} %bitcast.30, bf16[360,1024]{1,0:T(8,128)(2,1)S(1)} %collective-permute-done.7.w1_ref, ...), custom_call_target="tpu_custom_call" | custom-call | flops 754974720 | bytes 4194304 | tf_op jit(solution)/shard_map/pallas_call | solution.py:310
  45.9 0.5 collective-permute-start.12
  46.4 1.2 %collective-permute-done.14 = bf16[720,128]{1,0:T(8,128)(2,1)S(1)} collective-permute-done((bf16[720,128]{1,0:T(8,128)(2,1)S(1)}, bf16[720,128]{1,0:T(8,128)(2,1)S(1)}, u32[]{:S(2)}, u32[]{:S(2)}) %collective-permute-start.14) | collective-permute-done | bytes 184352 | tf_op jit(solution)/shard_map/ppermute | solution.py:248
  47.6 0.1 add_convert_fusion
  47.7 0.6 %collective-permute-start.15 = (bf16[720,128]{1,0:T(8,128)(2,1)S(1)}, bf16[720,128]{1,0:T(8,128)(2,1)S(1)}, u32[]{:S(2)}, u32[]{:S(2)}) collective-permute-start(bf16[720,128]{1,0:T(8,128)(2,1)S(1)} %add_convert_fusion), channel_id=1, source_target_pairs={{0,4},{1,5},{2,6},{3,7},{4,0},{5,1},{6,2},{7,3},{8,12},{9,13},{10,... | collective-permute-start | bytes 552968 | tf_op jit(solution)/shard_map/ppermute | solution.py:245
  48.3 3.4 %collective-permute-done.12 = bf16[720,128]{1,0:T(8,128)(2,1)S(1)} collective-permute-done((bf16[720,128]{1,0:T(8,128)(2,1)}, bf16[720,128]{1,0:T(8,128)(2,1)S(1)}, u32[]{:S(2)}, u32[]{:S(2)}) %collective-permute-start.12) | collective-permute-done | bytes 184352 | tf_op jit(solution)/shard_map/ppermute | solution.py:248
  51.7 1.6 %collective-permute-done.15 = bf16[720,128]{1,0:T(8,128)(2,1)S(1)} collective-permute-done((bf16[720,128]{1,0:T(8,128)(2,1)S(1)}, bf16[720,128]{1,0:T(8,128)(2,1)S(1)}, u32[]{:S(2)}, u32[]{:S(2)}) %collective-permute-start.15) | collective-permute-done | bytes 184352 | tf_op jit(solution)/shard_map/ppermute | solution.py:245
  53.3 0.1 fusion.3
  53.4 2.6 %collective-permute-start.16 = (bf16[720,128]{1,0:T(8,128)(2,1)S(1)}, bf16[720,128]{1,0:T(8,128)(2,1)S(1)}, u32[]{:S(2)}, u32[]{:S(2)}) collective-permute-start(bf16[720,128]{1,0:T(8,128)(2,1)S(1)} %fusion.3), channel_id=1, source_target_pairs={{0,16},{8,24},{16,0},{24,8},{1,17},{9,25},{17,1},{25,9},{2,18},{10... | collective-permute-start | bytes 552968 | tf_op jit(solution)/shard_map/ppermute | solution.py:248
  56.0 0.2 shard_map.119
  56.2 0.0 copy-start.10
  56.3 0.8 %reshape.36 = bf16[512,2,128]{2,1,0:T(2,128)(2,1)} reshape(bf16[512,256]{1,0:T(8,128)(2,1)S(1)} %shard_map.119) | data formatting | bytes 524288 | tf_op jit(solution)/shard_map/reshape | solution.py:329
  57.0 5.3 %collective-permute-done.16 = bf16[720,128]{1,0:T(8,128)(2,1)S(1)} collective-permute-done((bf16[720,128]{1,0:T(8,128)(2,1)S(1)}, bf16[720,128]{1,0:T(8,128)(2,1)S(1)}, u32[]{:S(2)}, u32[]{:S(2)}) %collective-permute-start.16) | collective-permute-done | bytes 184352 | tf_op jit(solution)/shard_map/ppermute | solution.py:248
  62.3 0.8 %fusion.4 = bf16[128,720]{0,1:T(8,128)(2,1)} fusion(bf16[720,128]{1,0:T(8,128)(2,1)S(1)} %collective-permute-done.16, bf16[720,128]{1,0:T(8,128)(2,1)S(1)} %collective-permute-done.15, bf16[720,128]{1,0:T(8,128)(2,1)S(1)} %collective-permute-done.12, bf16[720,128]{1,0:T(8,128)(2,1)S(1)} %get-tuple-element.20, f32[720]{0:T(1024)S(1)} %copy-done.10, pred[]{:T(512)S(6)} %eq.10), kind=kLoop, calls=%fused_computation.12 | loop fusion | flops 829440 | bytes 924481 | tf_op jit(solution)/shard_map/transpose | solution.py:329
  (30 shorter events, 0.1 us)
Async XLA Ops:
  0.6 1.1 %copy-start.9 = (bf16[128,2,128]{2,1,0:T(2,128)(2,1)S(1)}, bf16[128,2,128]{2,1,0:T(2,128)(2,1)}, u32[]{:S(2)}) copy-start(bf16[128,2,128]{2,1,0:T(2,128)(2,1)} %param.11) | copy-start | bytes 196612
  0.6 1.1 %copy-start.3 = (s32[128]{0:T(128)S(1)}, s32[128]{0:T(128)}, u32[]{:S(2)}) copy-start(s32[128]{0:T(128)} %refs_2_.5) | copy-start | bytes 1540
  0.7 1.1 %copy-start.4 = (s32[128]{0:T(128)S(1)}, s32[128]{0:T(128)}, u32[]{:S(2)}) copy-start(s32[128]{0:T(128)} %param.16) | copy-start | bytes 1540
  0.7 1.1 %copy-start.5 = (s32[512]{0:T(512)S(1)}, s32[512]{0:T(512)}, u32[]{:S(2)}) copy-start(s32[512]{0:T(512)} %param.13) | copy-start | bytes 6148
  0.7 1.1 %copy-start.7 = (s32[128]{0:T(128)S(1)}, s32[128]{0:T(128)}, u32[]{:S(2)}) copy-start(s32[128]{0:T(128)} %param.14) | copy-start | bytes 1540
  0.7 7.0 %copy-start.8 = (bf16[128,1024]{1,0:T(8,128)(2,1)S(1)}, bf16[128,1024]{1,0:T(8,128)(2,1)}, u32[]{:S(2)}) copy-start(bf16[128,1024]{1,0:T(8,128)(2,1)} %param.10) | copy-start | bytes 786436
  1.7 6.2 %copy-start = (bf16[1024,360]{0,1:T(8,128)(2,1)S(1)}, bf16[1024,360]{0,1:T(8,128)(2,1)}, u32[]{:S(2)}) copy-start(bf16[1024,360]{0,1:T(8,128)(2,1)} %param.18) | copy-start | bytes 2211844
  3.1 4.9 %collective-permute-start.1 = (bf16[1040,128]{1,0:T(8,128)(2,1)S(1)}, bf16[1040,128]{1,0:T(8,128)(2,1)S(1)}, u32[]{:S(2)}, u32[]{:S(2)}) collective-permute-start(bf16[1040,128]{1,0:T(8,128)(2,1)S(1)} %shard_map.113.refs_6_), channel_id=1, source_target_pairs={{0,1},{1,0},{2,3},{3,2},{4,5},{5,4},{6,7},{7,6},{8,9},{9,8},{10,11... | collective-permute-start | bytes 798728 | tf_op jit(solution)/shard_map/ppermute | solution.py:245
  3.6 9.6 %collective-permute-start = (bf16[1040,128]{1,0:T(8,128)(2,1)S(1)}, bf16[1040,128]{1,0:T(8,128)(2,1)S(1)}, u32[]{:S(2)}, u32[]{:S(2)}) collective-permute-start(bf16[1040,128]{1,0:T(8,128)(2,1)S(1)} %shard_map.113.refs_6_), channel_id=1, source_target_pairs={{0,2},{1,3},{2,0},{3,1},{4,6},{5,7},{6,4},{7,5},{8,10},{9,11},{10,... | collective-permute-start | bytes 798728 | tf_op jit(solution)/shard_map/ppermute | solution.py:245
  6.2 8.5 %collective-permute-start.4 = (bf16[1040,128]{1,0:T(8,128)(2,1)S(1)}, bf16[1040,128]{1,0:T(8,128)(2,1)S(1)}, u32[]{:S(2)}, u32[]{:S(2)}) collective-permute-start(bf16[1040,128]{1,0:T(8,128)(2,1)S(1)} %shard_map.113.refs_6_), channel_id=1, source_target_pairs={{0,4},{1,5},{2,6},{3,7},{4,0},{5,1},{6,2},{7,3},{8,12},{9,13},{10,... | collective-permute-start | bytes 798728 | tf_op jit(solution)/shard_map/ppermute | solution.py:245
  7.9 0.7 %copy-start.6 = (f32[16]{0:T(128)S(1)}, f32[16]{0:T(128)}, u32[]{:S(2)}) copy-start(f32[16]{0:T(128)} %refs_1_.5) | copy-start | bytes 196
  13.2 3.9 %collective-permute-start.3 = (bf16[1040,128]{1,0:T(8,128)(2,1)S(1)}, bf16[1040,128]{1,0:T(8,128)(2,1)}, u32[]{:S(2)}, u32[]{:S(2)}) collective-permute-start(bf16[1040,128]{1,0:T(8,128)(2,1)S(1)} %broadcast_add_fusion.1.refs_6_), channel_id=1, source_target_pairs={{0,1},{1,0},{2,3},{3,2},{4,5},{5,4},{6,7},{7,6},{8,9},{9,8},{10,11... | collective-permute-start | bytes 798728 | tf_op jit(solution)/shard_map/ppermute | solution.py:245
  14.6 2.5 %collective-permute-start.5 = (bf16[1040,128]{1,0:T(8,128)(2,1)S(1)}, bf16[1040,128]{1,0:T(8,128)(2,1)}, u32[]{:S(2)}, u32[]{:S(2)}) collective-permute-start(bf16[1040,128]{1,0:T(8,128)(2,1)S(1)} %collective-permute-done.4.refs_8_), channel_id=1, source_target_pairs={{0,1},{1,0},{2,3},{3,2},{4,5},{5,4},{6,7},{7,6},{8,9},{9,8},{10,11... | collective-permute-start | bytes 798728 | tf_op jit(solution)/shard_map/ppermute | solution.py:245
  14.6 8.9 %collective-permute-start.2 = (bf16[1040,128]{1,0:T(8,128)(2,1)S(1)}, bf16[1040,128]{1,0:T(8,128)(2,1)}, u32[]{:S(2)}, u32[]{:S(2)}) collective-permute-start(bf16[1040,128]{1,0:T(8,128)(2,1)S(1)} %broadcast_add_fusion.1.refs_6_), channel_id=1, source_target_pairs={{0,4},{1,5},{2,6},{3,7},{4,0},{5,1},{6,2},{7,3},{8,12},{9,13},{10,... | collective-permute-start | bytes 798728 | tf_op jit(solution)/shard_map/ppermute | solution.py:245
  16.2 18.8 %collective-permute-start.8 = (bf16[360,1024]{1,0:T(8,128)(2,1)}, bf16[360,1024]{1,0:T(8,128)(2,1)S(1)}, u32[]{:S(2)}, u32[]{:S(2)}) collective-permute-start(bf16[360,1024]{1,0:T(8,128)(2,1)} %get-tuple-element.18), channel_id=1, source_target_pairs={{0,2},{1,3},{2,0},{3,1},{4,6},{5,7},{6,4},{7,5},{8,10},{9,11},{10,... | collective-permute-start | bytes 2211848 | tf_op jit(solution)/shard_map/ppermute | solution.py:245
  21.9 0.9 %copy-start.1 = (f32[80,2048]{1,0:T(8,128)}, f32[80,2048]{1,0:T(8,128)S(1)}, u32[]{:S(2)}) copy-start(f32[80,2048]{1,0:T(8,128)S(1)} %get-tuple-element.16.refs_8_) | copy-start | bytes 1966084
  24.5 1.6 %collective-permute-start.6 = (bf16[1040,128]{1,0:T(8,128)(2,1)S(1)}, bf16[1040,128]{1,0:T(8,128)(2,1)S(1)}, u32[]{:S(2)}, u32[]{:S(2)}) collective-permute-start(bf16[1040,128]{1,0:T(8,128)(2,1)S(1)} %broadcast_add_fusion.refs_6_), channel_id=1, source_target_pairs={{0,1},{1,0},{2,3},{3,2},{4,5},{5,4},{6,7},{7,6},{8,9},{9,8},{10,11... | collective-permute-start | bytes 798728 | tf_op jit(solution)/shard_map/ppermute | solution.py:245
  24.6 11.9 %collective-permute-start.7 = (bf16[360,1024]{1,0:T(8,128)(2,1)}, bf16[360,1024]{1,0:T(8,128)(2,1)S(1)}, u32[]{:S(2)}, u32[]{:S(2)}) collective-permute-start(bf16[360,1024]{1,0:T(8,128)(2,1)} %get-tuple-element.18), channel_id=1, source_target_pairs={{0,1},{1,0},{2,3},{3,2},{4,5},{5,4},{6,7},{7,6},{8,9},{9,8},{10,11... | collective-permute-start | bytes 2211848 | tf_op jit(solution)/shard_map/ppermute | solution.py:245
  26.1 1.1 %copy-start.2 = (f32[80,2048]{1,0:T(8,128)S(1)}, f32[80,2048]{1,0:T(8,128)}, u32[]{:S(2)}) copy-start(f32[80,2048]{1,0:T(8,128)} %copy-done.1) | copy-start | bytes 1966084
  31.0 8.7 %collective-permute-start.13 = (bf16[1024,128]{1,0:T(8,128)(2,1)}, bf16[1024,128]{1,0:T(8,128)(2,1)}, u32[]{:S(2)}, u32[]{:S(2)}) collective-permute-start(bf16[1024,128]{1,0:T(8,128)(2,1)} %get-tuple-element.17.rows_ref), channel_id=1, source_target_pairs={{0,4},{1,5},{2,6},{3,7},{4,0},{5,1},{6,2},{7,3},{8,12},{9,13},{10,... | collective-permute-start | bytes 786440 | tf_op jit(solution)/shard_map/ppermute | solution.py:245
  36.0 3.8 %collective-permute-start.10 = (bf16[120,1024]{1,0:T(8,128)(2,1)}, bf16[120,1024]{1,0:T(8,128)(2,1)S(1)}, u32[]{:S(2)}, u32[]{:S(2)}) collective-permute-start(bf16[120,1024]{1,0:T(8,128)(2,1)} %get-tuple-element.25), channel_id=1, source_target_pairs={{0,1},{1,0},{2,3},{3,2},{4,5},{5,4},{6,7},{7,6},{8,9},{9,8},{10,11... | collective-permute-start | bytes 737288 | tf_op jit(solution)/shard_map/ppermute | solution.py:245
  36.0 3.8 %collective-permute-start.11 = (bf16[120,1024]{1,0:T(8,128)(2,1)}, bf16[120,1024]{1,0:T(8,128)(2,1)S(1)}, u32[]{:S(2)}, u32[]{:S(2)}) collective-permute-start(bf16[120,1024]{1,0:T(8,128)(2,1)} %get-tuple-element.24), channel_id=1, source_target_pairs={{0,1},{1,0},{2,3},{3,2},{4,5},{5,4},{6,7},{7,6},{8,9},{9,8},{10,11... | collective-permute-start | bytes 737288 | tf_op jit(solution)/shard_map/ppermute | solution.py:245
  36.5 3.3 %collective-permute-start.9 = (bf16[120,1024]{1,0:T(8,128)(2,1)}, bf16[120,1024]{1,0:T(8,128)(2,1)S(1)}, u32[]{:S(2)}, u32[]{:S(2)}) collective-permute-start(bf16[120,1024]{1,0:T(8,128)(2,1)} %get-tuple-element.26), channel_id=1, source_target_pairs={{0,1},{1,0},{2,3},{3,2},{4,5},{5,4},{6,7},{7,6},{8,9},{9,8},{10,11... | collective-permute-start | bytes 737288 | tf_op jit(solution)/shard_map/ppermute | solution.py:245
  41.7 5.9 %collective-permute-start.14 = (bf16[720,128]{1,0:T(8,128)(2,1)S(1)}, bf16[720,128]{1,0:T(8,128)(2,1)S(1)}, u32[]{:S(2)}, u32[]{:S(2)}) collective-permute-start(bf16[720,128]{1,0:T(8,128)(2,1)S(1)} %get-tuple-element.23), channel_id=1, source_target_pairs={{0,8},{8,0},{16,24},{24,16},{1,9},{9,1},{17,25},{25,17},{2,10},{10... | collective-permute-start | bytes 552968 | tf_op jit(solution)/shard_map/ppermute | solution.py:248
  45.9 5.8 %collective-permute-start.12 = (bf16[720,128]{1,0:T(8,128)(2,1)}, bf16[720,128]{1,0:T(8,128)(2,1)S(1)}, u32[]{:S(2)}, u32[]{:S(2)}) collective-permute-start(bf16[720,128]{1,0:T(8,128)(2,1)} %get-tuple-element.21), channel_id=1, source_target_pairs={{0,8},{8,0},{16,24},{24,16},{1,9},{9,1},{17,25},{25,17},{2,10},{10... | collective-permute-start | bytes 552968 | tf_op jit(solution)/shard_map/ppermute | solution.py:248
  47.7 5.6 %collective-permute-start.15 = (bf16[720,128]{1,0:T(8,128)(2,1)S(1)}, bf16[720,128]{1,0:T(8,128)(2,1)S(1)}, u32[]{:S(2)}, u32[]{:S(2)}) collective-permute-start(bf16[720,128]{1,0:T(8,128)(2,1)S(1)} %add_convert_fusion), channel_id=1, source_target_pairs={{0,4},{1,5},{2,6},{3,7},{4,0},{5,1},{6,2},{7,3},{8,12},{9,13},{10,... | collective-permute-start | bytes 552968 | tf_op jit(solution)/shard_map/ppermute | solution.py:245
  53.4 9.0 %collective-permute-start.16 = (bf16[720,128]{1,0:T(8,128)(2,1)S(1)}, bf16[720,128]{1,0:T(8,128)(2,1)S(1)}, u32[]{:S(2)}, u32[]{:S(2)}) collective-permute-start(bf16[720,128]{1,0:T(8,128)(2,1)S(1)} %fusion.3), channel_id=1, source_target_pairs={{0,16},{8,24},{16,0},{24,8},{1,17},{9,25},{17,1},{25,9},{2,18},{10... | collective-permute-start | bytes 552968 | tf_op jit(solution)/shard_map/ppermute | solution.py:248
  56.2 6.1 %copy-start.10 = (f32[720]{0:T(1024)S(1)}, f32[720]{0:T(1024)}, u32[]{:S(2)}) copy-start(f32[720]{0:T(1024)} %param.19) | copy-start | bytes 8644

commit v4 on v3

--- a/solution.py
+++ b/solution.py
@@ -151,14 +151,13 @@
         load.wait()
     half = heads // 2 * tokens
 
-    def pair(index, carry):
-        at = pl.multiple_of(index * 256, 256)
-        keys = key_scr[pl.ds(at, 256), :]
-        rows = row_scr[pl.ds(at, 256), :]
+    def block(at, size):
+        keys = key_scr[pl.ds(at, size), :]
+        rows = row_scr[pl.ds(at, size), :]
         seen = (rows[:, :1] == tseg) & (rows[:, 1:2] <= tok)
         bias = jnp.concatenate([jnp.where(seen, 0.0, HIDE)] * (heads // 2), axis=1)
-        turned = dot_nt(eye, val_scr[pl.ds(at, 256), :]).astype(BF16)
-        ones = jnp.ones((16, 256), BF16)
+        turned = dot_nt(eye, val_scr[pl.ds(at, size), :]).astype(BF16)
+        ones = jnp.ones((16, size), BF16)
         spans = [slice(group * half, (group + 1) * half) for group in range(2)]
         scores = [jnp.dot(keys, q_scr[:, span], preferred_element_type=F32) + bias for span in spans]
         peaks = [acc_scr[72:73, span] for span in spans]
@@ -169,9 +168,18 @@
             new = jnp.dot(vals, weights[group], preferred_element_type=F32)[:72, :]
             acc_scr[:72, span] = acc_scr[:72, span] * jnp.exp(peaks[group] - tops[group]) + new
             acc_scr[72:80, span] = jnp.broadcast_to(tops[group], (8, half))
+
+    def pair(index, carry):
+        block(pl.multiple_of(index * 256, 256), 256)
         return carry
 
-    lax.fori_loop(0, (used + 255) // 256, pair, 0)
+    tiles_used = (used + 127) >> 7
+    lax.fori_loop(0, tiles_used >> 1, pair, 0)
+
+    @pl.when((tiles_used & 1) == 1)
+    def _():
+        block(pl.multiple_of((tiles_used - 1) * 128, 128), 128)
+
     if not last:
         save = pltpu.make_async_copy(acc_scr, out_ref, moved.at[1])
         save.start()

time: 63.3 us -> 63.7 us (level)
  starting transfers between devices: 14.2 us -> 17.3 us
  waiting for transfers between devices: 22.6 us -> 20.6 us
  Pallas kernels: 17.7 us -> 16.8 us
    ppermute x14, starting transfers between devices: 9.44 us -> 12.6 us  [gy(): return lax.ppermute(value, 'gy', [(i, i ^ m) for i in range(8)])]
    ppermute x14, waiting for transfers between devices: 12.7 us -> 10 us  [gy(): return lax.ppermute(value, 'gy', [(i, i ^ m) for i in range(8)])]
    pallas_call x3, Pallas kernels: 11.7 us -> 10.7 us  [attend(): pl.pallas_call(functools.partial(attend_kernel, first, last, count), out_...]
    ppermute x3, waiting for transfers between devices: 9.93 us -> 10.6 us  [gx(): return lax.ppermute(value, 'gx', [(i, i ^ m) for i in range(4)])]
  transfers between devices with their start and end apart: 17 -> 17, of which waited for: 10 -> 10; matrix products, arithmetic and copies ran while one was open for 5% -> 5% of each run, Pallas kernels for 23% -> 21%
where the time goes in v4:
time: 63.7 us; the launch traced here: 63.4 us
  waiting for transfers between devices  20.6 us (32%)
  starting transfers between devices  17.3 us (27%)
  Pallas kernels  16.8 us (26%)
  local copies, waits for them, and re-layouts  4.62 us (7%)
  other arithmetic  3.18 us (5%)
  between operations  0.87 us (1%)
    ppermute x14, starting transfers between devices, gy(): return lax.ppermute(value, 'gy', [(i, i ^ m) for i in range(8)])  12.6 us
    pallas_call x3, Pallas kernels, attend(): pl.pallas_call(functools.partial(attend_kernel, first, last, count), out_...  10.7 us
    ppermute x3, waiting for transfers between devices, gx(): return lax.ppermute(value, 'gx', [(i, i ^ m) for i in range(4)])  10.6 us
    ppermute x14, waiting for transfers between devices, gy(): return lax.ppermute(value, 'gy', [(i, i ^ m) for i in range(8)])  10 us
    ppermute x3, starting transfers between devices, gx(): return lax.ppermute(value, 'gx', [(i, i ^ m) for i in range(4)])  4.75 us
    unnamed x25, local copies, waits for them, and re-layouts  3.86 us
    pallas_call x1, Pallas kernels, tuned(): keep_a, keep_b = project(pos, attention, w0, w1, w2, *w3)  2.6 us
    pallas_call x1, Pallas kernels, tuned(): send_a, send_b = project(pos, other, w0, w1, w2, *w3)  1.93 us
  transfers between devices with their start and end apart: 17, of which 10 were waited for; matrix products, arithmetic and copies ran while one was open for 5% of the time, Pallas kernels for 21%

profile of v4, /device:TPU:0, one launch (start us, length us, event | category | flops | bytes accessed | tf_op | source)
XLA Modules:
  0.0 63.4 jit_solution(14821893010855319796)
XLA Ops:
  0.7 1.0 %copy.17 = bf16[64,8,2,128]{3,1,2,0:T(8,128)(2,1)S(1)} copy(bf16[64,8,2,128]{3,2,1,0:T(2,128)(2,1)} %bitcast.52) | data formatting | bytes 524288
  1.7 0.0 copy-start
  1.8 1.3 %shard_map.113.refs_6_ = bf16[1040,128]{1,0:T(8,128)(2,1)S(1)} custom-call(s32[1]{0:T(128)} %bitcast.7.base_ref, bf16[512,256]{1,0:T(8,128)(2,1)S(1)} %bitcast.31, bf16[128,256]{1,0:T(8,128)(2,1)S(1)} %bitcast.36, s32[1,128]{1,0:T(1,128)S(1)} %bitcast.48, s32[1,128]{1,0:T(1,128)S(1)} %bitcast.42, s32[1,512]{1,0:T(1,128)S(1)} %bitcast.47, s32[1,128]{1,0:T(1,128)S(1)} %bitcast.38), custom_call_target="tpu_custom_call" | custom-call | tf_op jit(solution)/shard_map/pallas_call | solution.py:266
  3.1 0.5 collective-permute-start.1
  3.6 2.6 %collective-permute-start = (bf16[1040,128]{1,0:T(8,128)(2,1)S(1)}, bf16[1040,128]{1,0:T(8,128)(2,1)S(1)}, u32[]{:S(2)}, u32[]{:S(2)}) collective-permute-start(bf16[1040,128]{1,0:T(8,128)(2,1)S(1)} %shard_map.113.refs_6_), channel_id=1, source_target_pairs={{0,2},{1,3},{2,0},{3,1},{4,6},{5,7},{6,4},{7,5},{8,10},{9,11},{10,... | collective-permute-start | bytes 798728 | tf_op jit(solution)/shard_map/ppermute | solution.py:253
  6.2 1.5 %collective-permute-start.4 = (bf16[1040,128]{1,0:T(8,128)(2,1)S(1)}, bf16[1040,128]{1,0:T(8,128)(2,1)S(1)}, u32[]{:S(2)}, u32[]{:S(2)}) collective-permute-start(bf16[1040,128]{1,0:T(8,128)(2,1)S(1)} %shard_map.113.refs_6_), channel_id=1, source_target_pairs={{0,4},{1,5},{2,6},{3,7},{4,0},{5,1},{6,2},{7,3},{8,12},{9,13},{10,... | collective-permute-start | bytes 798728 | tf_op jit(solution)/shard_map/ppermute | solution.py:253
  7.7 0.2 copy.12
  7.9 0.1 pad_add_fusion.2.refs_0_
  7.9 0.7 %copy-done.6 = f32[16]{0:T(128)S(1)} copy-done((f32[16]{0:T(128)S(1)}, f32[16]{0:T(128)}, u32[]{:S(2)}) %copy-start.6) | copy-done | bytes 88
  8.6 3.1 %shard_map.114 = (f32[80,2048]{1,0:T(8,128)S(1)}, bf16[1,128]{1,0:T(2,128)(2,1)S(1)}, bf16[360,1024]{1,0:T(8,128)(2,1)}) custom-call(s32[2]{0:T(128)S(1)} %pad_add_fusion.2.refs_0_, f32[16]{0:T(128)S(1)} %copy-done.6, s32[128]{0:T(128)S(1)} %copy-done.3, bf16[1024,128]{1,0:T(8,128)(2,1)S(1)} %bitcast.33, s32[1,128]{1,0:T(1,128)S(1)} %bitcast.39, ...), custom_call_target="tpu_custom_call" | custom-call | flops 268435456 | bytes 1000000 | tf_op jit(solution)/shard_map/pallas_call | solution.py:208
  11.7 1.5 %collective-permute-done = bf16[1040,128]{1,0:T(8,128)(2,1)S(1)} collective-permute-done((bf16[1040,128]{1,0:T(8,128)(2,1)S(1)}, bf16[1040,128]{1,0:T(8,128)(2,1)S(1)}, u32[]{:S(2)}, u32[]{:S(2)}) %collective-permute-start) | collective-permute-done | bytes 266272 | tf_op jit(solution)/shard_map/ppermute | solution.py:253
  13.2 0.1 collective-permute-start.3
  13.3 1.4 %collective-permute-done.4.refs_8_ = bf16[1040,128]{1,0:T(8,128)(2,1)S(1)} collective-permute-done((bf16[1040,128]{1,0:T(8,128)(2,1)S(1)}, bf16[1040,128]{1,0:T(8,128)(2,1)S(1)}, u32[]{:S(2)}, u32[]{:S(2)}) %collective-permute-start.4) | collective-permute-done | bytes 266272 | tf_op jit(solution)/shard_map/ppermute | solution.py:253
  14.6 1.5 %collective-permute-start.2 = (bf16[1040,128]{1,0:T(8,128)(2,1)S(1)}, bf16[1040,128]{1,0:T(8,128)(2,1)}, u32[]{:S(2)}, u32[]{:S(2)}) collective-permute-start(bf16[1040,128]{1,0:T(8,128)(2,1)S(1)} %broadcast_add_fusion.1.refs_6_), channel_id=1, source_target_pairs={{0,4},{1,5},{2,6},{3,7},{4,0},{5,1},{6,2},{7,3},{8,12},{9,13},{10,... | collective-permute-start | bytes 798728 | tf_op jit(solution)/shard_map/ppermute | solution.py:253
  16.2 0.1 pad_add_fusion.3.refs_0_
  16.2 0.9 %collective-permute-start.8 = (bf16[360,1024]{1,0:T(8,128)(2,1)}, bf16[360,1024]{1,0:T(8,128)(2,1)S(1)}, u32[]{:S(2)}, u32[]{:S(2)}) collective-permute-start(bf16[360,1024]{1,0:T(8,128)(2,1)} %get-tuple-element.18), channel_id=1, source_target_pairs={{0,2},{1,3},{2,0},{3,1},{4,6},{5,7},{6,4},{7,5},{8,10},{9,11},{10,... | collective-permute-start | bytes 2211848 | tf_op jit(solution)/shard_map/ppermute | solution.py:253
  17.1 4.8 %shard_map.115 = (f32[80,2048]{1,0:T(8,128)S(1)}, bf16[1,128]{1,0:T(2,128)(2,1)S(1)}) custom-call(s32[4]{0:T(128)S(1)} %pad_add_fusion.3.refs_0_, f32[16]{0:T(128)S(1)} %copy-done.6, s32[128]{0:T(128)S(1)} %copy-done.3, bf16[1024,128]{1,0:T(8,128)(2,1)S(1)} %bitcast.34, s32[1,128]{1,0:T(1,128)S(1)} %bitcast.40, s32[1,128]{1,0:T(1,128)S(1)} %bitcast.44, ...), custom_call_target="tpu_custom_call" | custom-call | flops 536870912 | bytes 1000000 | tf_op jit(solution)/shard_map/pallas_call | solution.py:208
  22.0 0.9 %copy-done.1 = f32[80,2048]{1,0:T(8,128)} copy-done((f32[80,2048]{1,0:T(8,128)}, f32[80,2048]{1,0:T(8,128)S(1)}, u32[]{:S(2)}) %copy-start.1) | copy-done | bytes 655384
  22.8 0.7 %collective-permute-done.2 = bf16[1040,128]{1,0:T(8,128)(2,1)} collective-permute-done((bf16[1040,128]{1,0:T(8,128)(2,1)S(1)}, bf16[1040,128]{1,0:T(8,128)(2,1)}, u32[]{:S(2)}, u32[]{:S(2)}) %collective-permute-start.2) | collective-permute-done | bytes 266272 | tf_op jit(solution)/shard_map/ppermute | solution.py:253
  23.5 1.0 %broadcast_add_fusion.refs_6_ = bf16[1040,128]{1,0:T(8,128)(2,1)S(1)} fusion(bf16[1040,128]{1,0:T(8,128)(2,1)} %collective-permute-done.2, bf16[128]{0:T(256)(128)(2,1)S(1)} %bitcast.50), kind=kLoop, calls=%fused_computation.13 | loop fusion | flops 133120 | bytes 532736 | tf_op jit(solution)/shard_map/add | solution.py:301
  24.5 0.1 collective-permute-start.6
  24.6 0.5 collective-permute-start.7
  25.1 0.1 pad_add_fusion.1.refs_0_
  25.2 1.0 %collective-permute-done.6.refs_7_ = bf16[1040,128]{1,0:T(8,128)(2,1)S(1)} collective-permute-done((bf16[1040,128]{1,0:T(8,128)(2,1)S(1)}, bf16[1040,128]{1,0:T(8,128)(2,1)S(1)}, u32[]{:S(2)}, u32[]{:S(2)}) %collective-permute-start.6) | collective-permute-done | bytes 266272 | tf_op jit(solution)/shard_map/ppermute | solution.py:253
  26.1 1.1 %copy-done.2 = f32[80,2048]{1,0:T(8,128)S(1)} copy-done((f32[80,2048]{1,0:T(8,128)S(1)}, f32[80,2048]{1,0:T(8,128)}, u32[]{:S(2)}) %copy-start.2) | copy-done | bytes 655384
  27.2 2.8 %shard_map.116 = (bf16[1024,128]{1,0:T(8,128)(2,1)}, bf16[1,1024]{1,0:T(2,128)(2,1)S(1)}) custom-call(s32[2]{0:T(128)S(1)} %pad_add_fusion.1.refs_0_, f32[16]{0:T(128)S(1)} %copy-done.6, s32[128]{0:T(128)S(1)} %copy-done.3, bf16[1024,128]{1,0:T(8,128)(2,1)S(1)} %bitcast.35, s32[1,128]{1,0:T(1,128)S(1)} %bitcast.41, s32[1,128]{1,0:T(1,128)S(1)} %bitcast.45, ...), custom_call_target="tpu_custom_call" | custom-call | flops 268435456 | bytes 1000000 | tf_op jit(solution)/shard_map/pallas_call | solution.py:208
  30.1 3.2 %collective-permute-start.13 = (bf16[1024,128]{1,0:T(8,128)(2,1)}, bf16[1024,128]{1,0:T(8,128)(2,1)}, u32[]{:S(2)}, u32[]{:S(2)}) collective-permute-start(bf16[1024,128]{1,0:T(8,128)(2,1)} %get-tuple-element.17.rows_ref), channel_id=1, source_target_pairs={{0,4},{1,5},{2,6},{3,7},{4,0},{5,1},{6,2},{7,3},{8,12},{9,13},{10,... | collective-permute-start | bytes 786440 | tf_op jit(solution)/shard_map/ppermute | solution.py:253
  33.3 1.8 %collective-permute-done.8.w2_ref = bf16[360,1024]{1,0:T(8,128)(2,1)S(1)} collective-permute-done((bf16[360,1024]{1,0:T(8,128)(2,1)}, bf16[360,1024]{1,0:T(8,128)(2,1)S(1)}, u32[]{:S(2)}, u32[]{:S(2)}) %collective-permute-start.8) | collective-permute-done | bytes 737312 | tf_op jit(solution)/shard_map/ppermute | solution.py:253
  35.1 0.9 %slice_add_fusion = (bf16[120,1024]{1,0:T(8,128)(2,1)}, bf16[120,1024]{1,0:T(8,128)(2,1)}, bf16[120,1024]{1,0:T(8,128)(2,1)}) fusion(bf16[360,1024]{1,0:T(8,128)(2,1)S(1)} %collective-permute-done.8.w2_ref, bf16[1024]{0:T(1024)(128)(2,1)S(1)} %reduce), kind=kLoop, calls=%fused_computation.9 | loop fusion | flops 368640 | bytes 1476608 | tf_op jit(solution)/shard_map/add | solution.py:306
  36.0 0.5 collective-permute-start.11
  36.5 0.1 pad_add_fusion.pos_ref
  36.5 2.0 %collective-permute-done.13.rows_ref = bf16[1024,128]{1,0:T(8,128)(2,1)} collective-permute-done((bf16[1024,128]{1,0:T(8,128)(2,1)}, bf16[1024,128]{1,0:T(8,128)(2,1)}, u32[]{:S(2)}, u32[]{:S(2)}) %collective-permute-start.13) | collective-permute-done | bytes 262176 | tf_op jit(solution)/shard_map/ppermute | solution.py:253
  38.6 1.9 %shard_map.118 = (bf16[720,128]{1,0:T(8,128)(2,1)S(1)}, bf16[720,128]{1,0:T(8,128)(2,1)S(1)}) custom-call(s32[2]{0:T(128)S(1)} %pad_add_fusion.pos_ref, bf16[1024,128]{1,0:T(8,128)(2,1)} %collective-permute-done.13.rows_ref, bf16[360,1024]{1,0:T(8,128)(2,1)S(1)} %bitcast.29, bf16[360,1024]{1,0:T(8,128)(2,1)S(1)} %collective-permute-done.7.w1_ref, ...), custom_call_target="tpu_custom_call" | custom-call | flops 754974720 | bytes 4194304 | tf_op jit(solution)/shard_map/pallas_call | solution.py:320
  40.5 1.6 %collective-permute-start.14 = (bf16[720,128]{1,0:T(8,128)(2,1)S(1)}, bf16[720,128]{1,0:T(8,128)(2,1)S(1)}, u32[]{:S(2)}, u32[]{:S(2)}) collective-permute-start(bf16[720,128]{1,0:T(8,128)(2,1)S(1)} %get-tuple-element.23), channel_id=1, source_target_pairs={{0,8},{8,0},{16,24},{24,16},{1,9},{9,1},{17,25},{25,17},{2,10},{10... | collective-permute-start | bytes 552968 | tf_op jit(solution)/shard_map/ppermute | solution.py:256
  42.2 2.6 %shard_map.117 = (bf16[720,128]{1,0:T(8,128)(2,1)}, bf16[720,128]{1,0:T(8,128)(2,1)S(1)}) custom-call(s32[2]{0:T(128)S(1)} %pad_add_fusion.pos_ref, bf16[1024,128]{1,0:T(8,128)(2,1)} %get-tuple-element.17.rows_ref, bf16[360,1024]{1,0:T(8,128)(2,1)S(1)} %bitcast.30, bf16[360,1024]{1,0:T(8,128)(2,1)S(1)} %collective-permute-done.7.w1_ref, ...), custom_call_target="tpu_custom_call" | custom-call | flops 754974720 | bytes 4194304 | tf_op jit(solution)/shard_map/pallas_call | solution.py:318
  44.8 0.4 collective-permute-start.12
  45.2 1.9 %collective-permute-done.14 = bf16[720,128]{1,0:T(8,128)(2,1)S(1)} collective-permute-done((bf16[720,128]{1,0:T(8,128)(2,1)S(1)}, bf16[720,128]{1,0:T(8,128)(2,1)S(1)}, u32[]{:S(2)}, u32[]{:S(2)}) %collective-permute-start.14) | collective-permute-done | bytes 184352 | tf_op jit(solution)/shard_map/ppermute | solution.py:256
  47.1 0.1 add_convert_fusion
  47.1 1.2 %collective-permute-start.15 = (bf16[720,128]{1,0:T(8,128)(2,1)S(1)}, bf16[720,128]{1,0:T(8,128)(2,1)S(1)}, u32[]{:S(2)}, u32[]{:S(2)}) collective-permute-start(bf16[720,128]{1,0:T(8,128)(2,1)S(1)} %add_convert_fusion), channel_id=1, source_target_pairs={{0,4},{1,5},{2,6},{3,7},{4,0},{5,1},{6,2},{7,3},{8,12},{9,13},{10,... | collective-permute-start | bytes 552968 | tf_op jit(solution)/shard_map/ppermute | solution.py:253
  48.4 2.8 %collective-permute-done.12 = bf16[720,128]{1,0:T(8,128)(2,1)S(1)} collective-permute-done((bf16[720,128]{1,0:T(8,128)(2,1)}, bf16[720,128]{1,0:T(8,128)(2,1)S(1)}, u32[]{:S(2)}, u32[]{:S(2)}) %collective-permute-start.12) | collective-permute-done | bytes 184352 | tf_op jit(solution)/shard_map/ppermute | solution.py:256
  51.2 1.6 %collective-permute-done.15 = bf16[720,128]{1,0:T(8,128)(2,1)S(1)} collective-permute-done((bf16[720,128]{1,0:T(8,128)(2,1)S(1)}, bf16[720,128]{1,0:T(8,128)(2,1)S(1)}, u32[]{:S(2)}, u32[]{:S(2)}) %collective-permute-start.15) | collective-permute-done | bytes 184352 | tf_op jit(solution)/shard_map/ppermute | solution.py:253
  52.8 0.1 fusion.3
  52.9 2.7 %collective-permute-start.16 = (bf16[720,128]{1,0:T(8,128)(2,1)S(1)}, bf16[720,128]{1,0:T(8,128)(2,1)S(1)}, u32[]{:S(2)}, u32[]{:S(2)}) collective-permute-start(bf16[720,128]{1,0:T(8,128)(2,1)S(1)} %fusion.3), channel_id=1, source_target_pairs={{0,16},{8,24},{16,0},{24,8},{1,17},{9,25},{17,1},{25,9},{2,18},{10... | collective-permute-start | bytes 552968 | tf_op jit(solution)/shard_map/ppermute | solution.py:256
  55.6 0.2 shard_map.119
  55.8 0.0 copy-start.10
  55.8 0.8 %reshape.36 = bf16[512,2,128]{2,1,0:T(2,128)(2,1)} reshape(bf16[512,256]{1,0:T(8,128)(2,1)S(1)} %shard_map.119) | data formatting | bytes 524288 | tf_op jit(solution)/shard_map/reshape | solution.py:337
  56.6 5.9 %collective-permute-done.16 = bf16[720,128]{1,0:T(8,128)(2,1)S(1)} collective-permute-done((bf16[720,128]{1,0:T(8,128)(2,1)S(1)}, bf16[720,128]{1,0:T(8,128)(2,1)S(1)}, u32[]{:S(2)}, u32[]{:S(2)}) %collective-permute-start.16) | collective-permute-done | bytes 184352 | tf_op jit(solution)/shard_map/ppermute | solution.py:256
  62.5 0.8 %fusion.4 = bf16[128,720]{0,1:T(8,128)(2,1)} fusion(bf16[720,128]{1,0:T(8,128)(2,1)S(1)} %collective-permute-done.16, bf16[720,128]{1,0:T(8,128)(2,1)S(1)} %collective-permute-done.15, bf16[720,128]{1,0:T(8,128)(2,1)S(1)} %collective-permute-done.12, bf16[720,128]{1,0:T(8,128)(2,1)S(1)} %get-tuple-element.20, f32[720]{0:T(1024)S(1)} %copy-done.10, pred[]{:T(512)S(6)} %eq.10), kind=kLoop, calls=%fused_computation.12 | loop fusion | flops 829440 | bytes 924481 | tf_op jit(solution)/shard_map/transpose | solution.py:337
  (30 shorter events, 0.1 us)
Async XLA Ops:
  0.6 1.1 %copy-start.9 = (bf16[128,2,128]{2,1,0:T(2,128)(2,1)S(1)}, bf16[128,2,128]{2,1,0:T(2,128)(2,1)}, u32[]{:S(2)}) copy-start(bf16[128,2,128]{2,1,0:T(2,128)(2,1)} %param.11) | copy-start | bytes 196612
  0.6 1.1 %copy-start.3 = (s32[128]{0:T(128)S(1)}, s32[128]{0:T(128)}, u32[]{:S(2)}) copy-start(s32[128]{0:T(128)} %refs_2_.5) | copy-start | bytes 1540
  0.7 1.1 %copy-start.4 = (s32[128]{0:T(128)S(1)}, s32[128]{0:T(128)}, u32[]{:S(2)}) copy-start(s32[128]{0:T(128)} %param.16) | copy-start | bytes 1540
  0.7 1.1 %copy-start.5 = (s32[512]{0:T(512)S(1)}, s32[512]{0:T(512)}, u32[]{:S(2)}) copy-start(s32[512]{0:T(512)} %param.13) | copy-start | bytes 6148
  0.7 1.1 %copy-start.7 = (s32[128]{0:T(128)S(1)}, s32[128]{0:T(128)}, u32[]{:S(2)}) copy-start(s32[128]{0:T(128)} %param.14) | copy-start | bytes 1540
  0.7 7.0 %copy-start.8 = (bf16[128,1024]{1,0:T(8,128)(2,1)S(1)}, bf16[128,1024]{1,0:T(8,128)(2,1)}, u32[]{:S(2)}) copy-start(bf16[128,1024]{1,0:T(8,128)(2,1)} %param.10) | copy-start | bytes 786436
  1.7 6.2 %copy-start = (bf16[1024,360]{0,1:T(8,128)(2,1)S(1)}, bf16[1024,360]{0,1:T(8,128)(2,1)}, u32[]{:S(2)}) copy-start(bf16[1024,360]{0,1:T(8,128)(2,1)} %param.18) | copy-start | bytes 2211844
  3.1 4.9 %collective-permute-start.1 = (bf16[1040,128]{1,0:T(8,128)(2,1)S(1)}, bf16[1040,128]{1,0:T(8,128)(2,1)S(1)}, u32[]{:S(2)}, u32[]{:S(2)}) collective-permute-start(bf16[1040,128]{1,0:T(8,128)(2,1)S(1)} %shard_map.113.refs_6_), channel_id=1, source_target_pairs={{0,1},{1,0},{2,3},{3,2},{4,5},{5,4},{6,7},{7,6},{8,9},{9,8},{10,11... | collective-permute-start | bytes 798728 | tf_op jit(solution)/shard_map/ppermute | solution.py:253
  3.6 9.6 %collective-permute-start = (bf16[1040,128]{1,0:T(8,128)(2,1)S(1)}, bf16[1040,128]{1,0:T(8,128)(2,1)S(1)}, u32[]{:S(2)}, u32[]{:S(2)}) collective-permute-start(bf16[1040,128]{1,0:T(8,128)(2,1)S(1)} %shard_map.113.refs_6_), channel_id=1, source_target_pairs={{0,2},{1,3},{2,0},{3,1},{4,6},{5,7},{6,4},{7,5},{8,10},{9,11},{10,... | collective-permute-start | bytes 798728 | tf_op jit(solution)/shard_map/ppermute | solution.py:253
  6.2 8.5 %collective-permute-start.4 = (bf16[1040,128]{1,0:T(8,128)(2,1)S(1)}, bf16[1040,128]{1,0:T(8,128)(2,1)S(1)}, u32[]{:S(2)}, u32[]{:S(2)}) collective-permute-start(bf16[1040,128]{1,0:T(8,128)(2,1)S(1)} %shard_map.113.refs_6_), channel_id=1, source_target_pairs={{0,4},{1,5},{2,6},{3,7},{4,0},{5,1},{6,2},{7,3},{8,12},{9,13},{10,... | collective-permute-start | bytes 798728 | tf_op jit(solution)/shard_map/ppermute | solution.py:253
  7.9 0.7 %copy-start.6 = (f32[16]{0:T(128)S(1)}, f32[16]{0:T(128)}, u32[]{:S(2)}) copy-start(f32[16]{0:T(128)} %refs_1_.5) | copy-start | bytes 196
  13.2 3.9 %collective-permute-start.3 = (bf16[1040,128]{1,0:T(8,128)(2,1)S(1)}, bf16[1040,128]{1,0:T(8,128)(2,1)}, u32[]{:S(2)}, u32[]{:S(2)}) collective-permute-start(bf16[1040,128]{1,0:T(8,128)(2,1)S(1)} %broadcast_add_fusion.1.refs_6_), channel_id=1, source_target_pairs={{0,1},{1,0},{2,3},{3,2},{4,5},{5,4},{6,7},{7,6},{8,9},{9,8},{10,11... | collective-permute-start | bytes 798728 | tf_op jit(solution)/shard_map/ppermute | solution.py:253
  14.6 2.5 %collective-permute-start.5 = (bf16[1040,128]{1,0:T(8,128)(2,1)S(1)}, bf16[1040,128]{1,0:T(8,128)(2,1)}, u32[]{:S(2)}, u32[]{:S(2)}) collective-permute-start(bf16[1040,128]{1,0:T(8,128)(2,1)S(1)} %collective-permute-done.4.refs_8_), channel_id=1, source_target_pairs={{0,1},{1,0},{2,3},{3,2},{4,5},{5,4},{6,7},{7,6},{8,9},{9,8},{10,11... | collective-permute-start | bytes 798728 | tf_op jit(solution)/shard_map/ppermute | solution.py:253
  14.6 8.9 %collective-permute-start.2 = (bf16[1040,128]{1,0:T(8,128)(2,1)S(1)}, bf16[1040,128]{1,0:T(8,128)(2,1)}, u32[]{:S(2)}, u32[]{:S(2)}) collective-permute-start(bf16[1040,128]{1,0:T(8,128)(2,1)S(1)} %broadcast_add_fusion.1.refs_6_), channel_id=1, source_target_pairs={{0,4},{1,5},{2,6},{3,7},{4,0},{5,1},{6,2},{7,3},{8,12},{9,13},{10,... | collective-permute-start | bytes 798728 | tf_op jit(solution)/shard_map/ppermute | solution.py:253
  16.2 18.8 %collective-permute-start.8 = (bf16[360,1024]{1,0:T(8,128)(2,1)}, bf16[360,1024]{1,0:T(8,128)(2,1)S(1)}, u32[]{:S(2)}, u32[]{:S(2)}) collective-permute-start(bf16[360,1024]{1,0:T(8,128)(2,1)} %get-tuple-element.18), channel_id=1, source_target_pairs={{0,2},{1,3},{2,0},{3,1},{4,6},{5,7},{6,4},{7,5},{8,10},{9,11},{10,... | collective-permute-start | bytes 2211848 | tf_op jit(solution)/shard_map/ppermute | solution.py:253
  21.9 0.9 %copy-start.1 = (f32[80,2048]{1,0:T(8,128)}, f32[80,2048]{1,0:T(8,128)S(1)}, u32[]{:S(2)}) copy-start(f32[80,2048]{1,0:T(8,128)S(1)} %get-tuple-element.16.refs_8_) | copy-start | bytes 1966084
  24.5 1.6 %collective-permute-start.6 = (bf16[1040,128]{1,0:T(8,128)(2,1)S(1)}, bf16[1040,128]{1,0:T(8,128)(2,1)S(1)}, u32[]{:S(2)}, u32[]{:S(2)}) collective-permute-start(bf16[1040,128]{1,0:T(8,128)(2,1)S(1)} %broadcast_add_fusion.refs_6_), channel_id=1, source_target_pairs={{0,1},{1,0},{2,3},{3,2},{4,5},{5,4},{6,7},{7,6},{8,9},{9,8},{10,11... | collective-permute-start | bytes 798728 | tf_op jit(solution)/shard_map/ppermute | solution.py:253
  24.6 11.9 %collective-permute-start.7 = (bf16[360,1024]{1,0:T(8,128)(2,1)}, bf16[360,1024]{1,0:T(8,128)(2,1)S(1)}, u32[]{:S(2)}, u32[]{:S(2)}) collective-permute-start(bf16[360,1024]{1,0:T(8,128)(2,1)} %get-tuple-element.18), channel_id=1, source_target_pairs={{0,1},{1,0},{2,3},{3,2},{4,5},{5,4},{6,7},{7,6},{8,9},{9,8},{10,11... | collective-permute-start | bytes 2211848 | tf_op jit(solution)/shard_map/ppermute | solution.py:253
  26.1 1.1 %copy-start.2 = (f32[80,2048]{1,0:T(8,128)S(1)}, f32[80,2048]{1,0:T(8,128)}, u32[]{:S(2)}) copy-start(f32[80,2048]{1,0:T(8,128)} %copy-done.1) | copy-start | bytes 1966084
  30.1 8.5 %collective-permute-start.13 = (bf16[1024,128]{1,0:T(8,128)(2,1)}, bf16[1024,128]{1,0:T(8,128)(2,1)}, u32[]{:S(2)}, u32[]{:S(2)}) collective-permute-start(bf16[1024,128]{1,0:T(8,128)(2,1)} %get-tuple-element.17.rows_ref), channel_id=1, source_target_pairs={{0,4},{1,5},{2,6},{3,7},{4,0},{5,1},{6,2},{7,3},{8,12},{9,13},{10,... | collective-permute-start | bytes 786440 | tf_op jit(solution)/shard_map/ppermute | solution.py:253
  36.0 2.6 %collective-permute-start.10 = (bf16[120,1024]{1,0:T(8,128)(2,1)}, bf16[120,1024]{1,0:T(8,128)(2,1)S(1)}, u32[]{:S(2)}, u32[]{:S(2)}) collective-permute-start(bf16[120,1024]{1,0:T(8,128)(2,1)} %get-tuple-element.25), channel_id=1, source_target_pairs={{0,1},{1,0},{2,3},{3,2},{4,5},{5,4},{6,7},{7,6},{8,9},{9,8},{10,11... | collective-permute-start | bytes 737288 | tf_op jit(solution)/shard_map/ppermute | solution.py:253
  36.0 2.6 %collective-permute-start.11 = (bf16[120,1024]{1,0:T(8,128)(2,1)}, bf16[120,1024]{1,0:T(8,128)(2,1)S(1)}, u32[]{:S(2)}, u32[]{:S(2)}) collective-permute-start(bf16[120,1024]{1,0:T(8,128)(2,1)} %get-tuple-element.24), channel_id=1, source_target_pairs={{0,1},{1,0},{2,3},{3,2},{4,5},{5,4},{6,7},{7,6},{8,9},{9,8},{10,11... | collective-permute-start | bytes 737288 | tf_op jit(solution)/shard_map/ppermute | solution.py:253
  36.5 2.1 %collective-permute-start.9 = (bf16[120,1024]{1,0:T(8,128)(2,1)}, bf16[120,1024]{1,0:T(8,128)(2,1)S(1)}, u32[]{:S(2)}, u32[]{:S(2)}) collective-permute-start(bf16[120,1024]{1,0:T(8,128)(2,1)} %get-tuple-element.26), channel_id=1, source_target_pairs={{0,1},{1,0},{2,3},{3,2},{4,5},{5,4},{6,7},{7,6},{8,9},{9,8},{10,11... | collective-permute-start | bytes 737288 | tf_op jit(solution)/shard_map/ppermute | solution.py:253
  40.5 6.6 %collective-permute-start.14 = (bf16[720,128]{1,0:T(8,128)(2,1)S(1)}, bf16[720,128]{1,0:T(8,128)(2,1)S(1)}, u32[]{:S(2)}, u32[]{:S(2)}) collective-permute-start(bf16[720,128]{1,0:T(8,128)(2,1)S(1)} %get-tuple-element.23), channel_id=1, source_target_pairs={{0,8},{8,0},{16,24},{24,16},{1,9},{9,1},{17,25},{25,17},{2,10},{10... | collective-permute-start | bytes 552968 | tf_op jit(solution)/shard_map/ppermute | solution.py:256
  44.8 6.4 %collective-permute-start.12 = (bf16[720,128]{1,0:T(8,128)(2,1)}, bf16[720,128]{1,0:T(8,128)(2,1)S(1)}, u32[]{:S(2)}, u32[]{:S(2)}) collective-permute-start(bf16[720,128]{1,0:T(8,128)(2,1)} %get-tuple-element.21), channel_id=1, source_target_pairs={{0,8},{8,0},{16,24},{24,16},{1,9},{9,1},{17,25},{25,17},{2,10},{10... | collective-permute-start | bytes 552968 | tf_op jit(solution)/shard_map/ppermute | solution.py:256
  47.1 5.7 %collective-permute-start.15 = (bf16[720,128]{1,0:T(8,128)(2,1)S(1)}, bf16[720,128]{1,0:T(8,128)(2,1)S(1)}, u32[]{:S(2)}, u32[]{:S(2)}) collective-permute-start(bf16[720,128]{1,0:T(8,128)(2,1)S(1)} %add_convert_fusion), channel_id=1, source_target_pairs={{0,4},{1,5},{2,6},{3,7},{4,0},{5,1},{6,2},{7,3},{8,12},{9,13},{10,... | collective-permute-start | bytes 552968 | tf_op jit(solution)/shard_map/ppermute | solution.py:253
  52.9 9.6 %collective-permute-start.16 = (bf16[720,128]{1,0:T(8,128)(2,1)S(1)}, bf16[720,128]{1,0:T(8,128)(2,1)S(1)}, u32[]{:S(2)}, u32[]{:S(2)}) collective-permute-start(bf16[720,128]{1,0:T(8,128)(2,1)S(1)} %fusion.3), channel_id=1, source_target_pairs={{0,16},{8,24},{16,0},{24,8},{1,17},{9,25},{17,1},{25,9},{2,18},{10... | collective-permute-start | bytes 552968 | tf_op jit(solution)/shard_map/ppermute | solution.py:256
  55.8 6.7 %copy-start.10 = (f32[720]{0:T(1024)S(1)}, f32[720]{0:T(1024)}, u32[]{:S(2)}) copy-start(f32[720]{0:T(1024)} %param.19) | copy-start | bytes 8644
